TPU v7x, 32 devices: a whole 2x2x4 slice. The times are simulated.
32 devices in a mesh: dp: 4 (over y, x), expert: 8 (over z, core).
Axes of the slice: x: 2, y: 2, z: 4, core: 2. Of those that a mesh axis runs over, the one named last changes fastest.
Arguments:
- grad_rows: bfloat16 [4, 8, 5120, 512], P('dp', None, 'expert'), may hold values from -80 to 80
- momentum_rows: bfloat16 [4, 8, 5120, 512], P('dp', None, 'expert'), may hold values from -1.796875 to 1.796875
- weight_rows: bfloat16 [4, 8, 5120, 512], P('dp', None, 'expert'), may hold values from -0.099609375 to 0.099609375
- row_counts: int32 [4, 8, 8], P('dp', None, 'expert'), may hold values from 1 to 640, 4096 in all within a row
- logit_peaks: bfloat16 [4, 8, 8, 64], P('dp', 'expert'), may hold values from 0 to 300, as said below
Outputs:
- update_rows: bfloat16 [4, 8, 5120, 512], P('dp', None, 'expert')
- weights_out: bfloat16 [4, 8, 5120, 512], P('dp', None, 'expert')
Inputs may be any that keep to these rules, and one draw needn't show every extreme that they name: row_counts[d, m, :] sums to 4096, and its largest entry is 640. `logit_peaks`: positive.
All inputs are finite; a program needn't handle non-finite values. No bound on the sum of `row_counts` on one device may be relied on, other than what follows from the above.
Results may differ from a plain program's by a relative error of at most 0.012.
The roundings to bfloat16 on the way count: a program that leaves them out, or rounds other values in their place, can miss the bound.
Values may be sent and summed in bfloat16 or wider, within the bound.
No kernel may reach another device: no remote copies, remote signals or barrier semaphores. Data moves between devices by JAX's collectives and lax.ppermute only.
A program may use at most 128 MiB of HBM per device.

v0:
```python
import math

import jax
import jax.numpy as jnp
from jax import lax
from jax.sharding import PartitionSpec as P

KV_RANK = 512
NOPE = 128
VDIM = 128
NS_ITERS = 5
KV_ROWS = 16384


momentum_coef = 0.95
learn_rate = 0.02
decay_rate = 0.1
clip_limit = 100.0
coef_first = 3.4445
coef_second = -4.775
coef_third = 2.0315


def carried_in(part, axis, combine, identity):
    place = lax.axis_index(axis)
    gathered = lax.all_gather(part, axis)
    state = jnp.zeros_like(part) + jnp.asarray(identity, part.dtype)

    def one(hop, state):
        return combine(state, lax.dynamic_index_in_dim(gathered, hop, 0, False))

    return lax.fori_loop(0, place, one, state)


def orthogonal(matrix):
    squares = lax.psum(jnp.sum(jnp.square(matrix.astype(jnp.float32))), "dp")
    iterate = (matrix.astype(jnp.float32) / (jnp.sqrt(squares) + 1e-07)).astype(jnp.bfloat16)
    for repeat in range(NS_ITERS):
        local_gram = lax.dot_general(
            iterate, iterate, (((0,), (0,)), ((), ())), preferred_element_type=jnp.float32
        )
        gram_sum = lax.psum(local_gram, "dp")
        square = jnp.dot(gram_sum, gram_sum, precision=lax.Precision.HIGHEST)
        mixing = (coef_second * gram_sum + coef_third * square).astype(jnp.bfloat16)
        iterate = (
            coef_first * iterate.astype(jnp.float32)
            + jnp.dot(iterate, mixing, preferred_element_type=jnp.float32)
        ).astype(jnp.bfloat16)
    return iterate


def add_counts(earlier, later):
    return earlier + later


def local(grad_rows, momentum_rows, weight_rows, row_counts, logit_peaks):
    layers = grad_rows.shape[1]
    capacity = grad_rows.shape[2]
    features = grad_rows.shape[3]
    counts = row_counts[0, :, 0]
    slot_iota = lax.broadcasted_iota(jnp.int32, (layers, capacity), 1)
    slot_live = slot_iota < counts[:, None]
    gradient = grad_rows[0].astype(jnp.float32)
    velocity = momentum_coef * momentum_rows[0].astype(jnp.float32) + gradient
    nesterov = (gradient + momentum_coef * velocity).astype(jnp.bfloat16)
    count_column = counts[:, None]
    arrived, arrived_counts = (
        lax.all_to_all(nesterov, "expert", split_axis=0, concat_axis=0, tiled=True),
        lax.all_to_all(count_column, "expert", split_axis=0, concat_axis=0, tiled=True),
    )
    sources = arrived.shape[0]
    received = arrived_counts[:, 0]
    source_slot = lax.broadcasted_iota(jnp.int32, (sources, capacity), 1)
    present = source_slot < received[:, None]
    masked = jnp.where(present[..., None], arrived, jnp.zeros((), jnp.bfloat16)).reshape(
        sources * capacity, features
    )
    result_slots = orthogonal(masked).reshape(sources, capacity, features)
    returned = lax.all_to_all(result_slots, "expert", split_axis=0, concat_axis=0, tiled=True)
    peak_table = lax.pmax(logit_peaks[0, 0], ("dp", "expert"))
    before = carried_in(counts, "expert", add_counts, jnp.zeros_like(counts))
    rows_block = KV_ROWS // lax.axis_size("dp")
    row_index = lax.axis_index("dp") * rows_block + before[:, None] + slot_iota
    head_rows = NOPE + VDIM
    head_count = peak_table.shape[1]
    factor = jnp.sqrt(jnp.minimum(1.0, clip_limit / peak_table.astype(jnp.float32)))
    head_of = row_index // head_rows
    select_head = head_of[..., None] == lax.broadcasted_iota(jnp.int32, (1, 1, head_count), 2)
    row_factor = jnp.sum(jnp.where(select_head, factor[:, None, :], 0.0), axis=2)
    row_factor = jnp.where(row_index % head_rows < NOPE, row_factor, 1.0)
    rms_scale = 0.2 * math.sqrt(max(KV_ROWS, KV_RANK))
    updated = rms_scale * returned.astype(jnp.float32)
    retained = 1.0 - learn_rate * decay_rate
    new_weight = row_factor[..., None] * (
        weight_rows[0].astype(jnp.float32) * retained - learn_rate * updated
    )
    update_out = jnp.where(slot_live[..., None], updated, 0.0).astype(jnp.bfloat16)
    weight_out = jnp.where(slot_live[..., None], new_weight, 0.0).astype(jnp.bfloat16)
    return (update_out[None], weight_out[None])


def solution(mesh):
    return jax.shard_map(
        local,
        mesh=mesh,
        in_specs=(
            P("dp", None, "expert", None),
            P("dp", None, "expert", None),
            P("dp", None, "expert", None),
            P("dp", None, "expert"),
            P("dp", "expert", None, None),
        ),
        out_specs=(P("dp", None, "expert", None), P("dp", None, "expert", None)),
        check_vma=False,
    )
```

profile of v0, /device:TPU:0, one launch (start us, length us, event | category | flops | bytes accessed | tf_op | source)
XLA Modules:
  0.0 690.8 jit_solution(12321188264198859800)
XLA Ops:
  8.5 6.3 all-to-all-start
  14.8 8.6 %fusion.9 = bf16[8,640,512]{2,1,0:T(8,128)(2,1)} fusion(bf16[1,8,640,512]{3,2,1,0:T(8,128)(2,1)} %param.8, bf16[1,8,640,512]{3,2,1,0:T(8,128)(2,1)} %param.7), kind=kLoop, calls=%fused_computation.16 | loop fusion | flops 18350080 | bytes 15728640 | tf_op jit(solution)/shard_map/convert_element_type | solution.py:65
  23.5 5.1 all-to-all-start.1
  28.9 116.2 %all-to-all-done.1 = bf16[8,640,512]{2,1,0:T(8,128)(2,1)} async-done(((bf16[8,640,512]{2,1,0:T(8,128)(2,1)}), bf16[8,640,512]{2,1,0:T(8,128)(2,1)}, u32[]{:S(2)}, u32[]{:S(2)}) %all-to-all-start.1) | async-done | bytes 5242912 | tf_op jit(solution)/shard_map/all_to_all | solution.py:68
  145.1 5.7 fusion
  150.9 10.5 %psum.42 = f32[]{:T(128)} all-reduce(f32[]{:T(128)} %fusion), channel_id=1, replica_groups=mesh['dp'=4,'expert'=8] {'dp'}, use_global_device_ids=true, to_apply=%region_1.2 | all-reduce | flops 1 | bytes 8 | tf_op jit(solution)/shard_map/psum | solution.py:36
  162.1 4.0 fusion.1
  172.6 49.5 %all-reduce.6.cloned.1.call-done = f32[512,512]{1,0:T(8,128)} async-done(((f32[512,512]{1,0:T(8,128)}), f32[512,512]{1,0:T(8,128)}) %all-reduce.6.cloned.1.call-update) | async-done | bytes 1048592 | tf_op jit(solution)/shard_map/psum | solution.py:42
  222.1 3.9 fusion.17
  226.0 6.4 add_convert_fusion.4
  238.7 52.7 %all-reduce.8.cloned.1.call-done = f32[512,512]{1,0:T(8,128)} async-done(((f32[512,512]{1,0:T(8,128)}), f32[512,512]{1,0:T(8,128)}) %all-reduce.8.cloned.1.call-update) | async-done | bytes 1048592 | tf_op jit(solution)/shard_map/psum | solution.py:42
  291.3 3.9 fusion.18
  295.3 6.4 add_convert_fusion.3
  308.2 52.4 %all-reduce.10.cloned.1.call-done = f32[512,512]{1,0:T(8,128)} async-done(((f32[512,512]{1,0:T(8,128)}), f32[512,512]{1,0:T(8,128)}) %all-reduce.10.cloned.1.call-update) | async-done | bytes 1048592 | tf_op jit(solution)/shard_map/psum | solution.py:42
  360.6 3.9 fusion.19
  364.5 6.4 add_convert_fusion.2
  377.2 52.7 %all-reduce.12.cloned.1.call-done = f32[512,512]{1,0:T(8,128)} async-done(((f32[512,512]{1,0:T(8,128)}), f32[512,512]{1,0:T(8,128)}) %all-reduce.12.cloned.1.call-update) | async-done | bytes 1048592 | tf_op jit(solution)/shard_map/psum | solution.py:42
  433.8 6.4 add_convert_fusion.1
  446.5 52.7 %all-reduce.14.cloned.1.call-done = f32[512,512]{1,0:T(8,128)} async-done(((f32[512,512]{1,0:T(8,128)}), f32[512,512]{1,0:T(8,128)}) %all-reduce.14.cloned.1.call-update) | async-done | bytes 1048592 | tf_op jit(solution)/shard_map/psum | solution.py:42
  503.1 7.9 %add_convert_fusion = bf16[5120,512]{1,0:T(8,128)(2,1)} fusion(bf16[5120,512]{1,0:T(8,128)(2,1)} %copy-done.6, bf16[512,512]{1,0:T(8,128)(2,1)S(1)} %fusion.21), kind=kOutput, calls=%fused_computation.17 | convolution fusion | flops 2694840320 | bytes 11010048 | tf_op jit(solution)/shard_map/dot_general | solution.py:47
  511.0 4.8 all-to-all-start.2
  515.8 92.0 %all-gather = s32[8,8,1]{1,2,0:T(1,128)S(1)} all-gather(s32[1,8,1]{1,2,0:T(1,128)S(1)} %copy-done.1), channel_id=2, replica_groups=mesh['dp'=4,'expert'=8] {'expert'}, dimensions={0}, use_global_device_ids=true | all-gather | bytes 288 | tf_op jit(solution)/shard_map/all_gather | solution.py:26
  607.7 65.7 %pmax.7 = bf16[8,64]{1,0:T(8,128)(2,1)S(1)} all-reduce(bf16[8,64]{1,0:T(8,128)(2,1)S(1)} %bitcast.60), channel_id=1, replica_groups=mesh['dp'=4,'expert'=8] {'dp','expert'}, use_global_device_ids=true, to_apply=%region_9.10 | all-reduce | flops 512 | bytes 2048 | tf_op jit(solution)/shard_map/pmax | solution.py:80
  674.1 10.1 %fusion.10 = (bf16[1,8,640,512]{3,2,1,0:T(8,128)(2,1)}, bf16[1,8,640,512]{3,2,1,0:T(8,128)(2,1)}) fusion(bf16[8,640,512]{2,1,0:T(8,128)(2,1)} %all-to-all-done.2, bf16[1,8,640,512]{3,2,1,0:T(8,128)(2,1)} %param.9, f32[8,640]{1,0:T(8,128)S(1)} %fusion.26, pred[8,640]{1,0:T(8,128)(4,1)S(1)} %iota_compare_fusion.2), kind=kLoop, calls=%fused_computation.22 | loop fusion | flops 28835840 | bytes 20997120 | tf_op jit(solution)/shard_map/broadcast_in_dim | solution.py:99
  (44 shorter events, 41.9 us)
Async XLA Ops:
  8.5 15.0 %all-to-all-start = ((s32[8,1,1]{2,1,0:T(1,128)}), s32[8,1,1]{2,1,0:T(1,128)S(1)}, u32[]{:S(2)}, u32[]{:S(2)}) async-start(s32[8,1,1]{2,1,0:T(1,128)} %copy.13), calls=%async_computation | async-start | bytes 8192 | tf_op jit(solution)/shard_map/all_to_all | solution.py:69
  23.5 121.7 %all-to-all-start.1 = ((bf16[8,640,512]{2,1,0:T(8,128)(2,1)}), bf16[8,640,512]{2,1,0:T(8,128)(2,1)}, u32[]{:S(2)}, u32[]{:S(2)}) async-start(bf16[8,640,512]{2,1,0:T(8,128)(2,1)} %fusion.9), calls=%async_computation.1 | async-start | bytes 10485760 | tf_op jit(solution)/shard_map/all_to_all | solution.py:68
  28.6 193.5 %all-reduce.6.cloned.1.call-start = ((), (), s32[]{:S(2)}) async-start(), calls=%async_computation.3 | async-start | bytes 2097152 | tf_op jit(solution)/shard_map/psum | solution.py:42
  166.1 2.4 copy-start
  172.4 119.0 %all-reduce.8.cloned.1.call-start = ((), (), s32[]{:S(2)}) async-start(), calls=%async_computation.4 | async-start | bytes 2097152 | tf_op jit(solution)/shard_map/psum | solution.py:42
  232.4 2.4 copy-start.3
  238.6 122.0 %all-reduce.10.cloned.1.call-start = ((), (), s32[]{:S(2)}) async-start(), calls=%async_computation.5 | async-start | bytes 2097152 | tf_op jit(solution)/shard_map/psum | solution.py:42
  301.7 2.4 copy-start.4
  307.9 122.0 %all-reduce.12.cloned.1.call-start = ((), (), s32[]{:S(2)}) async-start(), calls=%async_computation.6 | async-start | bytes 2097152 | tf_op jit(solution)/shard_map/psum | solution.py:42
  370.9 2.4 copy-start.5
  377.2 122.0 %all-reduce.14.cloned.1.call-start = ((), (), s32[]{:S(2)}) async-start(), calls=%async_computation.7 | async-start | bytes 2097152 | tf_op jit(solution)/shard_map/psum | solution.py:42
  440.2 2.4 copy-start.6
  511.0 4.8 copy-start.1
  511.0 96.8 %copy-start.2 = (bf16[1,1,8,64]{3,2,1,0:T(8,128)(2,1)S(1)}, bf16[1,1,8,64]{3,2,1,0:T(8,128)(2,1)}, u32[]{:S(2)}) copy-start(bf16[1,1,8,64]{3,2,1,0:T(8,128)(2,1)} %param.11) | copy-start | bytes 3076
  511.0 163.1 %all-to-all-start.2 = ((bf16[8,640,512]{2,1,0:T(8,128)(2,1)}), bf16[8,640,512]{2,1,0:T(8,128)(2,1)}, u32[]{:S(2)}, u32[]{:S(2)}) async-start(bf16[8,640,512]{2,1,0:T(8,128)(2,1)} %bitcast.56), calls=%async_computation.2 | async-start | bytes 10485760 | tf_op jit(solution)/shard_map/all_to_all | solution.py:79
Sparse Core Ops, SparseCore 0:
  172.5 49.5 all-reduce.5
  238.8 52.5 all-reduce.7
  308.0 52.5 all-reduce.9
  377.3 52.5 all-reduce.11
  446.6 52.5 all-reduce.13
where the time goes:
time: 691 us
  waiting for transfers between devices  376 us (54%)
  blocking collectives  168 us (24%)
  matrix products  72.3 us (10%)
  other arithmetic  29.4 us (4%)
  starting transfers between devices  16.8 us (2%)
  between operations  14.6 us (2%)
  local copies, waits for them, and re-layouts  13.1 us (2%)
    psum x5, waiting for transfers between devices, orthogonal(): gram_sum = lax.psum(local_gram, 'dp')  260 us
    all_to_all x1, waiting for transfers between devices, local(): lax.all_to_all(nesterov, 'expert', split_axis=0, concat_axis=0, tiled=True)  116 us
    all_gather x1, blocking collectives, carried_in(): gathered = lax.all_gather(part, axis)  92 us
    pmax x1, blocking collectives, local(): peak_table = lax.pmax(logit_peaks[0, 0], ('dp', 'expert'))  65.7 us
    dot_general x5, matrix products, orthogonal(): jnp.dot(iterate, mixing, preferred_element_type=jnp.float32)  33.4 us
    dot_general x5, matrix products, orthogonal(): square = jnp.dot(gram_sum, gram_sum, precision=lax.Precision.HIGHEST)  19.5 us
    dot_general x5, matrix products, orthogonal(): lax.dot_general(iterate, iterate, (((0,), (0,)), ((), ())), preferred_ele...  19.3 us
  transfers between devices with their start and end apart: 8, of which 6 were waited for; matrix products, arithmetic and copies ran while one was open for 1% of the time, Pallas kernels for 0%

commit v1 on v0

v1 whole, which is shorter than its diff:
```python
import functools
import math

import jax
import jax.numpy as jnp
from jax import lax
from jax.experimental import pallas as pl
from jax.experimental.pallas import tpu as pltpu
from jax.sharding import PartitionSpec as P

KV_RANK = 512
NOPE = 128
VDIM = 128
NS_ITERS = 5
KV_ROWS = 16384

momentum_coef = 0.95
learn_rate = 0.02
decay_rate = 0.1
clip_limit = 100.0
coef_first = 3.4445
coef_second = -4.775
coef_third = 2.0315

f32 = jnp.float32
bf16 = jnp.bfloat16

LANES = 128
BLOCKS = KV_RANK // LANES
PAIRS = [(i, j) for i in range(BLOCKS) for j in range(i, BLOCKS)]
HALF = len(PAIRS) // 2
AUX = 8
HEAD_A = AUX + HALF * LANES
ROWS = AUX + len(PAIRS) * LANES
TAIL_B = ROWS - HEAD_A
AUX_P = 32
ROWS_P = AUX_P + len(PAIRS) * LANES
HALF_P = ROWS_P // 2


def params(**more):
    return pltpu.CompilerParams(vmem_limit_bytes=40 * 1024 * 1024, **more)


def whole(shape):
    return pl.BlockSpec(shape, lambda *_: (0,) * len(shape))


def gram_kernel(ids, counts, grad_ref, mom_ref, aux_ref, nes_ref, gram_ref):
    count = counts[ids[pl.program_id(0)]]
    gradient = grad_ref[0].astype(f32)
    velocity = momentum_coef * mom_ref[0].astype(f32) + gradient
    nesterov = gradient + momentum_coef * velocity
    slot = lax.broadcasted_iota(jnp.int32, nesterov.shape, 0)
    rows = jnp.where(slot < count, nesterov, 0.0).astype(bf16)
    nes_ref[0] = rows
    gram_ref[0, 0:AUX, :] = aux_ref[0]
    half = KV_RANK // 2
    dims = (((0,), (0,)), ((), ()))
    upper = lax.dot_general(rows[:, :half], rows, dims, preferred_element_type=f32)
    lower = lax.dot_general(rows[:, half:], rows[:, half:], dims, preferred_element_type=f32)
    for place, (i, j) in enumerate(PAIRS):
        at = AUX + place * LANES
        if i < 2:
            block = upper[i * LANES : (i + 1) * LANES, j * LANES : (j + 1) * LANES]
        else:
            block = lower[(i - 2) * LANES : (i - 1) * LANES, (j - 2) * LANES : (j - 1) * LANES]
        gram_ref[0, at : at + LANES, :] = block


def gram_parts(ids, counts, grad, mom, aux):
    number = ids.shape[0]
    capacity, features = grad.shape[1:]
    picked = lambda i, ids, counts: (ids[i], 0, 0)
    here = lambda i, ids, counts: (i, 0, 0)
    return pl.pallas_call(
        gram_kernel,
        grid_spec=pltpu.PrefetchScalarGridSpec(
            num_scalar_prefetch=2,
            grid=(number,),
            in_specs=[
                pl.BlockSpec((1, capacity, features), picked),
                pl.BlockSpec((1, capacity, features), picked),
                pl.BlockSpec((1, AUX, LANES), picked),
            ],
            out_specs=[
                pl.BlockSpec((1, capacity, features), here),
                pl.BlockSpec((1, ROWS, LANES), here),
            ],
        ),
        out_shape=[
            jax.ShapeDtypeStruct((number, capacity, features), bf16),
            jax.ShapeDtypeStruct((number, ROWS, LANES), f32),
        ],
        compiler_params=params(),
        cost_estimate=pl.CostEstimate(
            flops=number * capacity * features * features * 2,
            bytes_accessed=number * (capacity * features * 6 + ROWS * LANES * 4),
            transcendentals=0,
        ),
        name="gram_parts",
    )(ids, counts, grad, mom, aux)


def joined(first, second):
    row = lax.broadcasted_iota(jnp.int32, first.shape, 0)
    return jnp.where(row == 0, jnp.maximum(first, second), first + second)


def local_call(kernel, out_shapes, name, *args):
    size = sum(math.prod(x.shape) * x.dtype.itemsize for x in list(args) + list(out_shapes))
    return pl.pallas_call(
        kernel,
        in_specs=[pl.BlockSpec(memory_space=pltpu.VMEM)] * len(args),
        out_specs=[pl.BlockSpec(memory_space=pltpu.VMEM)] * len(out_shapes),
        out_shape=list(out_shapes),
        compiler_params=params(),
        cost_estimate=pl.CostEstimate(flops=size // 4, bytes_accessed=size, transcendentals=0),
        name=name,
    )(*args)


def split_kernel(kept, arrived, first_ref, second_ref):
    first_ref[...] = joined(kept[0, :HEAD_A], arrived[0, :HEAD_A])
    second_ref[...] = kept[0, HEAD_A:] + arrived[0, HEAD_A:]


def relay_kernel(kept, arrived, from_left, from_right, up_ref, down_ref, own_ref):
    up = kept[0, :HEAD_A], arrived[0, :HEAD_A]
    up_ref[:HEAD_A] = joined(joined(*up), from_left[...])
    up_ref[HEAD_A:] = kept[0, HEAD_A:] + arrived[0, HEAD_A:]
    down_ref[:HEAD_A] = joined(kept[1, :HEAD_A], arrived[1, :HEAD_A])
    down_ref[HEAD_A:] = kept[1, HEAD_A:] + arrived[1, HEAD_A:] + from_right[...]
    own_ref[...] = joined(kept[2], arrived[2])


def pass_kernel(kept_up, kept_down, from_left, from_right, up_ref, down_ref):
    up_ref[...] = joined(kept_up[...], from_left[...])
    down_ref[...] = joined(kept_down[...], from_right[...])


def own_kernel(own, from_left, from_right, first_ref, second_ref):
    first_ref[...] = joined(joined(own[:HEAD_A], from_left[:HEAD_A]), from_right[:HEAD_A])
    second_ref[...] = own[HEAD_A:] + from_left[HEAD_A:] + from_right[HEAD_A:]


def pair_kernel(first, first_other, second, second_other, first_ref, second_ref):
    first_ref[...] = joined(first[...], first_other[...])
    second_ref[...] = second[...] + second_other[...]


def mm(x, y):
    return jnp.dot(x, y, preferred_element_type=f32)


def parts_of(x):
    high = x.astype(bf16)
    return high, (x - high.astype(f32)).astype(bf16)


def iterate_kernel(first, first_other, second, second_other, out_ref, gram_ref):
    head = joined(first[...], first_other[...])
    tail = second[...] + second_other[...]
    row = lax.broadcasted_iota(jnp.int32, (LANES, LANES), 0)
    col = lax.broadcasted_iota(jnp.int32, (LANES, LANES), 1)
    eye_block = (row == col).astype(f32)
    squares = jnp.zeros((1, LANES), f32)
    for place, (i, j) in enumerate(PAIRS):
        if place < HALF:
            block = head[AUX + place * LANES : AUX + (place + 1) * LANES]
        else:
            block = tail[(place - HALF) * LANES : (place - HALF + 1) * LANES]
        gram_ref[i * LANES : (i + 1) * LANES, j * LANES : (j + 1) * LANES] = block
        if i != j:
            gram_ref[j * LANES : (j + 1) * LANES, i * LANES : (i + 1) * LANES] = block.T
        else:
            squares = squares + jnp.sum(block * eye_block, axis=0, keepdims=True)
    squares = jnp.sum(squares, axis=1, keepdims=True)
    inverse = 1.0 / (jnp.sqrt(squares) + 1e-07)
    gram = gram_ref[...] * inverse * inverse
    full_row = lax.broadcasted_iota(jnp.int32, (KV_RANK, KV_RANK), 0)
    full_col = lax.broadcasted_iota(jnp.int32, (KV_RANK, KV_RANK), 1)
    product = None
    for repeat in range(NS_ITERS):
        high, low = parts_of(gram)
        square = mm(high, high) + (mm(high, low) + mm(low, high))
        mixing = (coef_second * gram + coef_third * square).astype(bf16)
        if product is None:
            product = jnp.where(full_row == full_col, coef_first, 0.0) + mixing.astype(f32)
        else:
            product_high, product_low = parts_of(product)
            product = coef_first * product + (mm(product_high, mixing) + mm(product_low, mixing))
        if repeat < NS_ITERS - 1:
            half = coef_first * gram + (mm(high, mixing) + mm(low, mixing))
            half_high, half_low = parts_of(half)
            gram = coef_first * half + (mm(mixing, half_high) + mm(mixing, half_low))
    gram_ref[...] = product
    diagonals = []
    for place, (i, j) in enumerate(PAIRS):
        block = gram_ref[i * LANES : (i + 1) * LANES, j * LANES : (j + 1) * LANES]
        if i != j:
            other = gram_ref[j * LANES : (j + 1) * LANES, i * LANES : (i + 1) * LANES]
            block = 0.5 * (block + other.T)
        else:
            diagonals.append(jnp.sum(block * eye_block, axis=0, keepdims=True))
        at = AUX_P + place * LANES
        out_ref[at : at + LANES, :] = block.astype(bf16)

    def three(x):
        high = x.astype(bf16).astype(f32)
        middle = (x - high).astype(bf16).astype(f32)
        return high, middle, x - high - middle

    lines = [[], [], []]
    for diagonal in diagonals:
        for line, part in zip(lines, three(diagonal)):
            line.append(part)
    peaks = head[0:1]
    tallies = head[1:2]
    tally_high = tallies.astype(bf16).astype(f32)
    norm = three(jnp.broadcast_to(inverse, (1, LANES)))
    stacked = lines[0] + lines[1] + lines[2] + [peaks, tally_high, tallies - tally_high] + list(norm)
    place = lax.broadcasted_iota(jnp.int32, (AUX_P, LANES), 0)
    aux = jnp.zeros((AUX_P, LANES), f32)
    for number, line in enumerate(stacked):
        aux = jnp.where(place == number, line, aux)
    out_ref[0:AUX_P, :] = aux.astype(bf16)


def iterations(first, first_other, second, second_other):
    passes = 9 * NS_ITERS
    return pl.pallas_call(
        iterate_kernel,
        in_specs=[pl.BlockSpec(memory_space=pltpu.VMEM)] * 4,
        out_specs=pl.BlockSpec(memory_space=pltpu.VMEM),
        out_shape=jax.ShapeDtypeStruct((ROWS_P, LANES), bf16),
        scratch_shapes=[pltpu.VMEM((KV_RANK, KV_RANK), f32)],
        compiler_params=params(),
        cost_estimate=pl.CostEstimate(
            flops=passes * 2 * KV_RANK**3, bytes_accessed=4 * ROWS * LANES * 4, transcendentals=0
        ),
        name="iterations",
    )(first, first_other, second, second_other)


def apply_kernel(spread, seats, ids, counts, me, *refs):
    number = sum(1 for _ in {place for step in spread for place, _ in step})
    tables = refs[:number]
    nes_ref, weight_ref = refs[number : number + 2]
    update_ref, weight_out_ref, mat_ref, line_ref = refs[-4:]
    step_now = pl.program_id(0)
    row = lax.broadcasted_iota(jnp.int32, (LANES, LANES), 0)
    col = lax.broadcasted_iota(jnp.int32, (LANES, LANES), 1)

    def unpack(step):
        (place_a, start_a), (place_b, start_b) = spread[step]

        def rows_at(at, size):
            if at < HALF_P:
                piece = tables[place_a][start_a + at : start_a + min(at + size, HALF_P), :]
                if at + size > HALF_P:
                    piece = jnp.concatenate(
                        [piece, tables[place_b][start_b : start_b + at + size - HALF_P, :]], axis=0
                    )
                return piece.astype(f32)
            return tables[place_b][start_b + at - HALF_P : start_b + at + size - HALF_P, :].astype(f32)

        aux = rows_at(0, AUX_P)
        diagonal = [aux[i : i + 1] + aux[4 + i : 5 + i] + aux[8 + i : 9 + i] for i in range(BLOCKS)]
        inverse = [1.0 / line for line in diagonal]
        norm = aux[15:16] + aux[16:17] + aux[17:18]
        rms_scale = 0.2 * math.sqrt(max(KV_ROWS, KV_RANK))
        for i in range(BLOCKS):
            line_ref[0:1, i * LANES : (i + 1) * LANES] = diagonal[i] * (norm * rms_scale)
        peaks = aux[12:13]
        factor = jnp.sqrt(jnp.minimum(1.0, clip_limit / peaks))
        line_ref[1:2, 0:LANES] = factor
        line_ref[2:3, 0:LANES] = aux[13:14] + aux[14:15]
        for place, (i, j) in enumerate(PAIRS):
            block = rows_at(AUX_P + place * LANES, LANES)
            if i == j:
                scaled = jnp.where(row == col, 1.0, block * inverse[i])
                mat_ref[i * LANES : (i + 1) * LANES, i * LANES : (i + 1) * LANES] = scaled.astype(bf16)
            else:
                mat_ref[i * LANES : (i + 1) * LANES, j * LANES : (j + 1) * LANES] = (block * inverse[j]).astype(bf16)
                mat_ref[j * LANES : (j + 1) * LANES, i * LANES : (i + 1) * LANES] = (block.T * inverse[i]).astype(bf16)

    for step in range(len(spread)):
        pl.when(step_now == step)(functools.partial(unpack, step))

    capacity = nes_ref.shape[1]
    count = counts[ids[step_now]]
    groups, rows_block = seats
    lane = lax.broadcasted_iota(jnp.int32, (1, LANES), 1)
    lowest = me[0] * groups
    earlier = jnp.where((lane >= lowest) & (lane < lowest + me[1]), line_ref[2:3, 0:LANES], 0.0)
    before = jnp.sum(earlier, axis=1, keepdims=True).astype(jnp.int32)
    base = before + me[0] * rows_block
    head_rows = NOPE + VDIM
    first_head = base // head_rows
    factor = line_ref[1:2, 0:LANES]
    slot = lax.broadcasted_iota(jnp.int32, (capacity, LANES), 0)
    row_index = base + slot
    head_of = row_index // head_rows
    scale = jnp.ones((capacity, LANES), f32)
    for k in range((capacity - 1) // head_rows + 2):
        one = jnp.sum(jnp.where(lane == first_head + k, factor, 0.0), axis=1, keepdims=True)
        scale = jnp.where(head_of == first_head + k, one, scale)
    scale = jnp.where(row_index % head_rows < NOPE, scale, 1.0)
    scale = jnp.where(slot < count, scale, 0.0)
    kept = scale * (1.0 - learn_rate * decay_rate)
    moved = scale * learn_rate
    rows = nes_ref[0]
    half = KV_RANK // 2
    for side in range(2):
        product = mm(rows, mat_ref[:, side * half : (side + 1) * half])
        for part in range(half // LANES):
            at = side * half + part * LANES
            update = product[:, part * LANES : (part + 1) * LANES] * line_ref[0:1, at : at + LANES]
            update_ref[0, :, at : at + LANES] = update.astype(bf16)
            weight = weight_ref[0, :, at : at + LANES].astype(f32)
            weight_out_ref[0, :, at : at + LANES] = (weight * kept - update * moved).astype(bf16)


def apply_rows(spread, seats, ids, counts, me, tables, nes, order, weight, update, weight_out):
    number = len(spread)
    layers, capacity, features = weight.shape
    picked = lambda i, ids, counts, me: (ids[i], 0, 0)
    start = order[0]
    assert list(order) == list(range(start, start + number))
    in_specs = [whole(table.shape) for table in tables]
    in_specs += [
        pl.BlockSpec((1, capacity, features), lambda i, ids, counts, me: (i + start, 0, 0)),
        pl.BlockSpec((1, capacity, features), picked),
    ]
    args = list(tables) + [nes, weight]
    aliases = {}
    if update is not None:
        in_specs += [pl.BlockSpec(memory_space=pl.ANY)] * 2
        aliases = {3 + len(args): 0, 4 + len(args): 1}
        args += [update, weight_out]
    shape = jax.ShapeDtypeStruct((layers, capacity, features), bf16)
    return pl.pallas_call(
        functools.partial(apply_kernel, spread, seats),
        grid_spec=pltpu.PrefetchScalarGridSpec(
            num_scalar_prefetch=3,
            grid=(number,),
            in_specs=in_specs,
            out_specs=[pl.BlockSpec((1, capacity, features), picked)] * 2,
            scratch_shapes=[pltpu.VMEM((KV_RANK, KV_RANK), bf16), pltpu.VMEM((8, KV_RANK), f32)],
        ),
        out_shape=[shape, shape],
        input_output_aliases=aliases,
        compiler_params=params(),
        cost_estimate=pl.CostEstimate(
            flops=number * capacity * features * features * 2,
            bytes_accessed=number * capacity * features * 8,
            transcendentals=0,
        ),
        name="apply_rows",
    )(ids, counts, me, *args)


def local(dp_size, expert_size, grad_rows, momentum_rows, weight_rows, row_counts, logit_peaks):
    layers, capacity = grad_rows.shape[1:3]
    ring = expert_size // 2
    far = ring // 2
    assert layers == expert_size and ring >= 4 and ring % 2 == 0
    assert dp_size == 4 and dp_size * expert_size <= LANES
    dp = lax.axis_index("dp")
    expert = lax.axis_index("expert")
    seat, core = expert // 2, expert % 2
    counts = row_counts[0, :, 0]
    me = jnp.stack([dp, expert]).astype(jnp.int32)

    def layer(distance, own_core):
        return 2 * ((seat + distance) % ring) + (core if own_core else 1 - core)

    def across(x):
        return lax.ppermute(x, "expert", [(i, i ^ 1) for i in range(expert_size)])

    def along(x, by):
        return lax.ppermute(x, "expert", [(i, (i + 2 * by) % expert_size) for i in range(expert_size)])

    def over_dp(x, bit):
        return lax.ppermute(x, "dp", [(i, i ^ bit) for i in range(dp_size)])

    lane = lax.broadcasted_iota(jnp.int32, (layers, AUX, LANES), 2)
    line = lax.broadcasted_iota(jnp.int32, (layers, AUX, LANES), 1)
    peaks = jnp.pad(logit_peaks[0, 0].astype(f32), ((0, 0), (0, LANES - logit_peaks.shape[3])))
    mine = dp * expert_size + expert
    aux = jnp.where(line == 0, peaks[:, None, :], 0.0)
    aux = jnp.where((line == 1) & (lane == mine), counts[:, None, None].astype(f32), aux)

    def partials(distances, own_core):
        ids = jnp.stack([layer(distance, own_core) for distance in distances]).astype(jnp.int32)
        return gram_parts(ids, counts, grad_rows[0], momentum_rows[0], aux)

    near = [r for s in range(1, far) for r in (far - s, ring - far + s)] + [0]
    nes_far_other, far_other = partials([far], False)
    nes_far, far_own = partials([far], True)
    far_arrived = across(far_other)
    nes_near_other, near_other = partials(near, False)
    nes_near, near_own = partials(near, True)
    near_arrived = across(near_other)

    part = lambda rows: jax.ShapeDtypeStruct((rows, LANES), f32)
    first, second = local_call(split_kernel, [part(HEAD_A), part(TAIL_B)], "split", far_own, far_arrived)
    from_left, from_right = along(first, 1), along(second, -1)
    last = len(near) - 3
    if far == 2:
        up, down, own = local_call(
            relay_kernel, [part(ROWS)] * 3, "relay", near_own, near_arrived, from_left, from_right
        )
    else:
        rest = jnp.stack([joined(near_own[k], near_arrived[k]) for k in range(len(near))])
        pad_left = jnp.pad(from_left, ((0, TAIL_B), (0, 0)))
        pad_right = jnp.pad(from_right, ((HEAD_A, 0), (0, 0)))
        for k in range(0, last, 2):
            up, down = local_call(
                pass_kernel, [part(ROWS)] * 2, "pass", rest[k], rest[k + 1], pad_left, pad_right
            )
            pad_left, pad_right = along(up, 1), along(down, -1)
        up, down = local_call(
            pass_kernel, [part(ROWS)] * 2, "pass", rest[last], rest[last + 1], pad_left, pad_right
        )
        own = rest[last + 2]
    from_left, from_right = along(up, 1), along(down, -1)
    first, second = local_call(own_kernel, [part(HEAD_A), part(TAIL_B)], "own", own, from_left, from_right)
    first_other, second_other = over_dp(first, 1), over_dp(second, 2)
    first, second = local_call(
        pair_kernel, [part(HEAD_A), part(TAIL_B)], "pair", first, first_other, second, second_other
    )
    table = iterations(first, over_dp(first, 2), second, over_dp(second, 1))

    seats = (expert_size, KV_ROWS // dp_size)
    full = lambda place: ((place, 0), (place, HALF_P))
    weight = weight_rows[0]

    def ids_of(pairs):
        return jnp.stack([layer(distance, own_core) for distance, own_core in pairs]).astype(jnp.int32)

    left, right = along(table, 1), along(table, -1)
    own_tables = [table, across(table)]
    end = len(near) - 1
    update, weight_out = apply_rows(
        (full(0),), seats, ids_of([(0, True)]), counts, me, own_tables[:1], nes_near, [end], weight, None, None
    )
    update, weight_out = apply_rows(
        (full(0),), seats, ids_of([(0, False)]), counts, me, own_tables[1:], nes_near_other, [end], weight, update, weight_out
    )
    for hop in range(1, far):
        if hop == far - 1:
            next_left = along(left[:HALF_P], 1)
            next_right = along(right[HALF_P:], -1)
        else:
            next_left, next_right = along(left, 1), along(right, -1)
        place = near.index(hop)
        pair = [right, left]
        update, weight_out = apply_rows(
            (full(0), full(1)), seats, ids_of([(hop, True), (ring - hop, True)]), counts, me, pair, nes_near,
            [place, place + 1], weight, update, weight_out,
        )
        update, weight_out = apply_rows(
            (full(0), full(1)), seats, ids_of([(hop, False), (ring - hop, False)]), counts, me, [across(t) for t in pair],
            nes_near_other, [place, place + 1], weight, update, weight_out,
        )
        left, right = next_left, next_right
    halves = ((0, 0), (1, 0))
    update, weight_out = apply_rows(
        (halves,), seats, ids_of([(far, True)]), counts, me, [left, right], nes_far, [0], weight, update, weight_out
    )
    update, weight_out = apply_rows(
        (halves,), seats, ids_of([(far, False)]), counts, me, [across(left), across(right)], nes_far_other, [0],
        weight, update, weight_out,
    )
    return (update[None], weight_out[None])


def solution(mesh):
    return jax.shard_map(
        functools.partial(local, mesh.shape["dp"], mesh.shape["expert"]),
        mesh=mesh,
        in_specs=(
            P("dp", None, "expert", None),
            P("dp", None, "expert", None),
            P("dp", None, "expert", None),
            P("dp", None, "expert"),
            P("dp", "expert", None, None),
        ),
        out_specs=(P("dp", None, "expert", None), P("dp", None, "expert", None)),
        check_vma=False,
    )
```

time: 691 us -> 152 us (0.22)
  waiting for transfers between devices: 376 us -> 62 us
  blocking collectives: 168 us -> 0 us
  matrix products: 72.3 us -> 0 us
  Pallas kernels: 0 us -> 44 us
  other arithmetic: 29.4 us -> 1.81 us
  between operations: 14.6 us -> 0.88 us
  local copies, waits for them, and re-layouts: 13.1 us -> 20.6 us
    psum x5 -> x0, waiting for transfers between devices: 260 us -> none  [orthogonal(): gram_sum = lax.psum(local_gram, 'dp')]
    all_to_all x3 -> x0, waiting for transfers between devices: 116 us -> none  [the longest x1 116 us: local(): lax.all_to_all(nesterov, 'expert', split_axis=0, concat_axis=0, tiled=True)]
    all_gather x1 -> x0, blocking collectives: 92 us -> none  [carried_in(): gathered = lax.all_gather(part, axis)]
    dot_general x15 -> x0, matrix products: 72.3 us -> none  [the longest x5 33.4 us: orthogonal(): jnp.dot(iterate, mixing, preferred_element_type=jnp.float32)]
    pmax x1 -> x0, blocking collectives: 65.7 us -> none  [local(): peak_table = lax.pmax(logit_peaks[0, 0], ('dp', 'expert'))]
    ppermute x0 -> x19, waiting for transfers between devices: none -> 62 us  [the longest x8 47.5 us: along(): lax.ppermute(x, 'expert', [(i, (i + 2 * by) % expert_size) for i in range...]
    pallas_call x0 -> x15, Pallas kernels: none -> 44 us  [the longest x6 18.8 us: apply_rows(): pl.pallas_call(functools.partial(apply_kernel, spread, seats), grid_spec=...]
    ppermute x0 -> x19, starting transfers between devices: none -> 22.3 us  [the longest x8 15.9 us: along(): lax.ppermute(x, 'expert', [(i, (i + 2 * by) % expert_size) for i in range...]
  transfers between devices with their start and end apart: 8 -> 19, of which waited for: 6 -> 8; matrix products, arithmetic and copies ran while one was open for 1% -> 0% of each run, Pallas kernels for 0% -> 15%
where the time goes in v1:
time: 152 us
  waiting for transfers between devices  62 us (41%)
  Pallas kernels  44 us (29%)
  starting transfers between devices  22.3 us (15%)
  local copies, waits for them, and re-layouts  20.6 us (14%)
  other arithmetic  1.81 us (1%)
    ppermute x8, waiting for transfers between devices, along(): lax.ppermute(x, 'expert', [(i, (i + 2 * by) % expert_size) for i in range...  47.5 us
    unnamed x28, local copies, waits for them, and re-layouts  20.6 us
    pallas_call x6, Pallas kernels, apply_rows(): pl.pallas_call(functools.partial(apply_kernel, spread, seats), grid_spec=...  18.8 us
    ppermute x8, starting transfers between devices, along(): lax.ppermute(x, 'expert', [(i, (i + 2 * by) % expert_size) for i in range...  15.9 us
    ppermute x4, waiting for transfers between devices, over_dp(): return lax.ppermute(x, 'dp', [(i, i ^ bit) for i in range(dp_size)])  14.6 us
    pallas_call x1, Pallas kernels, iterations(): pl.pallas_call(iterate_kernel, in_specs=[pl.BlockSpec(memory_space=pltpu....  12.2 us
    pallas_call x4, Pallas kernels, gram_parts(): pl.pallas_call(gram_kernel, grid_spec=pltpu.PrefetchScalarGridSpec(num_sc...  9.84 us
    ppermute x4, starting transfers between devices, over_dp(): return lax.ppermute(x, 'dp', [(i, i ^ bit) for i in range(dp_size)])  5.19 us
  transfers between devices with their start and end apart: 19, of which 8 were waited for; matrix products, arithmetic and copies ran while one was open for 0% of the time, Pallas kernels for 15%

profile of v1, /device:TPU:0, one launch (start us, length us, event | category | flops | bytes accessed | tf_op | source)
XLA Modules:
  0.0 151.6 jit_solution(18101250669789888369)
XLA Ops:
  7.9 3.7 %gram_parts.5 = (bf16[3,640,512]{2,1,0:T(8,128)(2,1)S(1)}, f32[3,1288,128]{2,1,0:T(8,128)}) custom-call(s32[3]{0:T(128)S(1)} %pad_add_fusion.2.ids, s32[8]{0:T(128)S(1)} %bitcast.34, bf16[8,640,512]{2,1,0:T(8,128)(2,1)S(1)} %bitcast.26, bf16[8,640,512]{2,1,0:T(8,128)(2,1)S(1)} %bitcast.30, f32[8,8,128]{2,1,0:T(8,128)S(1)} %select_select_fusion.aux_ref), custom_call_target="tpu_custom_call" | custom-call | flops 1006632960 | bytes 7876608 | tf_op jit(solution)/shard_map/gram_parts/pallas_call | solution.py:76
  12.1 2.5 %copy-done.1 = bf16[1,8,640,512]{3,2,1,0:T(8,128)(2,1)S(1)} copy-done((bf16[1,8,640,512]{3,2,1,0:T(8,128)(2,1)S(1)}, bf16[1,8,640,512]{3,2,1,0:T(8,128)(2,1)}, u32[]{:S(2)}) %copy-start.1) | copy-done | bytes 5242904
  14.6 2.5 %copy-done.5 = bf16[1,8,640,512]{3,2,1,0:T(8,128)(2,1)S(1)} copy-done((bf16[1,8,640,512]{3,2,1,0:T(8,128)(2,1)S(1)}, bf16[1,8,640,512]{3,2,1,0:T(8,128)(2,1)}, u32[]{:S(2)}) %copy-start.5) | copy-done | bytes 5242904
  21.7 2.5 %copy-done.6 = bf16[1,8,640,512]{3,2,1,0:T(8,128)(2,1)S(1)} copy-done((bf16[1,8,640,512]{3,2,1,0:T(8,128)(2,1)S(1)}, bf16[1,8,640,512]{3,2,1,0:T(8,128)(2,1)}, u32[]{:S(2)}) %copy-start.6) | copy-done | bytes 5242904
  26.5 3.0 %collective-permute-start.2 = (f32[648,128]{1,0:T(8,128)}, f32[648,128]{1,0:T(8,128)S(1)}, u32[]{:S(2)}, u32[]{:S(2)}) collective-permute-start(f32[648,128]{1,0:T(8,128)} %get-tuple-element.35), channel_id=1, source_target_pairs={{0,2},{1,3},{2,4},{3,5},{4,6},{5,7},{6,0},{7,1},{8,10},{9,11},{10,... | collective-permute-start | bytes 995336 | tf_op jit(solution)/shard_map/ppermute | solution.py:383
  31.7 2.5 %copy-done.3 = bf16[1,8,640,512]{3,2,1,0:T(8,128)(2,1)S(1)} copy-done((bf16[1,8,640,512]{3,2,1,0:T(8,128)(2,1)S(1)}, bf16[1,8,640,512]{3,2,1,0:T(8,128)(2,1)}, u32[]{:S(2)}) %copy-start.3) | copy-done | bytes 5242904
  36.6 2.8 %gram_parts.4 = (bf16[3,640,512]{2,1,0:T(8,128)(2,1)S(1)}, f32[3,1288,128]{2,1,0:T(8,128)S(1)}) custom-call(s32[3]{0:T(128)S(1)} %pad_add_fusion.1.ids, s32[8]{0:T(128)S(1)} %bitcast.37, bf16[8,640,512]{2,1,0:T(8,128)(2,1)S(1)} %bitcast.29, bf16[8,640,512]{2,1,0:T(8,128)(2,1)S(1)} %bitcast.33, f32[8,8,128]{2,1,0:T(8,128)S(1)} %select_select_fusion.aux_ref), custom_call_target="tpu_custom_call" | custom-call | flops 1006632960 | bytes 7876608 | tf_op jit(solution)/shard_map/gram_parts/pallas_call | solution.py:76
  39.4 6.8 %collective-permute-done.3.from_right = f32[640,128]{1,0:T(8,128)S(1)} collective-permute-done((f32[640,128]{1,0:T(8,128)}, f32[640,128]{1,0:T(8,128)S(1)}, u32[]{:S(2)}, u32[]{:S(2)}) %collective-permute-start.3) | collective-permute-done | bytes 327712 | tf_op jit(solution)/shard_map/ppermute | solution.py:383
  49.3 2.7 %collective-permute-start.5 = (f32[1288,128]{1,0:T(8,128)S(1)}, f32[1288,128]{1,0:T(8,128)S(1)}, u32[]{:S(2)}, u32[]{:S(2)}) collective-permute-start(f32[1288,128]{1,0:T(8,128)S(1)} %get-tuple-element.39), channel_id=1, source_target_pairs={{0,6},{1,7},{2,0},{3,1},{4,2},{5,3},{6,4},{7,5},{8,14},{9,15},{10,... | collective-permute-start | bytes 1978376 | tf_op jit(solution)/shard_map/ppermute | solution.py:383
  52.0 15.7 %collective-permute-done.4.from_left = f32[1288,128]{1,0:T(8,128)S(1)} collective-permute-done((f32[1288,128]{1,0:T(8,128)S(1)}, f32[1288,128]{1,0:T(8,128)S(1)}, u32[]{:S(2)}, u32[]{:S(2)}) %collective-permute-start.4) | collective-permute-done | bytes 659488 | tf_op jit(solution)/shard_map/ppermute | solution.py:383
  67.7 12.2 %collective-permute-done.5.from_right = f32[1288,128]{1,0:T(8,128)S(1)} collective-permute-done((f32[1288,128]{1,0:T(8,128)S(1)}, f32[1288,128]{1,0:T(8,128)S(1)}, u32[]{:S(2)}, u32[]{:S(2)}) %collective-permute-start.5) | collective-permute-done | bytes 659488 | tf_op jit(solution)/shard_map/ppermute | solution.py:383
  83.1 7.4 %collective-permute-done.7.second_other = f32[640,128]{1,0:T(8,128)S(1)} collective-permute-done((f32[640,128]{1,0:T(8,128)S(1)}, f32[640,128]{1,0:T(8,128)S(1)}, u32[]{:S(2)}, u32[]{:S(2)}) %collective-permute-start.7) | collective-permute-done | bytes 327712 | tf_op jit(solution)/shard_map/ppermute | solution.py:386
  92.7 7.2 %collective-permute-done.9.second_other = f32[640,128]{1,0:T(8,128)S(1)} collective-permute-done((f32[640,128]{1,0:T(8,128)S(1)}, f32[640,128]{1,0:T(8,128)S(1)}, u32[]{:S(2)}, u32[]{:S(2)}) %collective-permute-start.9) | collective-permute-done | bytes 327712 | tf_op jit(solution)/shard_map/ppermute | solution.py:386
  99.9 12.2 %iterations.1.refs_0_ = bf16[1312,128]{1,0:T(8,128)(2,1)S(1)} custom-call(f32[648,128]{1,0:T(8,128)S(1)} %get-tuple-element.42.first, f32[648,128]{1,0:T(8,128)S(1)} %collective-permute-done.8.first_other, f32[640,128]{1,0:T(8,128)S(1)} %get-tuple-element.43.second, f32[640,128]{1,0:T(8,128)S(1)} %collective-permute-done.9.second_other), custom_call_target="tpu_custom_call" | custom-call | flops 12079595520 | bytes 2637824 | tf_op jit(solution)/shard_map/iterations/pallas_call | solution.py:232
  112.7 3.3 %collective-permute-start.13 = (bf16[1312,128]{1,0:T(8,128)(2,1)S(1)}, bf16[1312,128]{1,0:T(8,128)(2,1)S(1)}, u32[]{:S(2)}, u32[]{:S(2)}) collective-permute-start(bf16[1312,128]{1,0:T(8,128)(2,1)S(1)} %iterations.1.refs_0_), channel_id=1, source_target_pairs={{0,6},{1,7},{2,0},{3,1},{4,2},{5,3},{6,4},{7,5},{8,14},{9,15},{10,... | collective-permute-start | bytes 1007624 | tf_op jit(solution)/shard_map/ppermute | solution.py:383
  116.1 8.8 %collective-permute-done.10.refs_1_ = bf16[1312,128]{1,0:T(8,128)(2,1)S(1)} collective-permute-done((bf16[1312,128]{1,0:T(8,128)(2,1)S(1)}, bf16[1312,128]{1,0:T(8,128)(2,1)S(1)}, u32[]{:S(2)}, u32[]{:S(2)}) %collective-permute-start.10) | collective-permute-done | bytes 335904 | tf_op jit(solution)/shard_map/ppermute | solution.py:383
  124.9 3.6 %collective-permute-done.13.refs_0_ = bf16[1312,128]{1,0:T(8,128)(2,1)S(1)} collective-permute-done((bf16[1312,128]{1,0:T(8,128)(2,1)S(1)}, bf16[1312,128]{1,0:T(8,128)(2,1)S(1)}, u32[]{:S(2)}, u32[]{:S(2)}) %collective-permute-start.13) | collective-permute-done | bytes 335904 | tf_op jit(solution)/shard_map/ppermute | solution.py:383
  128.5 3.1 %collective-permute-start.14 = (bf16[656,128]{1,0:T(8,128)(2,1)S(1)}, bf16[656,128]{1,0:T(8,128)(2,1)S(1)}, u32[]{:S(2)}, u32[]{:S(2)}) collective-permute-start(bf16[656,128]{1,0:T(8,128)(2,1)S(1)} %slice.9), channel_id=1, source_target_pairs={{0,6},{1,7},{2,0},{3,1},{4,2},{5,3},{6,4},{7,5},{8,14},{9,15},{10,... | collective-permute-start | bytes 503816 | tf_op jit(solution)/shard_map/ppermute | solution.py:383
  132.3 2.7 %apply_rows.6 = (bf16[8,640,512]{2,1,0:T(8,128)(2,1)}, bf16[8,640,512]{2,1,0:T(8,128)(2,1)}) custom-call(s32[1]{0:T(128)} %bitcast.6.ids, s32[8]{0:T(128)S(1)} %bitcast.38, s32[2]{0:T(128)S(1)} %pad_add_fusion.me, bf16[1312,128]{1,0:T(8,128)(2,1)S(1)} %iterations.1.refs_0_, bf16[3,640,512]{2,1,0:T(8,128)(2,1)S(1)} %get-tuple-element.47.refs_1_.refs_2_, ...), custom_call_target="tpu_custom_call" | custom-call | flops 335544320 | bytes 2621440 | tf_op jit(solution)/shard_map/apply_rows/pallas_call | solution.py:343
  135.5 2.7 %apply_rows.7 = (bf16[8,640,512]{2,1,0:T(8,128)(2,1)}, bf16[8,640,512]{2,1,0:T(8,128)(2,1)}) custom-call(s32[1]{0:T(128)} %bitcast.12.ids, s32[8]{0:T(128)S(1)} %bitcast.39, s32[2]{0:T(128)S(1)} %pad_add_fusion.me, bf16[1312,128]{1,0:T(8,128)(2,1)S(1)} %collective-permute-done.18.refs_0_, ...), custom_call_target="tpu_custom_call", output_to_operand_aliasing={{0}: (6, {}), {1}: (7, {})} | custom-call | flops 335544320 | bytes 2621440 | tf_op jit(solution)/shard_map/apply_rows/pallas_call | solution.py:343
  138.2 4.0 %apply_rows.8 = (bf16[8,640,512]{2,1,0:T(8,128)(2,1)}, bf16[8,640,512]{2,1,0:T(8,128)(2,1)}) custom-call(s32[2]{0:T(128)S(1)} %pad_add_fusion.4.ids, s32[8]{0:T(128)S(1)} %bitcast.40, s32[2]{0:T(128)S(1)} %pad_add_fusion.me, bf16[1312,128]{1,0:T(8,128)(2,1)S(1)} %collective-permute-done.13.refs_0_, ...), custom_call_target="tpu_custom_call", output_to_operand_aliasing={{0}: (7, {}), {1}: (8, {})} | custom-call | flops 671088640 | bytes 5242880 | tf_op jit(solution)/shard_map/apply_rows/pallas_call | solution.py:343
  142.2 4.0 %apply_rows.9 = (bf16[8,640,512]{2,1,0:T(8,128)(2,1)}, bf16[8,640,512]{2,1,0:T(8,128)(2,1)}) custom-call(s32[2]{0:T(128)S(1)} %pad_add_fusion.3.ids, s32[8]{0:T(128)S(1)} %bitcast.41, s32[2]{0:T(128)S(1)} %pad_add_fusion.me, bf16[1312,128]{1,0:T(8,128)(2,1)S(1)} %collective-permute-done.16.refs_0_, ...), custom_call_target="tpu_custom_call", output_to_operand_aliasing={{0}: (7, {}), {1}: (8, {})} | custom-call | flops 671088640 | bytes 5242880 | tf_op jit(solution)/shard_map/apply_rows/pallas_call | solution.py:343
  146.2 2.7 %apply_rows.10 = (bf16[8,640,512]{2,1,0:T(8,128)(2,1)}, bf16[8,640,512]{2,1,0:T(8,128)(2,1)}) custom-call(s32[1]{0:T(128)} %bitcast.13.ids, s32[8]{0:T(128)S(1)} %bitcast.42, s32[2]{0:T(128)S(1)} %pad_add_fusion.me, bf16[656,128]{1,0:T(8,128)(2,1)S(1)} %collective-permute-done.11.refs_0_, ...), custom_call_target="tpu_custom_call", output_to_operand_aliasing={{0}: (7, {}), {1}: (8, {})} | custom-call | flops 335544320 | bytes 2621440 | tf_op jit(solution)/shard_map/apply_rows/pallas_call | solution.py:343
  148.9 2.7 %apply_rows.11 = (bf16[8,640,512]{2,1,0:T(8,128)(2,1)}, bf16[8,640,512]{2,1,0:T(8,128)(2,1)}) custom-call(s32[1]{0:T(128)} %bitcast.ids, s32[8]{0:T(128)S(1)} %bitcast.43, s32[2]{0:T(128)S(1)} %pad_add_fusion.me, bf16[656,128]{1,0:T(8,128)(2,1)S(1)} %collective-permute-done.12.refs_0_, ...), custom_call_target="tpu_custom_call", output_to_operand_aliasing={{0}: (7, {}), {1}: (8, {})} | custom-call | flops 335544320 | bytes 2621440 | tf_op jit(solution)/shard_map/apply_rows/pallas_call | solution.py:343
  (70 shorter events, 29.6 us)
Async XLA Ops:
  2.3 2.5 %copy-start = (bf16[1,8,640,512]{3,2,1,0:T(8,128)(2,1)S(1)}, bf16[1,8,640,512]{3,2,1,0:T(8,128)(2,1)}, u32[]{:S(2)}) copy-start(bf16[1,8,640,512]{3,2,1,0:T(8,128)(2,1)} %param.5) | copy-start | bytes 15728644
  7.9 4.2 %copy-start.11 = (s32[1,8,1]{1,2,0:T(1,128)S(1)}, s32[1,8,1]{1,2,0:T(1,128)}, u32[]{:S(2)}) copy-start(s32[1,8,1]{1,2,0:T(1,128)} %param.8) | copy-start | bytes 100
  11.6 34.6 %collective-permute-start = (f32[3,1288,128]{2,1,0:T(8,128)}, f32[3,1288,128]{2,1,0:T(8,128)}, u32[]{:S(2)}, u32[]{:S(2)}) collective-permute-start(f32[3,1288,128]{2,1,0:T(8,128)} %get-tuple-element.32), channel_id=1, source_target_pairs={{0,1},{1,0},{2,3},{3,2},{4,5},{5,4},{6,7},{7,6},{8,9},{9,8},{10,11... | collective-permute-start | bytes 5935112 | tf_op jit(solution)/shard_map/ppermute | solution.py:380
  19.2 6.3 %collective-permute-start.1 = (f32[1,1288,128]{2,1,0:T(8,128)}, f32[1,1288,128]{2,1,0:T(8,128)S(1)}, u32[]{:S(2)}, u32[]{:S(2)}) collective-permute-start(f32[1,1288,128]{2,1,0:T(8,128)} %get-tuple-element.34), channel_id=1, source_target_pairs={{0,1},{1,0},{2,3},{3,2},{4,5},{5,4},{6,7},{7,6},{8,9},{9,8},{10,11... | collective-permute-start | bytes 1978376 | tf_op jit(solution)/shard_map/ppermute | solution.py:380
  26.5 19.7 %collective-permute-start.2 = (f32[648,128]{1,0:T(8,128)}, f32[648,128]{1,0:T(8,128)S(1)}, u32[]{:S(2)}, u32[]{:S(2)}) collective-permute-start(f32[648,128]{1,0:T(8,128)} %get-tuple-element.35), channel_id=1, source_target_pairs={{0,2},{1,3},{2,4},{3,5},{4,6},{5,7},{6,0},{7,1},{8,10},{9,11},{10,... | collective-permute-start | bytes 995336 | tf_op jit(solution)/shard_map/ppermute | solution.py:383
  29.6 16.7 %collective-permute-start.3 = (f32[640,128]{1,0:T(8,128)}, f32[640,128]{1,0:T(8,128)S(1)}, u32[]{:S(2)}, u32[]{:S(2)}) collective-permute-start(f32[640,128]{1,0:T(8,128)} %get-tuple-element.36), channel_id=1, source_target_pairs={{0,6},{1,7},{2,0},{3,1},{4,2},{5,3},{6,4},{7,5},{8,14},{9,15},{10,... | collective-permute-start | bytes 983048 | tf_op jit(solution)/shard_map/ppermute | solution.py:383
  48.1 19.6 %collective-permute-start.4 = (f32[1288,128]{1,0:T(8,128)S(1)}, f32[1288,128]{1,0:T(8,128)S(1)}, u32[]{:S(2)}, u32[]{:S(2)}) collective-permute-start(f32[1288,128]{1,0:T(8,128)S(1)} %get-tuple-element.38), channel_id=1, source_target_pairs={{0,2},{1,3},{2,4},{3,5},{4,6},{5,7},{6,0},{7,1},{8,10},{9,11},{10,... | collective-permute-start | bytes 1978376 | tf_op jit(solution)/shard_map/ppermute | solution.py:383
  49.3 30.6 %collective-permute-start.5 = (f32[1288,128]{1,0:T(8,128)S(1)}, f32[1288,128]{1,0:T(8,128)S(1)}, u32[]{:S(2)}, u32[]{:S(2)}) collective-permute-start(f32[1288,128]{1,0:T(8,128)S(1)} %get-tuple-element.39), channel_id=1, source_target_pairs={{0,6},{1,7},{2,0},{3,1},{4,2},{5,3},{6,4},{7,5},{8,14},{9,15},{10,... | collective-permute-start | bytes 1978376 | tf_op jit(solution)/shard_map/ppermute | solution.py:383
  80.0 10.5 %collective-permute-start.6 = (f32[648,128]{1,0:T(8,128)S(1)}, f32[648,128]{1,0:T(8,128)S(1)}, u32[]{:S(2)}, u32[]{:S(2)}) collective-permute-start(f32[648,128]{1,0:T(8,128)S(1)} %get-tuple-element.40.first), channel_id=1, source_target_pairs={{0,8},{8,0},{16,24},{24,16},{1,9},{9,1},{17,25},{25,17},{2,10},{10... | collective-permute-start | bytes 995336 | tf_op jit(solution)/shard_map/ppermute | solution.py:386
  81.6 8.9 %collective-permute-start.7 = (f32[640,128]{1,0:T(8,128)S(1)}, f32[640,128]{1,0:T(8,128)S(1)}, u32[]{:S(2)}, u32[]{:S(2)}) collective-permute-start(f32[640,128]{1,0:T(8,128)S(1)} %get-tuple-element.41.second), channel_id=1, source_target_pairs={{0,16},{8,24},{16,0},{24,8},{1,17},{9,25},{17,1},{25,9},{2,18},{10... | collective-permute-start | bytes 983048 | tf_op jit(solution)/shard_map/ppermute | solution.py:386
  90.6 9.3 %collective-permute-start.8 = (f32[648,128]{1,0:T(8,128)S(1)}, f32[648,128]{1,0:T(8,128)S(1)}, u32[]{:S(2)}, u32[]{:S(2)}) collective-permute-start(f32[648,128]{1,0:T(8,128)S(1)} %get-tuple-element.42.first), channel_id=1, source_target_pairs={{0,16},{8,24},{16,0},{24,8},{1,17},{9,25},{17,1},{25,9},{2,18},{10... | collective-permute-start | bytes 995336 | tf_op jit(solution)/shard_map/ppermute | solution.py:386
  92.1 40.1 %slice-start = ((s8[5242880]{0:T(1024)(128)(4,1)}), s8[4194304]{0:T(1024)(128)(4,1)S(1)}, s32[]{:S(2)}) async-start(s8[5242880]{0:T(1024)(128)(4,1)} %bitcast.18), calls=%async_computation | async-start | bytes 8388608
  92.1 40.1 %slice-start.1 = ((s8[5242880]{0:T(1024)(128)(4,1)}), s8[1048576]{0:T(1024)(128)(4,1)S(1)}, s32[]{:S(2)}) async-start(s8[5242880]{0:T(1024)(128)(4,1)} %bitcast.18), calls=%async_computation.1 | async-start | bytes 2097152
  92.2 7.7 %collective-permute-start.9 = (f32[640,128]{1,0:T(8,128)S(1)}, f32[640,128]{1,0:T(8,128)S(1)}, u32[]{:S(2)}, u32[]{:S(2)}) collective-permute-start(f32[640,128]{1,0:T(8,128)S(1)} %get-tuple-element.43.second), channel_id=1, source_target_pairs={{0,8},{8,0},{16,24},{24,16},{1,9},{9,1},{17,25},{25,17},{2,10},{10... | collective-permute-start | bytes 983048 | tf_op jit(solution)/shard_map/ppermute | solution.py:386
  112.1 12.7 %collective-permute-start.10 = (bf16[1312,128]{1,0:T(8,128)(2,1)S(1)}, bf16[1312,128]{1,0:T(8,128)(2,1)S(1)}, u32[]{:S(2)}, u32[]{:S(2)}) collective-permute-start(bf16[1312,128]{1,0:T(8,128)(2,1)S(1)} %iterations.1.refs_0_), channel_id=1, source_target_pairs={{0,2},{1,3},{2,4},{3,5},{4,6},{5,7},{6,0},{7,1},{8,10},{9,11},{10,... | collective-permute-start | bytes 1007624 | tf_op jit(solution)/shard_map/ppermute | solution.py:383
  112.7 15.8 %collective-permute-start.13 = (bf16[1312,128]{1,0:T(8,128)(2,1)S(1)}, bf16[1312,128]{1,0:T(8,128)(2,1)S(1)}, u32[]{:S(2)}, u32[]{:S(2)}) collective-permute-start(bf16[1312,128]{1,0:T(8,128)(2,1)S(1)} %iterations.1.refs_0_), channel_id=1, source_target_pairs={{0,6},{1,7},{2,0},{3,1},{4,2},{5,3},{6,4},{7,5},{8,14},{9,15},{10,... | collective-permute-start | bytes 1007624 | tf_op jit(solution)/shard_map/ppermute | solution.py:383
  116.0 19.5 %collective-permute-start.18 = (bf16[1312,128]{1,0:T(8,128)(2,1)S(1)}, bf16[1312,128]{1,0:T(8,128)(2,1)S(1)}, u32[]{:S(2)}, u32[]{:S(2)}) collective-permute-start(bf16[1312,128]{1,0:T(8,128)(2,1)S(1)} %iterations.1.refs_0_), channel_id=1, source_target_pairs={{0,1},{1,0},{2,3},{3,2},{4,5},{5,4},{6,7},{7,6},{8,9},{9,8},{10,11... | collective-permute-start | bytes 1007624 | tf_op jit(solution)/shard_map/ppermute | solution.py:380
  124.9 10.1 %collective-permute-start.11 = (bf16[656,128]{1,0:T(8,128)(2,1)S(1)}, bf16[656,128]{1,0:T(8,128)(2,1)S(1)}, u32[]{:S(2)}, u32[]{:S(2)}) collective-permute-start(bf16[656,128]{1,0:T(8,128)(2,1)S(1)} %slice.8), channel_id=1, source_target_pairs={{0,2},{1,3},{2,4},{3,5},{4,6},{5,7},{6,0},{7,1},{8,10},{9,11},{10,... | collective-permute-start | bytes 503816 | tf_op jit(solution)/shard_map/ppermute | solution.py:383
  128.5 6.8 %collective-permute-start.14 = (bf16[656,128]{1,0:T(8,128)(2,1)S(1)}, bf16[656,128]{1,0:T(8,128)(2,1)S(1)}, u32[]{:S(2)}, u32[]{:S(2)}) collective-permute-start(bf16[656,128]{1,0:T(8,128)(2,1)S(1)} %slice.9), channel_id=1, source_target_pairs={{0,6},{1,7},{2,0},{3,1},{4,2},{5,3},{6,4},{7,5},{8,14},{9,15},{10,... | collective-permute-start | bytes 503816 | tf_op jit(solution)/shard_map/ppermute | solution.py:383
  131.6 10.6 %collective-permute-start.16 = (bf16[1312,128]{1,0:T(8,128)(2,1)S(1)}, bf16[1312,128]{1,0:T(8,128)(2,1)S(1)}, u32[]{:S(2)}, u32[]{:S(2)}) collective-permute-start(bf16[1312,128]{1,0:T(8,128)(2,1)S(1)} %collective-permute-done.13.refs_0_), channel_id=1, source_target_pairs={{0,1},{1,0},{2,3},{3,2},{4,5},{5,4},{6,7},{7,6},{8,9},{9,8},{10,11... | collective-permute-start | bytes 1007624 | tf_op jit(solution)/shard_map/ppermute | solution.py:380
  131.6 10.6 %collective-permute-start.17 = (bf16[1312,128]{1,0:T(8,128)(2,1)S(1)}, bf16[1312,128]{1,0:T(8,128)(2,1)S(1)}, u32[]{:S(2)}, u32[]{:S(2)}) collective-permute-start(bf16[1312,128]{1,0:T(8,128)(2,1)S(1)} %collective-permute-done.10.refs_1_), channel_id=1, source_target_pairs={{0,1},{1,0},{2,3},{3,2},{4,5},{5,4},{6,7},{7,6},{8,9},{9,8},{10,11... | collective-permute-start | bytes 1007624 | tf_op jit(solution)/shard_map/ppermute | solution.py:380
  135.0 13.9 %collective-permute-start.12 = (bf16[656,128]{1,0:T(8,128)(2,1)S(1)}, bf16[656,128]{1,0:T(8,128)(2,1)S(1)}, u32[]{:S(2)}, u32[]{:S(2)}) collective-permute-start(bf16[656,128]{1,0:T(8,128)(2,1)S(1)} %collective-permute-done.11.refs_0_), channel_id=1, source_target_pairs={{0,1},{1,0},{2,3},{3,2},{4,5},{5,4},{6,7},{7,6},{8,9},{9,8},{10,11... | collective-permute-start | bytes 503816 | tf_op jit(solution)/shard_map/ppermute | solution.py:380
  135.4 13.6 %collective-permute-start.15 = (bf16[656,128]{1,0:T(8,128)(2,1)S(1)}, bf16[656,128]{1,0:T(8,128)(2,1)S(1)}, u32[]{:S(2)}, u32[]{:S(2)}) collective-permute-start(bf16[656,128]{1,0:T(8,128)(2,1)S(1)} %collective-permute-done.14.refs_1_), channel_id=1, source_target_pairs={{0,1},{1,0},{2,3},{3,2},{4,5},{5,4},{6,7},{7,6},{8,9},{9,8},{10,11... | collective-permute-start | bytes 503816 | tf_op jit(solution)/shard_map/ppermute | solution.py:380
  142.2 4.0 %copy-start.9 = (bf16[1,640,512]{2,1,0:T(8,128)(2,1)S(1)}, bf16[1,640,512]{2,1,0:T(8,128)(2,1)}, u32[]{:S(2)}) copy-start(bf16[1,640,512]{2,1,0:T(8,128)(2,1)} %copy-done.8) | copy-start | bytes 1966084
  (9 other events, 19.1 us)

commit v2 on v0

v2 whole, which is shorter than its diff:
```python
import functools
import math

import jax
import jax.numpy as jnp
from jax import lax
from jax.experimental import pallas as pl
from jax.experimental.pallas import tpu as pltpu
from jax.sharding import PartitionSpec as P

KV_RANK = 512
NOPE = 128
VDIM = 128
NS_ITERS = 5
KV_ROWS = 16384

momentum_coef = 0.95
learn_rate = 0.02
decay_rate = 0.1
clip_limit = 100.0
coef_first = 3.4445
coef_second = -4.775
coef_third = 2.0315

f32 = jnp.float32
bf16 = jnp.bfloat16
i16 = jnp.int16
i32 = jnp.int32

LANES = 128
BLOCKS = KV_RANK // LANES
HALVES = (
    ((0, 1, True), (0, 1, False), (0, 2, False), (1, 2, False)),
    ((2, 3, True), (0, 3, False), (1, 3, False), (2, 3, False)),
)
AUX = 8
HALF = AUX + 4 * LANES
AUX_CODE = 16
HALF_CODE = AUX_CODE + 4 * LANES
AUX_P = 32
HEAD_P = AUX_P + 4 * LANES
ROWS_P = AUX_P + 8 * LANES
UNIT = 32000.0


def params(mebibytes=40):
    return pltpu.CompilerParams(vmem_limit_bytes=mebibytes * 1024 * 1024)


def whole(shape):
    return pl.BlockSpec(shape, lambda *_: (0,) * len(shape))


def square_iotas():
    row = lax.broadcasted_iota(i32, (LANES, LANES), 0)
    col = lax.broadcasted_iota(i32, (LANES, LANES), 1)
    return row, col


def layer_of(me, relative, own_core):
    core = me[1] if own_core else 1 - me[1]
    return 2 * (me[0] ^ relative) + core


def gram_kernel(own_core, me, counts, grad_ref, mom_ref, peaks_ref, *refs):
    nes_ref, gram_ref = refs[-2:]
    layer = layer_of(me, pl.program_id(0), own_core)
    count = counts[layer]
    gradient = grad_ref[0].astype(f32)
    velocity = momentum_coef * mom_ref[0].astype(f32) + gradient
    nesterov = gradient + momentum_coef * velocity
    slot = lax.broadcasted_iota(i32, nesterov.shape, 0)
    rows = jnp.where(slot < count, nesterov, 0.0).astype(bf16)
    nes_ref[0] = rows
    half = KV_RANK // 2
    dims = (((0,), (0,)), ((), ()))
    upper = lax.dot_general(rows[:, :half], rows, dims, preferred_element_type=f32)
    lower = lax.dot_general(rows[:, half:], rows[:, half:], dims, preferred_element_type=f32)

    def block(i, j):
        if i < 2:
            return upper[i * LANES : (i + 1) * LANES, j * LANES : (j + 1) * LANES]
        return lower[(i - 2) * LANES : (i - 1) * LANES, (j - 2) * LANES : (j - 1) * LANES]

    row, col = square_iotas()
    line = lax.broadcasted_iota(i32, (AUX, LANES), 0)
    lane = lax.broadcasted_iota(i32, (AUX, LANES), 1)
    aux = jnp.where((line == 5) & (lane == me[2]), count.astype(f32), 0.0)
    peaks = peaks_ref[...].astype(f32)
    pick = lax.broadcasted_iota(i32, peaks.shape, 0) == layer
    peaks = jnp.sum(jnp.where(pick, peaks, 0.0), axis=0, keepdims=True)
    peaks = jnp.concatenate([peaks, jnp.zeros((1, LANES - peaks.shape[1]), f32)], axis=1)
    aux = jnp.where(line == 4, peaks, aux)
    for i in range(BLOCKS):
        diagonal = jnp.sum(jnp.where(row == col, block(i, i), 0.0), axis=0, keepdims=True)
        aux = jnp.where(line == i, diagonal, aux)
    for number, entries in enumerate(HALVES):
        base = number * HALF
        gram_ref[0, base : base + AUX, :] = aux
        for place, (i, j, triangle) in enumerate(entries):
            at = base + AUX + place * LANES
            value = jnp.where(row <= col, block(i, i), block(j, j)) if triangle else block(i, j)
            gram_ref[0, at : at + LANES, :] = value


def gram_parts(own_core, me, counts, grad, mom, peaks, nes):
    layers, capacity, features = grad.shape
    number = layers // 2
    picked = lambda i, me, counts: (layer_of(me, i, own_core), 0, 0)
    in_specs = [
        pl.BlockSpec((1, capacity, features), picked),
        pl.BlockSpec((1, capacity, features), picked),
        whole(peaks.shape),
    ]
    args = [grad, mom, peaks]
    aliases = {}
    if nes is not None:
        in_specs.append(pl.BlockSpec(memory_space=pl.ANY))
        args.append(nes)
        aliases = {5: 0}
    return pl.pallas_call(
        functools.partial(gram_kernel, own_core),
        grid_spec=pltpu.PrefetchScalarGridSpec(
            num_scalar_prefetch=2,
            grid=(number,),
            in_specs=in_specs,
            out_specs=[
                pl.BlockSpec((1, capacity, features), picked),
                pl.BlockSpec((1, 2 * HALF, LANES), lambda i, me, counts: (i, 0, 0)),
            ],
        ),
        out_shape=[
            jax.ShapeDtypeStruct((layers, capacity, features), bf16),
            jax.ShapeDtypeStruct((number, 2 * HALF, LANES), f32),
        ],
        input_output_aliases=aliases,
        compiler_params=params(60),
        cost_estimate=pl.CostEstimate(
            flops=number * capacity * features * features * 2,
            bytes_accessed=number * (capacity * features * 6 + 2 * HALF * LANES * 4),
            transcendentals=0,
        ),
        name="gram_parts",
    )(me, counts, *args)


def joined(first, second):
    line = lax.broadcasted_iota(i32, (AUX, LANES), 0)
    aux = jnp.where(line == 4, jnp.maximum(first[0], second[0]), first[0] + second[0])
    return [aux] + [x + y for x, y in zip(first[1:], second[1:])]


def load_half(ref, index, base=0):
    starts = [base + AUX + place * LANES for place in range(4)]
    return [ref[index, base : base + AUX, :]] + [ref[index, at : at + LANES, :] for at in starts]


def store_half(ref, index, half):
    ref[index, 0:AUX, :] = half[0]
    for place in range(4):
        at = AUX + place * LANES
        ref[index, at : at + LANES, :] = half[1 + place]


def outer_scales(which, scale):
    row, col = square_iotas()
    across = [scale[g : g + 1] for g in range(BLOCKS)]
    down = {}

    def outer(i, j):
        if i not in down:
            down[i] = jnp.broadcast_to(across[i], (LANES, LANES)).T
        return down[i] * across[j]

    return [
        jnp.where(row <= col, outer(i, i), outer(j, j)) if triangle else outer(i, j)
        for i, j, triangle in HALVES[which]
    ]


def decoded(which, ref, index):
    line = lax.broadcasted_iota(i32, (AUX, LANES), 0)
    codes = ref[index, 0:AUX_CODE, :].astype(i32).astype(f32)
    low, high = codes[0:AUX], codes[AUX:AUX_CODE]
    scale = jnp.where(line < 4, jnp.exp2(low) * jnp.sqrt(high * (1.0 / UNIT)), 0.0)
    aux = jnp.where(line < 4, scale * scale, jnp.where(line == 4, low * (1.0 / 64.0), low))
    half = [aux]
    for place, factor in enumerate(outer_scales(which, scale)):
        at = AUX_CODE + place * LANES
        half.append(ref[index, at : at + LANES, :].astype(i32).astype(f32) * (factor * (1.0 / UNIT)))
    return half


def encode(which, ref, index, half):
    line = lax.broadcasted_iota(i32, (AUX, LANES), 0)
    aux = half[0]
    diagonal = jnp.maximum(aux, 1e-30)
    power = jnp.ceil(0.5 * jnp.log2(diagonal))
    high = jnp.clip(jnp.floor(diagonal * jnp.exp2(-2.0 * power) * UNIT + 0.5), 1.0, 32767.0)
    low = jnp.where(line < 4, power, jnp.where(line == 4, jnp.floor(aux * 64.0 + 0.5), aux))
    high = jnp.where(line < 4, high, 0.0)
    ref[index, 0:AUX_CODE, :] = jnp.concatenate([low, high], axis=0).astype(i32).astype(i16)
    inverse = jnp.where(line < 4, jnp.exp2(-power) * lax.rsqrt(high * (1.0 / UNIT)), 0.0)
    for place, factor in enumerate(outer_scales(which, inverse)):
        at = AUX_CODE + place * LANES
        value = jnp.floor(half[1 + place] * (factor * UNIT) + 0.5)
        value = jnp.clip(value, -32767.0, 32767.0)
        ref[index, at : at + LANES, :] = value.astype(i32).astype(i16)


def local_call(kernel, out_shapes, name, *args):
    size = sum(math.prod(x.shape) * x.dtype.itemsize for x in list(args) + list(out_shapes))
    return pl.pallas_call(
        kernel,
        in_specs=[pl.BlockSpec(memory_space=pltpu.VMEM)] * len(args),
        out_specs=[pl.BlockSpec(memory_space=pltpu.VMEM)] * len(out_shapes),
        out_shape=list(out_shapes),
        compiler_params=params(),
        cost_estimate=pl.CostEstimate(flops=size * 4, bytes_accessed=size, transcendentals=0),
        name=name,
    )(*args)


def first_kernel(sends, keeps, kept, arrived, *refs):
    for which in range(2):
        message, stay = refs[2 * which : 2 * which + 2]
        for index in range(kept.shape[0]):
            base = which * HALF
            half = joined(load_half(kept, index, base), load_half(arrived, index, base))
            if index in sends[which]:
                encode(which, message, sends[which].index(index), half)
            else:
                store_half(stay, keeps[which].index(index), half)


def next_kernel(sends, keeps, *refs):
    for which in range(2):
        kept, arrived = refs[2 * which : 2 * which + 2]
        message, stay = refs[4 + 2 * which : 6 + 2 * which]
        for index in range(kept.shape[0]):
            half = joined(load_half(kept, index), decoded(which, arrived, index))
            if index in sends[which]:
                encode(which, message, sends[which].index(index), half)
            if index in keeps[which]:
                store_half(stay, keeps[which].index(index), half)


def mm(x, y):
    return jnp.dot(x, y, preferred_element_type=f32)


def parts_of(x):
    high = x.astype(bf16)
    return high, (x - high.astype(f32)).astype(bf16)


def unpack_symmetric(which, blocks, diagonal, store):
    row, col = square_iotas()
    for (i, j, triangle), block in zip(HALVES[which], blocks):
        other = block.T
        if triangle:
            first = jnp.where(row < col, block, other)
            second = jnp.where(row > col, block, other)
            store(i, i, jnp.where(row == col, diagonal(i), first))
            store(j, j, jnp.where(row == col, diagonal(j), second))
        else:
            store(i, j, block)
            store(j, i, other)


def iterate_kernel(kept_a, arrived_a, kept_b, arrived_b, out_ref, gram_ref):
    row, col = square_iotas()

    def store(i, j, block):
        gram_ref[i * LANES : (i + 1) * LANES, j * LANES : (j + 1) * LANES] = block

    aux = None
    for which, kept, arrived in ((0, kept_a, arrived_a), (1, kept_b, arrived_b)):
        half = joined(load_half(kept, 0), decoded(which, arrived, 0))
        if aux is None:
            aux = half[0]
        unpack_symmetric(which, half[1:], lambda g: aux[g : g + 1], store)
    line = lax.broadcasted_iota(i32, (AUX, LANES), 0)
    squares = jnp.sum(jnp.where(line < 4, aux, 0.0), axis=0, keepdims=True)
    squares = jnp.sum(squares, axis=1, keepdims=True)
    inverse = 1.0 / (jnp.sqrt(squares) + 1e-07)
    gram = gram_ref[...] * inverse * inverse
    full_row = lax.broadcasted_iota(i32, (KV_RANK, KV_RANK), 0)
    full_col = lax.broadcasted_iota(i32, (KV_RANK, KV_RANK), 1)
    product = None
    for repeat in range(NS_ITERS):
        high, low = parts_of(gram)
        square = mm(high, high) + (mm(high, low) + mm(low, high))
        mixing = (coef_second * gram + coef_third * square).astype(bf16)
        if product is None:
            product = jnp.where(full_row == full_col, coef_first, 0.0) + mixing.astype(f32)
        else:
            product_high, product_low = parts_of(product)
            product = coef_first * product + (mm(product_high, mixing) + mm(product_low, mixing))
        if repeat < NS_ITERS - 1:
            half = coef_first * gram + (mm(high, mixing) + mm(low, mixing))
            half_high, half_low = parts_of(half)
            gram = coef_first * half + (mm(mixing, half_high) + mm(mixing, half_low))
    gram_ref[...] = product
    at = AUX_P
    for entries in HALVES:
        for i, j, triangle in entries:
            load = lambda i, j: gram_ref[i * LANES : (i + 1) * LANES, j * LANES : (j + 1) * LANES]
            if triangle:
                block = jnp.where(row <= col, load(i, i), load(j, j))
            else:
                block = 0.5 * (load(i, j) + load(j, i).T)
            out_ref[at : at + LANES, :] = block.astype(bf16)
            at += LANES

    def three(x):
        high = x.astype(bf16).astype(f32)
        middle = (x - high).astype(bf16).astype(f32)
        return high, middle, x - high - middle

    lines = [[], [], []]
    for i in range(BLOCKS):
        block = gram_ref[i * LANES : (i + 1) * LANES, i * LANES : (i + 1) * LANES]
        diagonal = jnp.sum(jnp.where(row == col, block, 0.0), axis=0, keepdims=True)
        for lines_of, part in zip(lines, three(diagonal)):
            lines_of.append(part)
    peaks = aux[4:5]
    tallies = aux[5:6]
    tally_high = tallies.astype(bf16).astype(f32)
    norm = three(jnp.broadcast_to(inverse, (1, LANES)))
    stacked = lines[0] + lines[1] + lines[2] + [peaks, tally_high, tallies - tally_high] + list(norm)
    place = lax.broadcasted_iota(i32, (AUX_P, LANES), 0)
    table = jnp.zeros((AUX_P, LANES), f32)
    for number, one in enumerate(stacked):
        table = jnp.where(place == number, one, table)
    out_ref[0:AUX_P, :] = table.astype(bf16)


def iterations(*args):
    return pl.pallas_call(
        iterate_kernel,
        in_specs=[pl.BlockSpec(memory_space=pltpu.VMEM)] * 4,
        out_specs=pl.BlockSpec(memory_space=pltpu.VMEM),
        out_shape=jax.ShapeDtypeStruct((ROWS_P, LANES), bf16),
        scratch_shapes=[pltpu.VMEM((KV_RANK, KV_RANK), f32)],
        compiler_params=params(),
        cost_estimate=pl.CostEstimate(
            flops=9 * NS_ITERS * 2 * KV_RANK**3, bytes_accessed=12 * HALF * LANES, transcendentals=0
        ),
        name="iterations",
    )(*args)


def apply_kernel(steps, spread, seats, me, counts, *refs):
    number = 1 + max(place for step in spread for place, _ in step)
    tables = refs[:number]
    nes_ref, weight_ref = refs[number : number + 2]
    update_ref, weight_out_ref, mat_ref, line_ref = refs[-4:]
    step_now = pl.program_id(0)

    def unpack(step):
        (place_a, start_a), (place_b, start_b) = spread[step]
        aux = tables[place_a][start_a : start_a + AUX_P, :].astype(f32)
        diagonal = [aux[i : i + 1] + aux[4 + i : 5 + i] + aux[8 + i : 9 + i] for i in range(BLOCKS)]
        inverse = [1.0 / line for line in diagonal]
        norm = aux[15:16] + aux[16:17] + aux[17:18]
        rms_scale = 0.2 * math.sqrt(max(KV_ROWS, KV_RANK))
        for i in range(BLOCKS):
            line_ref[0:1, i * LANES : (i + 1) * LANES] = diagonal[i] * (norm * rms_scale)
        peaks = aux[12:13]
        line_ref[1:2, 0:LANES] = jnp.sqrt(jnp.minimum(1.0, clip_limit / peaks))
        line_ref[2:3, 0:LANES] = aux[13:14] + aux[14:15]

        def store(i, j, block):
            mat_ref[i * LANES : (i + 1) * LANES, j * LANES : (j + 1) * LANES] = (block * inverse[j]).astype(bf16)

        for which, (place, start) in enumerate(((place_a, start_a + AUX_P), (place_b, start_b))):
            blocks = [
                tables[place][start + k * LANES : start + (k + 1) * LANES, :].astype(f32) for k in range(4)
            ]
            unpack_symmetric(which, blocks, lambda g: diagonal[g], store)

    for step in range(len(spread)):
        pl.when(step_now == step)(functools.partial(unpack, step))

    capacity = nes_ref.shape[1]
    count = counts[chosen_layer(steps, step_now, me)]
    groups, rows_block = seats
    dp, expert = me[2] // groups, me[2] % groups
    lane = lax.broadcasted_iota(i32, (1, LANES), 1)
    lowest = dp * groups
    earlier = jnp.where((lane >= lowest) & (lane < lowest + expert), line_ref[2:3, 0:LANES], 0.0)
    before = jnp.sum(earlier, axis=1, keepdims=True).astype(i32)
    base = before + dp * rows_block
    head_rows = NOPE + VDIM
    first_head = base // head_rows
    factor = line_ref[1:2, 0:LANES]
    slot = lax.broadcasted_iota(i32, (capacity, LANES), 0)
    row_index = base + slot
    head_of = row_index // head_rows
    scale = jnp.ones((capacity, LANES), f32)
    for k in range((capacity - 1) // head_rows + 2):
        one = jnp.sum(jnp.where(lane == first_head + k, factor, 0.0), axis=1, keepdims=True)
        scale = jnp.where(head_of == first_head + k, one, scale)
    scale = jnp.where(row_index % head_rows < NOPE, scale, 1.0)
    scale = jnp.where(slot < count, scale, 0.0)
    kept = scale * (1.0 - learn_rate * decay_rate)
    moved = scale * learn_rate
    rows = nes_ref[0]
    half = KV_RANK // 2
    for side in range(2):
        product = mm(rows, mat_ref[:, side * half : (side + 1) * half])
        for part in range(half // LANES):
            at = side * half + part * LANES
            update = product[:, part * LANES : (part + 1) * LANES] * line_ref[0:1, at : at + LANES]
            update_ref[0, :, at : at + LANES] = update.astype(bf16)
            weight = weight_ref[0, :, at : at + LANES].astype(f32)
            weight_out_ref[0, :, at : at + LANES] = (weight * kept - update * moved).astype(bf16)


def chosen_layer(steps, i, me):
    layer = layer_of(me, *steps[0])
    for number in range(1, len(steps)):
        layer = jnp.where(i == number, layer_of(me, *steps[number]), layer)
    return layer


def apply_rows(steps, spread, seats, me, counts, tables, nes, weight, update, weight_out):
    number = len(steps)
    layers, capacity, features = weight.shape
    picked = lambda i, me, counts: (chosen_layer(steps, i, me), 0, 0)
    in_specs = [whole(table.shape) for table in tables]
    in_specs += [pl.BlockSpec((1, capacity, features), picked)] * 2
    args = list(tables) + [nes, weight]
    aliases = {}
    if update is not None:
        in_specs += [pl.BlockSpec(memory_space=pl.ANY)] * 2
        aliases = {2 + len(args): 0, 3 + len(args): 1}
        args += [update, weight_out]
    shape = jax.ShapeDtypeStruct((layers, capacity, features), bf16)
    return pl.pallas_call(
        functools.partial(apply_kernel, steps, spread, seats),
        grid_spec=pltpu.PrefetchScalarGridSpec(
            num_scalar_prefetch=2,
            grid=(number,),
            in_specs=in_specs,
            out_specs=[pl.BlockSpec((1, capacity, features), picked)] * 2,
            scratch_shapes=[pltpu.VMEM((KV_RANK, KV_RANK), bf16), pltpu.VMEM((8, KV_RANK), f32)],
        ),
        out_shape=[shape, shape],
        input_output_aliases=aliases,
        compiler_params=params(),
        cost_estimate=pl.CostEstimate(
            flops=number * capacity * features * features * 2,
            bytes_accessed=number * capacity * features * 8,
            transcendentals=0,
        ),
        name="apply_rows",
    )(me, counts, *args)


def local(dp_size, expert_size, grad_rows, momentum_rows, weight_rows, row_counts, logit_peaks):
    layers = grad_rows.shape[1]
    expert_bits = expert_size.bit_length() - 1
    bits = expert_bits - 1
    assert layers == expert_size == 1 << expert_bits and bits >= 2
    assert dp_size == 4 and dp_size * expert_size <= LANES
    dp = lax.axis_index("dp")
    expert = lax.axis_index("expert")
    counts = row_counts.reshape(layers)
    owner = ((dp >> 1) << (bits - 1)) | ((expert >> 1) & ((1 << (bits - 1)) - 1))
    me = jnp.stack([owner, expert & 1, dp * expert_size + expert]).astype(i32)
    owner_axes = [("expert", 1 << (p + 1)) for p in range(bits - 1)] + [("dp", 2)]
    copy_axes = [("dp", 1), ("expert", 1 << (expert_bits - 1))]
    sizes = {"dp": dp_size, "expert": expert_size}

    def over(x, axis_bit):
        axis, bit = axis_bit
        return lax.ppermute(x, axis, [(i, i ^ bit) for i in range(sizes[axis])])

    core_axis = ("expert", 1)
    grad, mom, peaks = grad_rows[0], momentum_rows[0], logit_peaks[0, 0]
    nes, other = gram_parts(False, me, counts, grad, mom, peaks, None)
    arrived = over(other, core_axis)
    nes, own = gram_parts(True, me, counts, grad, mom, peaks, nes)

    codes = lambda n: jax.ShapeDtypeStruct((n, HALF_CODE, LANES), i16)
    plain = lambda n: jax.ShapeDtypeStruct((n, HALF, LANES), f32)
    orders = (list(range(bits - 1, -1, -1)), list(range(bits)))
    current = [list(range(1 << bits)) for _ in range(2)]
    state = None
    for step in range(bits + 2):
        if step < bits:
            axes = [owner_axes[orders[which][step]] for which in range(2)]
            sends = [[k for k, r in enumerate(current[w]) if r >> orders[w][step] & 1] for w in range(2)]
            keeps = [[k for k in range(len(current[w])) if k not in sends[w]] for w in range(2)]
            current = [[current[w][k] for k in keeps[w]] for w in range(2)]
        else:
            axes = [copy_axes[step - bits], copy_axes[1 - (step - bits)]]
            sends = keeps = [[0], [0]]
        shapes = [s for w in range(2) for s in (codes(len(sends[w])), plain(len(keeps[w])))]
        if state is None:
            kernel, state = first_kernel, (own, arrived)
        else:
            kernel = next_kernel
        out = local_call(functools.partial(kernel, sends, keeps), shapes, "sum" + str(step), *state)
        state = (out[1], over(out[0], axes[0]), out[3], over(out[2], axes[1]))
    table = iterations(*state)

    seats = (expert_size, KV_ROWS // dp_size)
    weight = weight_rows[0]
    full = lambda place: ((place, 0), (place, HEAD_P))
    apply = lambda steps, spread, tables, *outs: apply_rows(
        steps, spread, seats, me, counts, tables, nes, weight, *outs
    )
    tables = {0: table}
    for position in range(bits - 1, -1, -1) if bits > 2 else ():
        for known in list(tables):
            tables[known | 1 << position] = over(tables[known], owner_axes[position])
    if bits == 2:
        tables[2], tables[1] = over(table, owner_axes[1]), over(table, owner_axes[0])
    pair = [table, over(table, core_axis)]
    update, weight_out = apply(((0, True), (0, False)), (full(0), full(1)), pair, None, None)
    if bits == 2:
        tables[1], tables[2], update = lax.optimization_barrier((tables[1], tables[2], update))
        tail = [over(tables[1][:HEAD_P], owner_axes[1]), over(tables[2][HEAD_P:], owner_axes[0])]
        near = [tables[1], tables[2]]
        near += [over(x, core_axis) for x in near]
        update, weight_out = apply(
            ((1, True), (2, True), (1, False), (2, False)), tuple(full(k) for k in range(4)), near, update, weight_out
        )
        tail += [over(x, core_axis) for x in tail]
        spread = (((0, 0), (1, 0)), ((2, 0), (3, 0)))
        update, weight_out = apply(((3, True), (3, False)), spread, tail, update, weight_out)
    else:
        for relative in range(1, 1 << bits):
            pair = [tables[relative], over(tables[relative], core_axis)]
            update, weight_out = apply(
                ((relative, True), (relative, False)), (full(0), full(1)), pair, update, weight_out
            )
    return (update[None], weight_out[None])


def solution(mesh):
    return jax.shard_map(
        functools.partial(local, mesh.shape["dp"], mesh.shape["expert"]),
        mesh=mesh,
        in_specs=(
            P("dp", None, "expert", None),
            P("dp", None, "expert", None),
            P("dp", None, "expert", None),
            P("dp", None, "expert"),
            P("dp", "expert", None, None),
        ),
        out_specs=(P("dp", None, "expert", None), P("dp", None, "expert", None)),
        check_vma=False,
    )
```

time: 691 us -> 92 us (0.13)
  waiting for transfers between devices: 376 us -> 28.5 us
  blocking collectives: 168 us -> 0 us
  matrix products: 72.3 us -> 0 us
  Pallas kernels: 0 us -> 42.1 us
  other arithmetic: 29.4 us -> 0.65 us
  between operations: 14.6 us -> 0.78 us
  local copies, waits for them, and re-layouts: 13.1 us -> 1.64 us
    psum x5 -> x0, waiting for transfers between devices: 260 us -> none  [orthogonal(): gram_sum = lax.psum(local_gram, 'dp')]
    all_to_all x3 -> x0, waiting for transfers between devices: 116 us -> none  [the longest x1 116 us: local(): lax.all_to_all(nesterov, 'expert', split_axis=0, concat_axis=0, tiled=True)]
    all_gather x1 -> x0, blocking collectives: 92 us -> none  [carried_in(): gathered = lax.all_gather(part, axis)]
    dot_general x15 -> x0, matrix products: 72.3 us -> none  [the longest x5 33.4 us: orthogonal(): jnp.dot(iterate, mixing, preferred_element_type=jnp.float32)]
    pmax x1 -> x0, blocking collectives: 65.7 us -> none  [local(): peak_table = lax.pmax(logit_peaks[0, 0], ('dp', 'expert'))]
    pallas_call x0 -> x10, Pallas kernels: none -> 42.1 us  [the longest x3 14.9 us: apply_rows(): pl.pallas_call(functools.partial(apply_kernel, steps, spread, seats), gri...]
    ppermute x0 -> x18, waiting for transfers between devices: none -> 28.5 us  [over(): return lax.ppermute(x, axis, [(i, i ^ bit) for i in range(sizes[axis])])]
    ppermute x0 -> x18, starting transfers between devices: none -> 17.9 us  [over(): return lax.ppermute(x, axis, [(i, i ^ bit) for i in range(sizes[axis])])]
  transfers between devices with their start and end apart: 8 -> 18, of which waited for: 6 -> 11; matrix products, arithmetic and copies ran while one was open for 1% -> 0% of each run, Pallas kernels for 0% -> 19%
where the time goes in v2:
time: 92 us; the launch traced here: 91.6 us
  Pallas kernels  42.1 us (46%)
  waiting for transfers between devices  28.5 us (31%)
  starting transfers between devices  17.9 us (19%)
  local copies, waits for them, and re-layouts  1.64 us (2%)
    ppermute x18, waiting for transfers between devices, over(): return lax.ppermute(x, axis, [(i, i ^ bit) for i in range(sizes[axis])])  28.5 us
    ppermute x18, starting transfers between devices, over(): return lax.ppermute(x, axis, [(i, i ^ bit) for i in range(sizes[axis])])  17.9 us
    pallas_call x3, Pallas kernels, apply_rows(): pl.pallas_call(functools.partial(apply_kernel, steps, spread, seats), gri...  14.9 us
    pallas_call x2, Pallas kernels, gram_parts(): pl.pallas_call(functools.partial(gram_kernel, own_core), grid_spec=pltpu....  13.2 us
    pallas_call x1, Pallas kernels, iterations(): pl.pallas_call(iterate_kernel, in_specs=[pl.BlockSpec(memory_space=pltpu....  12.3 us
  transfers between devices with their start and end apart: 18, of which 11 were waited for; matrix products, arithmetic and copies ran while one was open for 0% of the time, Pallas kernels for 19%

profile of v2, /device:TPU:0, one launch (start us, length us, event | category | flops | bytes accessed | tf_op | source)
XLA Modules:
  0.0 91.6 jit_solution(15035561642909450347)
XLA Ops:
  1.3 6.6 %gram_parts.2 = (bf16[8,640,512]{2,1,0:T(8,128)(2,1)}, f32[4,1040,128]{2,1,0:T(8,128)}) custom-call(s32[3]{0:T(128)} %pad_add_fusion.me, s32[8]{0:T(128)} %bitcast.17, bf16[8,640,512]{2,1,0:T(8,128)(2,1)} %bitcast.22, bf16[8,640,512]{2,1,0:T(8,128)(2,1)} %bitcast.24, bf16[8,64]{1,0:T(8,128)(2,1)} %bitcast.28), custom_call_target="tpu_custom_call" | custom-call | flops 1342177280 | bytes 9994240 | tf_op jit(solution)/shard_map/gram_parts/pallas_call | solution.py:121
  8.4 6.6 %gram_parts.3 = (bf16[8,640,512]{2,1,0:T(8,128)(2,1)}, f32[4,1040,128]{2,1,0:T(8,128)}) custom-call(s32[3]{0:T(128)} %pad_add_fusion.me, s32[8]{0:T(128)} %bitcast.18, bf16[8,640,512]{2,1,0:T(8,128)(2,1)} %bitcast.23, bf16[8,640,512]{2,1,0:T(8,128)(2,1)} %bitcast.25, bf16[8,64]{1,0:T(8,128)(2,1)} %bitcast.29, ...), custom_call_target="tpu_custom_call", output_to_operand_aliasing={{0}: (5, {})} | custom-call | flops 1342177280 | bytes 9994240 | tf_op jit(solution)/shard_map/gram_parts/pallas_call | solution.py:121
  15.0 1.6 %copy-done = f32[4,1040,128]{2,1,0:T(8,128)S(1)} copy-done((f32[4,1040,128]{2,1,0:T(8,128)S(1)}, f32[4,1040,128]{2,1,0:T(8,128)}, u32[]{:S(2)}) %copy-start) | copy-done | bytes 2129944
  17.1 2.6 %collective-permute-start.1 = (s16[2,528,128]{2,1,0:T(8,128)(2,1)S(1)}, s16[2,528,128]{2,1,0:T(8,128)(2,1)S(1)}, u32[]{:S(2)}, u32[]{:S(2)}) collective-permute-start(s16[2,528,128]{2,1,0:T(8,128)(2,1)S(1)} %get-tuple-element.35), channel_id=1, source_target_pairs={{0,16},{8,24},{16,0},{24,8},{1,17},{9,25},{17,1},{25,9},{2,18},{10... | collective-permute-start | bytes 811016 | tf_op jit(solution)/shard_map/ppermute | solution.py:479
  19.7 1.6 %collective-permute-start.2 = (s16[2,528,128]{2,1,0:T(8,128)(2,1)S(1)}, s16[2,528,128]{2,1,0:T(8,128)(2,1)S(1)}, u32[]{:S(2)}, u32[]{:S(2)}) collective-permute-start(s16[2,528,128]{2,1,0:T(8,128)(2,1)S(1)} %get-tuple-element.37), channel_id=1, source_target_pairs={{0,2},{1,3},{2,0},{3,1},{4,6},{5,7},{6,4},{7,5},{8,10},{9,11},{10,... | collective-permute-start | bytes 811016 | tf_op jit(solution)/shard_map/ppermute | solution.py:479
  21.3 5.6 %collective-permute-done.1.refs_1_ = s16[2,528,128]{2,1,0:T(8,128)(2,1)S(1)} collective-permute-done((s16[2,528,128]{2,1,0:T(8,128)(2,1)S(1)}, s16[2,528,128]{2,1,0:T(8,128)(2,1)S(1)}, u32[]{:S(2)}, u32[]{:S(2)}) %collective-permute-start.1) | collective-permute-done | bytes 270368 | tf_op jit(solution)/shard_map/ppermute | solution.py:479
  26.8 1.5 %collective-permute-done.2.refs_3_ = s16[2,528,128]{2,1,0:T(8,128)(2,1)S(1)} collective-permute-done((s16[2,528,128]{2,1,0:T(8,128)(2,1)S(1)}, s16[2,528,128]{2,1,0:T(8,128)(2,1)S(1)}, u32[]{:S(2)}, u32[]{:S(2)}) %collective-permute-start.2) | collective-permute-done | bytes 270368 | tf_op jit(solution)/shard_map/ppermute | solution.py:479
  28.8 1.6 %collective-permute-start.3 = (s16[1,528,128]{2,1,0:T(8,128)(2,1)S(1)}, s16[1,528,128]{2,1,0:T(8,128)(2,1)S(1)}, u32[]{:S(2)}, u32[]{:S(2)}) collective-permute-start(s16[1,528,128]{2,1,0:T(8,128)(2,1)S(1)} %get-tuple-element.39), channel_id=1, source_target_pairs={{0,2},{1,3},{2,0},{3,1},{4,6},{5,7},{6,4},{7,5},{8,10},{9,11},{10,... | collective-permute-start | bytes 405512 | tf_op jit(solution)/shard_map/ppermute | solution.py:479
  30.9 2.9 %collective-permute-done.3.refs_1_ = s16[1,528,128]{2,1,0:T(8,128)(2,1)S(1)} collective-permute-done((s16[1,528,128]{2,1,0:T(8,128)(2,1)S(1)}, s16[1,528,128]{2,1,0:T(8,128)(2,1)S(1)}, u32[]{:S(2)}, u32[]{:S(2)}) %collective-permute-start.3) | collective-permute-done | bytes 135200 | tf_op jit(solution)/shard_map/ppermute | solution.py:479
  33.9 1.6 %collective-permute-done.4.refs_3_ = s16[1,528,128]{2,1,0:T(8,128)(2,1)S(1)} collective-permute-done((s16[1,528,128]{2,1,0:T(8,128)(2,1)S(1)}, s16[1,528,128]{2,1,0:T(8,128)(2,1)S(1)}, u32[]{:S(2)}, u32[]{:S(2)}) %collective-permute-start.4) | collective-permute-done | bytes 135200 | tf_op jit(solution)/shard_map/ppermute | solution.py:479
  35.8 1.6 %collective-permute-start.5 = (s16[1,528,128]{2,1,0:T(8,128)(2,1)S(1)}, s16[1,528,128]{2,1,0:T(8,128)(2,1)S(1)}, u32[]{:S(2)}, u32[]{:S(2)}) collective-permute-start(s16[1,528,128]{2,1,0:T(8,128)(2,1)S(1)} %get-tuple-element.43), channel_id=1, source_target_pairs={{0,8},{8,0},{16,24},{24,16},{1,9},{9,1},{17,25},{25,17},{2,10},{10... | collective-permute-start | bytes 405512 | tf_op jit(solution)/shard_map/ppermute | solution.py:479
  37.4 2.6 %collective-permute-start.6 = (s16[1,528,128]{2,1,0:T(8,128)(2,1)S(1)}, s16[1,528,128]{2,1,0:T(8,128)(2,1)S(1)}, u32[]{:S(2)}, u32[]{:S(2)}) collective-permute-start(s16[1,528,128]{2,1,0:T(8,128)(2,1)S(1)} %get-tuple-element.45), channel_id=1, source_target_pairs={{0,4},{1,5},{2,6},{3,7},{4,0},{5,1},{6,2},{7,3},{8,12},{9,13},{10,... | collective-permute-start | bytes 405512 | tf_op jit(solution)/shard_map/ppermute | solution.py:479
  40.9 3.7 %collective-permute-done.6.refs_3_ = s16[1,528,128]{2,1,0:T(8,128)(2,1)S(1)} collective-permute-done((s16[1,528,128]{2,1,0:T(8,128)(2,1)S(1)}, s16[1,528,128]{2,1,0:T(8,128)(2,1)S(1)}, u32[]{:S(2)}, u32[]{:S(2)}) %collective-permute-start.6) | collective-permute-done | bytes 135200 | tf_op jit(solution)/shard_map/ppermute | solution.py:479
  45.0 1.4 %collective-permute-start.7 = (s16[1,528,128]{2,1,0:T(8,128)(2,1)S(1)}, s16[1,528,128]{2,1,0:T(8,128)(2,1)S(1)}, u32[]{:S(2)}, u32[]{:S(2)}) collective-permute-start(s16[1,528,128]{2,1,0:T(8,128)(2,1)S(1)} %get-tuple-element.47), channel_id=1, source_target_pairs={{0,4},{1,5},{2,6},{3,7},{4,0},{5,1},{6,2},{7,3},{8,12},{9,13},{10,... | collective-permute-start | bytes 405512 | tf_op jit(solution)/shard_map/ppermute | solution.py:479
  46.9 5.1 %collective-permute-done.7.arrived_a = s16[1,528,128]{2,1,0:T(8,128)(2,1)S(1)} collective-permute-done((s16[1,528,128]{2,1,0:T(8,128)(2,1)S(1)}, s16[1,528,128]{2,1,0:T(8,128)(2,1)S(1)}, u32[]{:S(2)}, u32[]{:S(2)}) %collective-permute-start.7) | collective-permute-done | bytes 135200 | tf_op jit(solution)/shard_map/ppermute | solution.py:479
  52.1 12.3 %iterations.1.refs_0_ = bf16[1056,128]{1,0:T(8,128)(2,1)S(1)} custom-call(f32[1,520,128]{2,1,0:T(8,128)S(1)} %get-tuple-element.46.kept_a, s16[1,528,128]{2,1,0:T(8,128)(2,1)S(1)} %collective-permute-done.7.arrived_a, f32[1,520,128]{2,1,0:T(8,128)S(1)} %get-tuple-element.48.kept_b, s16[1,528,128]{2,1,0:T(8,128)(2,1)S(1)} %collective-permute-done.8.arrived_b), custom_call_target="tpu_custom_call" | custom-call | flops 12079595520 | bytes 798720 | tf_op jit(solution)/shard_map/iterations/pallas_call | solution.py:340
  66.2 4.2 %apply_rows.3 = (bf16[8,640,512]{2,1,0:T(8,128)(2,1)}, bf16[8,640,512]{2,1,0:T(8,128)(2,1)}) custom-call(s32[3]{0:T(128)S(1)} %copy-done.1, s32[8]{0:T(128)S(1)} %bitcast.19, bf16[1056,128]{1,0:T(8,128)(2,1)S(1)} %iterations.1.refs_0_, bf16[1056,128]{1,0:T(8,128)(2,1)S(1)} %collective-permute-done.11.refs_1_, bf16[8,640,512]{2,1,0:T(8,128)(2,1)S(1)} %bitcast.11, ...), custom_call_target="tpu_custom_call" | custom-call | flops 671088640 | bytes 5242880 | tf_op jit(solution)/shard_map/apply_rows/pallas_call | solution.py:441
  70.5 2.9 %collective-permute-done.10.refs_1_ = bf16[1056,128]{1,0:T(8,128)(2,1)S(1)} collective-permute-done((bf16[1056,128]{1,0:T(8,128)(2,1)S(1)}, bf16[1056,128]{1,0:T(8,128)(2,1)S(1)}, u32[]{:S(2)}, u32[]{:S(2)}) %collective-permute-start.10) | collective-permute-done | bytes 270368 | tf_op jit(solution)/shard_map/ppermute | solution.py:479
  74.1 1.6 %collective-permute-start.12 = (bf16[544,128]{1,0:T(8,128)(2,1)S(1)}, bf16[544,128]{1,0:T(8,128)(2,1)S(1)}, u32[]{:S(2)}, u32[]{:S(2)}) collective-permute-start(bf16[544,128]{1,0:T(8,128)(2,1)S(1)} %slice.6), channel_id=1, source_target_pairs={{0,16},{8,24},{16,0},{24,8},{1,17},{9,25},{17,1},{25,9},{2,18},{10... | collective-permute-start | bytes 417800 | tf_op jit(solution)/shard_map/ppermute | solution.py:479
  75.7 1.2 %collective-permute-start.13 = (bf16[512,128]{1,0:T(8,128)(2,1)S(1)}, bf16[512,128]{1,0:T(8,128)(2,1)S(1)}, u32[]{:S(2)}, u32[]{:S(2)}) collective-permute-start(bf16[512,128]{1,0:T(8,128)(2,1)S(1)} %slice.7), channel_id=1, source_target_pairs={{0,2},{1,3},{2,0},{3,1},{4,6},{5,7},{6,4},{7,5},{8,10},{9,11},{10,... | collective-permute-start | bytes 393224 | tf_op jit(solution)/shard_map/ppermute | solution.py:479
  76.9 2.9 %collective-permute-done.12.refs_0_ = bf16[544,128]{1,0:T(8,128)(2,1)S(1)} collective-permute-done((bf16[544,128]{1,0:T(8,128)(2,1)S(1)}, bf16[544,128]{1,0:T(8,128)(2,1)S(1)}, u32[]{:S(2)}, u32[]{:S(2)}) %collective-permute-start.12) | collective-permute-done | bytes 139296 | tf_op jit(solution)/shard_map/ppermute | solution.py:479
  79.8 1.1 %collective-permute-done.13.refs_1_ = bf16[512,128]{1,0:T(8,128)(2,1)S(1)} collective-permute-done((bf16[512,128]{1,0:T(8,128)(2,1)S(1)}, bf16[512,128]{1,0:T(8,128)(2,1)S(1)}, u32[]{:S(2)}, u32[]{:S(2)}) %collective-permute-start.13) | collective-permute-done | bytes 131104 | tf_op jit(solution)/shard_map/ppermute | solution.py:479
  80.9 6.6 %apply_rows.4 = (bf16[8,640,512]{2,1,0:T(8,128)(2,1)}, bf16[8,640,512]{2,1,0:T(8,128)(2,1)}) custom-call(s32[3]{0:T(128)S(1)} %copy-done.1, s32[8]{0:T(128)S(1)} %bitcast.20, bf16[1056,128]{1,0:T(8,128)(2,1)S(1)} %collective-permute-done.9.refs_0_, ...), custom_call_target="tpu_custom_call", output_to_operand_aliasing={{0}: (8, {}), {1}: (9, {})} | custom-call | flops 1342177280 | bytes 10485760 | tf_op jit(solution)/shard_map/apply_rows/pallas_call | solution.py:441
  87.5 4.1 %apply_rows.5 = (bf16[8,640,512]{2,1,0:T(8,128)(2,1)}, bf16[8,640,512]{2,1,0:T(8,128)(2,1)}) custom-call(s32[3]{0:T(128)S(1)} %copy-done.1, s32[8]{0:T(128)S(1)} %bitcast.21, bf16[544,128]{1,0:T(8,128)(2,1)S(1)} %collective-permute-done.12.refs_0_, ...), custom_call_target="tpu_custom_call", output_to_operand_aliasing={{0}: (8, {}), {1}: (9, {})} | custom-call | flops 671088640 | bytes 5242880 | tf_op jit(solution)/shard_map/apply_rows/pallas_call | solution.py:441
  (41 shorter events, 7.4 us)
Async XLA Ops:
  7.9 7.1 %collective-permute-start = (f32[4,1040,128]{2,1,0:T(8,128)}, f32[4,1040,128]{2,1,0:T(8,128)S(1)}, u32[]{:S(2)}, u32[]{:S(2)}) collective-permute-start(f32[4,1040,128]{2,1,0:T(8,128)} %get-tuple-element.33), channel_id=1, source_target_pairs={{0,1},{1,0},{2,3},{3,2},{4,5},{5,4},{6,7},{7,6},{8,9},{9,8},{10,11... | collective-permute-start | bytes 6389768 | tf_op jit(solution)/shard_map/ppermute | solution.py:479
  17.1 9.7 %collective-permute-start.1 = (s16[2,528,128]{2,1,0:T(8,128)(2,1)S(1)}, s16[2,528,128]{2,1,0:T(8,128)(2,1)S(1)}, u32[]{:S(2)}, u32[]{:S(2)}) collective-permute-start(s16[2,528,128]{2,1,0:T(8,128)(2,1)S(1)} %get-tuple-element.35), channel_id=1, source_target_pairs={{0,16},{8,24},{16,0},{24,8},{1,17},{9,25},{17,1},{25,9},{2,18},{10... | collective-permute-start | bytes 811016 | tf_op jit(solution)/shard_map/ppermute | solution.py:479
  19.7 8.6 %collective-permute-start.2 = (s16[2,528,128]{2,1,0:T(8,128)(2,1)S(1)}, s16[2,528,128]{2,1,0:T(8,128)(2,1)S(1)}, u32[]{:S(2)}, u32[]{:S(2)}) collective-permute-start(s16[2,528,128]{2,1,0:T(8,128)(2,1)S(1)} %get-tuple-element.37), channel_id=1, source_target_pairs={{0,2},{1,3},{2,0},{3,1},{4,6},{5,7},{6,4},{7,5},{8,10},{9,11},{10,... | collective-permute-start | bytes 811016 | tf_op jit(solution)/shard_map/ppermute | solution.py:479
  28.8 5.1 %collective-permute-start.3 = (s16[1,528,128]{2,1,0:T(8,128)(2,1)S(1)}, s16[1,528,128]{2,1,0:T(8,128)(2,1)S(1)}, u32[]{:S(2)}, u32[]{:S(2)}) collective-permute-start(s16[1,528,128]{2,1,0:T(8,128)(2,1)S(1)} %get-tuple-element.39), channel_id=1, source_target_pairs={{0,2},{1,3},{2,0},{3,1},{4,6},{5,7},{6,4},{7,5},{8,10},{9,11},{10,... | collective-permute-start | bytes 405512 | tf_op jit(solution)/shard_map/ppermute | solution.py:479
  30.4 5.0 %collective-permute-start.4 = (s16[1,528,128]{2,1,0:T(8,128)(2,1)S(1)}, s16[1,528,128]{2,1,0:T(8,128)(2,1)S(1)}, u32[]{:S(2)}, u32[]{:S(2)}) collective-permute-start(s16[1,528,128]{2,1,0:T(8,128)(2,1)S(1)} %get-tuple-element.41), channel_id=1, source_target_pairs={{0,16},{8,24},{16,0},{24,8},{1,17},{9,25},{17,1},{25,9},{2,18},{10... | collective-permute-start | bytes 405512 | tf_op jit(solution)/shard_map/ppermute | solution.py:479
  35.8 5.1 %collective-permute-start.5 = (s16[1,528,128]{2,1,0:T(8,128)(2,1)S(1)}, s16[1,528,128]{2,1,0:T(8,128)(2,1)S(1)}, u32[]{:S(2)}, u32[]{:S(2)}) collective-permute-start(s16[1,528,128]{2,1,0:T(8,128)(2,1)S(1)} %get-tuple-element.43), channel_id=1, source_target_pairs={{0,8},{8,0},{16,24},{24,16},{1,9},{9,1},{17,25},{25,17},{2,10},{10... | collective-permute-start | bytes 405512 | tf_op jit(solution)/shard_map/ppermute | solution.py:479
  37.4 7.2 %collective-permute-start.6 = (s16[1,528,128]{2,1,0:T(8,128)(2,1)S(1)}, s16[1,528,128]{2,1,0:T(8,128)(2,1)S(1)}, u32[]{:S(2)}, u32[]{:S(2)}) collective-permute-start(s16[1,528,128]{2,1,0:T(8,128)(2,1)S(1)} %get-tuple-element.45), channel_id=1, source_target_pairs={{0,4},{1,5},{2,6},{3,7},{4,0},{5,1},{6,2},{7,3},{8,12},{9,13},{10,... | collective-permute-start | bytes 405512 | tf_op jit(solution)/shard_map/ppermute | solution.py:479
  44.6 21.6 %slice-start = ((s8[5242880]{0:T(1024)(128)(4,1)}), s8[4194304]{0:T(1024)(128)(4,1)S(1)}, s32[]{:S(2)}) async-start(s8[5242880]{0:T(1024)(128)(4,1)} %bitcast.10), calls=%async_computation | async-start | bytes 8388608
  44.6 21.6 %slice-start.2 = ((s8[5242880]{0:T(1024)(128)(4,1)}), s8[4194304]{0:T(1024)(128)(4,1)S(1)}, s32[]{:S(2)}) async-start(s8[5242880]{0:T(1024)(128)(4,1)} %bitcast.12), calls=%async_computation.2 | async-start | bytes 8388608
  45.0 7.1 %collective-permute-start.7 = (s16[1,528,128]{2,1,0:T(8,128)(2,1)S(1)}, s16[1,528,128]{2,1,0:T(8,128)(2,1)S(1)}, u32[]{:S(2)}, u32[]{:S(2)}) collective-permute-start(s16[1,528,128]{2,1,0:T(8,128)(2,1)S(1)} %get-tuple-element.47), channel_id=1, source_target_pairs={{0,4},{1,5},{2,6},{3,7},{4,0},{5,1},{6,2},{7,3},{8,12},{9,13},{10,... | collective-permute-start | bytes 405512 | tf_op jit(solution)/shard_map/ppermute | solution.py:479
  46.4 5.7 %collective-permute-start.8 = (s16[1,528,128]{2,1,0:T(8,128)(2,1)S(1)}, s16[1,528,128]{2,1,0:T(8,128)(2,1)S(1)}, u32[]{:S(2)}, u32[]{:S(2)}) collective-permute-start(s16[1,528,128]{2,1,0:T(8,128)(2,1)S(1)} %get-tuple-element.49), channel_id=1, source_target_pairs={{0,8},{8,0},{16,24},{24,16},{1,9},{9,1},{17,25},{25,17},{2,10},{10... | collective-permute-start | bytes 405512 | tf_op jit(solution)/shard_map/ppermute | solution.py:479
  52.1 14.1 %slice-start.1 = ((s8[5242880]{0:T(1024)(128)(4,1)}), s8[1048576]{0:T(1024)(128)(4,1)S(1)}, s32[]{:S(2)}) async-start(s8[5242880]{0:T(1024)(128)(4,1)} %bitcast.10), calls=%async_computation.1 | async-start | bytes 2097152
  52.1 14.1 %slice-start.3 = ((s8[5242880]{0:T(1024)(128)(4,1)}), s8[1048576]{0:T(1024)(128)(4,1)S(1)}, s32[]{:S(2)}) async-start(s8[5242880]{0:T(1024)(128)(4,1)} %bitcast.12), calls=%async_computation.3 | async-start | bytes 2097152
  52.1 14.1 %copy-start.1 = (s32[3]{0:T(128)S(1)}, s32[3]{0:T(128)}, u32[]{:S(2)}) copy-start(s32[3]{0:T(128)} %pad_add_fusion.me) | copy-start | bytes 40
  52.1 14.1 %copy-start.2 = (s32[1,8,1]{1,2,0:T(1,128)S(1)}, s32[1,8,1]{1,2,0:T(1,128)}, u32[]{:S(2)}) copy-start(s32[1,8,1]{1,2,0:T(1,128)} %param.8) | copy-start | bytes 100
  64.4 1.8 %collective-permute-start.11 = (bf16[1056,128]{1,0:T(8,128)(2,1)S(1)}, bf16[1056,128]{1,0:T(8,128)(2,1)S(1)}, u32[]{:S(2)}, u32[]{:S(2)}) collective-permute-start(bf16[1056,128]{1,0:T(8,128)(2,1)S(1)} %iterations.1.refs_0_), channel_id=1, source_target_pairs={{0,1},{1,0},{2,3},{3,2},{4,5},{5,4},{6,7},{7,6},{8,9},{9,8},{10,11... | collective-permute-start | bytes 811016 | tf_op jit(solution)/shard_map/ppermute | solution.py:479
  64.5 8.9 %collective-permute-start.10 = (bf16[1056,128]{1,0:T(8,128)(2,1)S(1)}, bf16[1056,128]{1,0:T(8,128)(2,1)S(1)}, u32[]{:S(2)}, u32[]{:S(2)}) collective-permute-start(bf16[1056,128]{1,0:T(8,128)(2,1)S(1)} %iterations.1.refs_0_), channel_id=1, source_target_pairs={{0,16},{8,24},{16,0},{24,8},{1,17},{9,25},{17,1},{25,9},{2,18},{10... | collective-permute-start | bytes 811016 | tf_op jit(solution)/shard_map/ppermute | solution.py:479
  65.0 8.6 %collective-permute-start.9 = (bf16[1056,128]{1,0:T(8,128)(2,1)S(1)}, bf16[1056,128]{1,0:T(8,128)(2,1)S(1)}, u32[]{:S(2)}, u32[]{:S(2)}) collective-permute-start(bf16[1056,128]{1,0:T(8,128)(2,1)S(1)} %iterations.1.refs_0_), channel_id=1, source_target_pairs={{0,2},{1,3},{2,0},{3,1},{4,6},{5,7},{6,4},{7,5},{8,10},{9,11},{10,... | collective-permute-start | bytes 811016 | tf_op jit(solution)/shard_map/ppermute | solution.py:479
  73.6 7.3 %collective-permute-start.16 = (bf16[1056,128]{1,0:T(8,128)(2,1)S(1)}, bf16[1056,128]{1,0:T(8,128)(2,1)S(1)}, u32[]{:S(2)}, u32[]{:S(2)}) collective-permute-start(bf16[1056,128]{1,0:T(8,128)(2,1)S(1)} %collective-permute-done.9.refs_0_), channel_id=1, source_target_pairs={{0,1},{1,0},{2,3},{3,2},{4,5},{5,4},{6,7},{7,6},{8,9},{9,8},{10,11... | collective-permute-start | bytes 811016 | tf_op jit(solution)/shard_map/ppermute | solution.py:479
  73.6 7.3 %collective-permute-start.17 = (bf16[1056,128]{1,0:T(8,128)(2,1)S(1)}, bf16[1056,128]{1,0:T(8,128)(2,1)S(1)}, u32[]{:S(2)}, u32[]{:S(2)}) collective-permute-start(bf16[1056,128]{1,0:T(8,128)(2,1)S(1)} %collective-permute-done.10.refs_1_), channel_id=1, source_target_pairs={{0,1},{1,0},{2,3},{3,2},{4,5},{5,4},{6,7},{7,6},{8,9},{9,8},{10,11... | collective-permute-start | bytes 811016 | tf_op jit(solution)/shard_map/ppermute | solution.py:479
  74.1 5.6 %collective-permute-start.12 = (bf16[544,128]{1,0:T(8,128)(2,1)S(1)}, bf16[544,128]{1,0:T(8,128)(2,1)S(1)}, u32[]{:S(2)}, u32[]{:S(2)}) collective-permute-start(bf16[544,128]{1,0:T(8,128)(2,1)S(1)} %slice.6), channel_id=1, source_target_pairs={{0,16},{8,24},{16,0},{24,8},{1,17},{9,25},{17,1},{25,9},{2,18},{10... | collective-permute-start | bytes 417800 | tf_op jit(solution)/shard_map/ppermute | solution.py:479
  75.7 5.2 %collective-permute-start.13 = (bf16[512,128]{1,0:T(8,128)(2,1)S(1)}, bf16[512,128]{1,0:T(8,128)(2,1)S(1)}, u32[]{:S(2)}, u32[]{:S(2)}) collective-permute-start(bf16[512,128]{1,0:T(8,128)(2,1)S(1)} %slice.7), channel_id=1, source_target_pairs={{0,2},{1,3},{2,0},{3,1},{4,6},{5,7},{6,4},{7,5},{8,10},{9,11},{10,... | collective-permute-start | bytes 393224 | tf_op jit(solution)/shard_map/ppermute | solution.py:479
  79.8 7.7 %collective-permute-start.14 = (bf16[544,128]{1,0:T(8,128)(2,1)S(1)}, bf16[544,128]{1,0:T(8,128)(2,1)S(1)}, u32[]{:S(2)}, u32[]{:S(2)}) collective-permute-start(bf16[544,128]{1,0:T(8,128)(2,1)S(1)} %collective-permute-done.12.refs_0_), channel_id=1, source_target_pairs={{0,1},{1,0},{2,3},{3,2},{4,5},{5,4},{6,7},{7,6},{8,9},{9,8},{10,11... | collective-permute-start | bytes 417800 | tf_op jit(solution)/shard_map/ppermute | solution.py:479
  80.9 6.6 %collective-permute-start.15 = (bf16[512,128]{1,0:T(8,128)(2,1)S(1)}, bf16[512,128]{1,0:T(8,128)(2,1)S(1)}, u32[]{:S(2)}, u32[]{:S(2)}) collective-permute-start(bf16[512,128]{1,0:T(8,128)(2,1)S(1)} %collective-permute-done.13.refs_1_), channel_id=1, source_target_pairs={{0,1},{1,0},{2,3},{3,2},{4,5},{5,4},{6,7},{7,6},{8,9},{9,8},{10,11... | collective-permute-start | bytes 393224 | tf_op jit(solution)/shard_map/ppermute | solution.py:479
  (1 other events, 1.6 us)

commit v3 on v2

v3 whole, which is shorter than its diff:
```python
import functools
import math

import jax
import jax.numpy as jnp
from jax import lax
from jax.experimental import pallas as pl
from jax.experimental.pallas import tpu as pltpu
from jax.sharding import PartitionSpec as P

KV_RANK = 512
NOPE = 128
VDIM = 128
NS_ITERS = 5
KV_ROWS = 16384

momentum_coef = 0.95
learn_rate = 0.02
decay_rate = 0.1
clip_limit = 100.0
coef_first = 3.4445
coef_second = -4.775
coef_third = 2.0315

f32 = jnp.float32
bf16 = jnp.bfloat16
i16 = jnp.int16
i32 = jnp.int32

LANES = 128
BLOCKS = KV_RANK // LANES
HALVES = (
    ((0, 1, True), (0, 1, False), (0, 2, False), (1, 2, False)),
    ((2, 3, True), (0, 3, False), (1, 3, False), (2, 3, False)),
)
AUX = 8
HALF = AUX + 4 * LANES
AUX_CODE = 16
HALF_CODE = AUX_CODE + 4 * LANES
AUX_P = 32
HEAD_P = AUX_P + 4 * LANES
ROWS_P = AUX_P + 8 * LANES
UNIT = 32000.0
CHUNKS = 2


def params(mebibytes=40):
    return pltpu.CompilerParams(vmem_limit_bytes=mebibytes * 1024 * 1024)


def pinned(x):
    return pltpu.with_memory_space_constraint(x, pltpu.HBM)


def square_iotas():
    row = lax.broadcasted_iota(i32, (LANES, LANES), 0)
    col = lax.broadcasted_iota(i32, (LANES, LANES), 1)
    return row, col


def layer_of(me, relative, own_core):
    core = me[1] if own_core else 1 - me[1]
    return 2 * (me[0] ^ relative) + core


def gram_kernel(picks, me, counts_ref, grad_ref, mom_ref, peaks_ref, nes_ref, *refs):
    number = len(picks)
    outs = refs[:-7]
    counts, counts_arrival, peaks_buf, peaks_arrival, grad_buf, mom_buf, arrivals = refs[-7:]
    layers = [layer_of(me, *pick) for pick in picks]
    copies = []
    for k, layer in enumerate(layers):
        copies.append(pltpu.make_async_copy(grad_ref.at[layer], grad_buf.at[k], arrivals.at[0, k]))
        copies.append(pltpu.make_async_copy(mom_ref.at[layer], mom_buf.at[k], arrivals.at[1, k]))
    small = [
        pltpu.make_async_copy(counts_ref, counts, counts_arrival),
        pltpu.make_async_copy(peaks_ref, peaks_buf, peaks_arrival),
    ]
    for copy in copies[:2] + small + copies[2:]:
        copy.start()
    for copy in small:
        copy.wait()
    row, col = square_iotas()
    line = lax.broadcasted_iota(i32, (AUX, LANES), 0)
    lane = lax.broadcasted_iota(i32, (AUX, LANES), 1)
    every_peak = peaks_buf[...].astype(f32)
    every_peak = jnp.concatenate(
        [every_peak, jnp.zeros((every_peak.shape[0], LANES - every_peak.shape[1]), f32)], axis=1
    )
    pick_row = lax.broadcasted_iota(i32, every_peak.shape, 0)
    width = KV_RANK // 2
    dims = (((0,), (0,)), ((), ()))
    slot = lax.broadcasted_iota(i32, (grad_buf.shape[1], LANES), 0)

    def form_rows(k):
        copies[2 * k].wait()
        copies[2 * k + 1].wait()
        live = slot < counts[layers[k]]
        for i in range(BLOCKS):
            span = slice(i * LANES, (i + 1) * LANES)
            gradient = grad_buf[k, :, span].astype(f32)
            velocity = momentum_coef * mom_buf[k, :, span].astype(f32) + gradient
            nesterov = gradient + momentum_coef * velocity
            nes_ref[k, :, span] = jnp.where(live, nesterov, 0.0).astype(bf16)

    form_rows(0)
    for k, layer in enumerate(layers):
        if k + 1 < number:
            form_rows(k + 1)
        rows = nes_ref[k]
        upper = lax.dot_general(rows[:, :width], rows, dims, preferred_element_type=f32)
        lower = lax.dot_general(rows[:, width:], rows[:, width:], dims, preferred_element_type=f32)

        def block(i, j):
            if i < 2:
                return upper[i * LANES : (i + 1) * LANES, j * LANES : (j + 1) * LANES]
            return lower[(i - 2) * LANES : (i - 1) * LANES, (j - 2) * LANES : (j - 1) * LANES]

        aux = jnp.where((line == 5) & (lane == me[2]), counts[layer].astype(f32), 0.0)
        peaks = jnp.sum(jnp.where(pick_row == layer, every_peak, 0.0), axis=0, keepdims=True)
        aux = jnp.where(line == 4, peaks, aux)
        for i in range(BLOCKS):
            diagonal = jnp.sum(jnp.where(row == col, block(i, i), 0.0), axis=0, keepdims=True)
            aux = jnp.where(line == i, diagonal, aux)
        for which, entries in enumerate(HALVES):
            half = [aux]
            for i, j, triangle in entries:
                half.append(jnp.where(row <= col, block(i, i), block(j, j)) if triangle else block(i, j))
            if len(outs) > 1:
                store_half(outs[2 * k + which], 0, half)
            else:
                store_half(outs[0], k, half, which * HALF)


def gram_parts(picks, out_shapes, me, counts, grad, mom, peaks):
    capacity, features = grad.shape[1:]
    number = len(picks)
    smem = pl.BlockSpec(memory_space=pltpu.SMEM)
    vmem = pl.BlockSpec(memory_space=pltpu.VMEM)
    hbm = pl.BlockSpec(memory_space=pltpu.HBM)
    out_shapes = [jax.ShapeDtypeStruct((number, capacity, features), bf16)] + list(out_shapes)
    return pl.pallas_call(
        functools.partial(gram_kernel, picks),
        in_specs=[smem, hbm, hbm, hbm, hbm],
        out_specs=[vmem] * len(out_shapes),
        out_shape=out_shapes,
        scratch_shapes=[
            pltpu.SMEM(counts.shape, i32),
            pltpu.SemaphoreType.DMA(()),
            pltpu.VMEM(peaks.shape, bf16),
            pltpu.SemaphoreType.DMA(()),
            pltpu.VMEM((number, capacity, features), bf16),
            pltpu.VMEM((number, capacity, features), bf16),
            pltpu.SemaphoreType.DMA((2, number)),
        ],
        compiler_params=params(),
        cost_estimate=pl.CostEstimate(
            flops=number * capacity * features * features * 2,
            bytes_accessed=number * (capacity * features * 6 + 2 * HALF * LANES * 4),
            transcendentals=0,
        ),
        name="gram_parts",
    )(me, pinned(counts), pinned(grad), pinned(mom), pinned(peaks))


def joined(first, second):
    line = lax.broadcasted_iota(i32, (AUX, LANES), 0)
    aux = jnp.where(line == 4, jnp.maximum(first[0], second[0]), first[0] + second[0])
    return [aux] + [x + y for x, y in zip(first[1:], second[1:])]


def load_half(ref, index, base=0):
    starts = [base + AUX + place * LANES for place in range(4)]
    return [ref[index, base : base + AUX, :]] + [ref[index, at : at + LANES, :] for at in starts]


def store_half(ref, index, half, base=0):
    ref[index, base : base + AUX, :] = half[0]
    for place in range(4):
        at = base + AUX + place * LANES
        ref[index, at : at + LANES, :] = half[1 + place]


def outer_scales(which, scale):
    row, col = square_iotas()
    across = [scale[g : g + 1] for g in range(BLOCKS)]
    down = {}

    def outer(i, j):
        if i not in down:
            down[i] = jnp.broadcast_to(across[i], (LANES, LANES)).T
        return down[i] * across[j]

    return [
        jnp.where(row <= col, outer(i, i), outer(j, j)) if triangle else outer(i, j)
        for i, j, triangle in HALVES[which]
    ]


def decoded(which, ref, index):
    line = lax.broadcasted_iota(i32, (AUX, LANES), 0)
    codes = ref[index, 0:AUX_CODE, :].astype(i32).astype(f32)
    low, high = codes[0:AUX], codes[AUX:AUX_CODE]
    scale = jnp.where(line < 4, jnp.exp2(low) * jnp.sqrt(high * (1.0 / UNIT)), 0.0)
    aux = jnp.where(line < 4, scale * scale, jnp.where(line == 4, low * (1.0 / 64.0), low))
    half = [aux]
    for place, factor in enumerate(outer_scales(which, scale)):
        at = AUX_CODE + place * LANES
        half.append(ref[index, at : at + LANES, :].astype(i32).astype(f32) * (factor * (1.0 / UNIT)))
    return half


def encode(which, ref, index, half):
    line = lax.broadcasted_iota(i32, (AUX, LANES), 0)
    aux = half[0]
    diagonal = jnp.maximum(aux, 1e-30)
    power = jnp.ceil(0.5 * jnp.log2(diagonal))
    high = jnp.clip(jnp.floor(diagonal * jnp.exp2(-2.0 * power) * UNIT + 0.5), 1.0, 32767.0)
    low = jnp.where(line < 4, power, jnp.where(line == 4, jnp.floor(aux * 64.0 + 0.5), aux))
    high = jnp.where(line < 4, high, 0.0)
    ref[index, 0:AUX_CODE, :] = jnp.concatenate([low, high], axis=0).astype(i32).astype(i16)
    inverse = jnp.where(line < 4, jnp.exp2(-power) * lax.rsqrt(high * (1.0 / UNIT)), 0.0)
    for place, factor in enumerate(outer_scales(which, inverse)):
        at = AUX_CODE + place * LANES
        value = jnp.floor(half[1 + place] * (factor * UNIT) + 0.5)
        value = jnp.clip(value, -32767.0, 32767.0)
        ref[index, at : at + LANES, :] = value.astype(i32).astype(i16)


def local_call(kernel, out_shapes, name, *args):
    size = sum(math.prod(x.shape) * x.dtype.itemsize for x in list(args) + list(out_shapes))
    return pl.pallas_call(
        kernel,
        in_specs=[pl.BlockSpec(memory_space=pltpu.VMEM)] * len(args),
        out_specs=[pl.BlockSpec(memory_space=pltpu.VMEM)] * len(out_shapes),
        out_shape=list(out_shapes),
        compiler_params=params(),
        cost_estimate=pl.CostEstimate(flops=size * 4, bytes_accessed=size, transcendentals=0),
        name=name,
    )(*args)


def first_kernel(message_of, kept, arrived, *refs):
    for which in range(2):
        message, stay = refs[2 * which : 2 * which + 2]
        for index, (send, place) in enumerate(message_of[which]):
            base = which * HALF
            half = joined(load_half(kept, index, base), load_half(arrived, index, base))
            if send:
                encode(which, message, place, half)
            else:
                store_half(stay, place, half)


def sum_kernel(sends, keeps, late, *refs):
    outs = refs[8 if late else 4 :]
    for which in range(2):
        kept, arrived = refs[2 * which : 2 * which + 2]
        message, stay = outs[2 * which : 2 * which + 2]
        for index in range(arrived.shape[0]):
            if late and index == 0:
                half = joined(load_half(refs[4 + which], 0), load_half(refs[6 + which], 0))
            else:
                half = load_half(kept, index - 1 if late else index)
            half = joined(half, decoded(which, arrived, index))
            if index in sends[which]:
                encode(which, message, sends[which].index(index), half)
            if index in keeps[which]:
                store_half(stay, keeps[which].index(index), half)


def mm(x, y):
    return jnp.dot(x, y, preferred_element_type=f32)


def wide(*parts):
    return jnp.concatenate(parts, axis=1)


def tall(*parts):
    return jnp.concatenate(parts, axis=0)


def parts_of(x):
    high = x.astype(bf16)
    return high, (x - high.astype(f32)).astype(bf16)


def unpack_symmetric(which, blocks, diagonal, store):
    row, col = square_iotas()
    for (i, j, triangle), block in zip(HALVES[which], blocks):
        other = block.T
        if triangle:
            first = jnp.where(row < col, block, other)
            second = jnp.where(row > col, block, other)
            store(i, i, jnp.where(row == col, diagonal(i), first))
            store(j, j, jnp.where(row == col, diagonal(j), second))
        else:
            store(i, j, block)
            store(j, i, other)


def iterate_kernel(kept_a, arrived_a, kept_b, arrived_b, out_ref, gram_ref):
    row, col = square_iotas()

    def store(i, j, block):
        gram_ref[i * LANES : (i + 1) * LANES, j * LANES : (j + 1) * LANES] = block

    aux = None
    for which, kept, arrived in ((0, kept_a, arrived_a), (1, kept_b, arrived_b)):
        half = joined(load_half(kept, 0), decoded(which, arrived, 0))
        if aux is None:
            aux = half[0]
        unpack_symmetric(which, half[1:], lambda g: aux[g : g + 1], store)
    line = lax.broadcasted_iota(i32, (AUX, LANES), 0)
    squares = jnp.sum(jnp.where(line < 4, aux, 0.0), axis=0, keepdims=True)
    squares = jnp.sum(squares, axis=1, keepdims=True)
    inverse = 1.0 / (jnp.sqrt(squares) + 1e-07)
    gram = gram_ref[...] * inverse * inverse
    full_row = lax.broadcasted_iota(i32, (KV_RANK, KV_RANK), 0)
    full_col = lax.broadcasted_iota(i32, (KV_RANK, KV_RANK), 1)
    product = None
    for repeat in range(NS_ITERS):
        high, low = parts_of(gram)
        if repeat >= 2:
            square = mm(wide(high, high, low), tall(high, low, high))
        else:
            square = mm(high, high)
        mixing = (coef_second * gram + coef_third * square).astype(bf16)
        if product is None:
            product = jnp.where(full_row == full_col, coef_first, 0.0) + mixing.astype(f32)
        else:
            product_high, product_low = parts_of(product)
            product = coef_first * product + mm(wide(product_high, product_low), tall(mixing, mixing))
        if repeat < NS_ITERS - 1:
            half = coef_first * gram + mm(wide(high, low), tall(mixing, mixing))
            half_high, half_low = parts_of(half)
            gram = coef_first * half + mm(wide(mixing, mixing), tall(half_high, half_low))
    gram_ref[...] = product
    at = AUX_P
    for entries in HALVES:
        for i, j, triangle in entries:
            load = lambda i, j: gram_ref[i * LANES : (i + 1) * LANES, j * LANES : (j + 1) * LANES]
            if triangle:
                block = jnp.where(row <= col, load(i, i), load(j, j))
                block = 0.5 * (block + jnp.where(row <= col, load(i, i).T, load(j, j).T))
            else:
                block = 0.5 * (load(i, j) + load(j, i).T)
            out_ref[at : at + LANES, :] = block.astype(bf16)
            at += LANES

    def three(x):
        high = x.astype(bf16).astype(f32)
        middle = (x - high).astype(bf16).astype(f32)
        return high, middle, x - high - middle

    lines = [[], [], []]
    for i in range(BLOCKS):
        block = gram_ref[i * LANES : (i + 1) * LANES, i * LANES : (i + 1) * LANES]
        diagonal = jnp.sum(jnp.where(row == col, block, 0.0), axis=0, keepdims=True)
        for lines_of, part in zip(lines, three(diagonal)):
            lines_of.append(part)
    peaks = aux[4:5]
    tallies = aux[5:6]
    tally_high = tallies.astype(bf16).astype(f32)
    norm = three(jnp.broadcast_to(inverse, (1, LANES)))
    stacked = lines[0] + lines[1] + lines[2] + [peaks, tally_high, tallies - tally_high] + list(norm)
    place = lax.broadcasted_iota(i32, (AUX_P, LANES), 0)
    table = jnp.zeros((AUX_P, LANES), f32)
    for number, one in enumerate(stacked):
        table = jnp.where(place == number, one, table)
    out_ref[0:AUX_P, :] = table.astype(bf16)


def iterations(*args):
    return pl.pallas_call(
        iterate_kernel,
        in_specs=[pl.BlockSpec(memory_space=pltpu.VMEM)] * 4,
        out_specs=pl.BlockSpec(memory_space=pltpu.VMEM),
        out_shape=jax.ShapeDtypeStruct((ROWS_P, LANES), bf16),
        scratch_shapes=[pltpu.VMEM((KV_RANK, KV_RANK), f32)],
        compiler_params=params(),
        cost_estimate=pl.CostEstimate(
            flops=9 * NS_ITERS * 2 * KV_RANK**3, bytes_accessed=12 * HALF * LANES, transcendentals=0
        ),
        name="iterations",
    )(*args)


def apply_kernel(steps, spread, places, seats, number_of, me, counts, *refs):
    tables = refs[: number_of[0]]
    rows_in = refs[number_of[0] : sum(number_of)]
    weight_ref = refs[sum(number_of)]
    update_out, weight_out, mat_ref, update_ref, new_ref, leaving = refs[-6:]
    groups, rows_block = seats
    dp, expert = me[2] // groups, me[2] % groups
    capacity = weight_ref.shape[1]
    head_rows = NOPE + VDIM
    rms_scale = 0.2 * math.sqrt(max(KV_ROWS, KV_RANK))
    lane = lax.broadcasted_iota(i32, (1, LANES), 1)
    head_shift = head_rows.bit_length() - 1
    assert head_rows == 1 << head_shift and capacity % (16 * CHUNKS) == 0
    rows_of_slots = -(-capacity // LANES)
    slot = lax.broadcasted_iota(i32, (rows_of_slots, LANES), 0) * LANES
    slot = slot + lax.broadcasted_iota(i32, (rows_of_slots, LANES), 1)
    copies = []
    for step, pick in enumerate(steps):
        layer = layer_of(me, *pick)
        (place_a, start_a), (place_b, start_b) = spread[step]
        aux = tables[place_a][start_a : start_a + AUX_P, :].astype(f32)
        diagonal = [aux[i : i + 1] + aux[4 + i : 5 + i] + aux[8 + i : 9 + i] for i in range(BLOCKS)]
        inverse = [1.0 / line for line in diagonal]
        norm = (aux[15:16] + aux[16:17] + aux[17:18]) * rms_scale
        factor = jnp.sqrt(jnp.minimum(1.0, clip_limit / aux[12:13]))
        tallies = aux[13:14] + aux[14:15]

        def store(i, j, block):
            block = (block * inverse[j]).astype(bf16)
            mat_ref[step, i * LANES : (i + 1) * LANES, j * LANES : (j + 1) * LANES] = block

        for which, (place, start) in enumerate(((place_a, start_a + AUX_P), (place_b, start_b))):
            blocks = [
                tables[place][start + k * LANES : start + (k + 1) * LANES, :].astype(f32) for k in range(4)
            ]
            unpack_symmetric(which, blocks, lambda g: diagonal[g], store)
        lowest = dp * groups
        earlier = jnp.where((lane >= lowest) & (lane < lowest + expert), tallies, 0.0)
        base = jnp.sum(earlier, axis=1, keepdims=True).astype(i32) + dp * rows_block
        first_head = base >> head_shift
        row_index = base + slot
        head_of = row_index >> head_shift
        scale = jnp.ones(slot.shape, f32)
        for k in range((capacity - 1) // head_rows + 2):
            one = jnp.sum(jnp.where(lane == first_head + k, factor, 0.0), axis=1, keepdims=True)
            scale = jnp.where(head_of == first_head + k, one, scale)
        scale = jnp.where((row_index & (head_rows - 1)) < NOPE, scale, 1.0)
        scale = jnp.where(slot < counts[layer], scale, 0.0)
        columns = [jnp.broadcast_to(scale[k : k + 1], (LANES, LANES)).T for k in range(slot.shape[0])]
        scale = jnp.concatenate(columns, axis=0)[:capacity]
        kept = scale * (1.0 - learn_rate * decay_rate)
        moved = scale * learn_rate
        source, index = places[step]
        for chunk in range(CHUNKS):
            size = capacity // CHUNKS
            among = slice(chunk * size, (chunk + 1) * size)
            product = mm(rows_in[source][index, among, :], mat_ref[step])
            for i in range(BLOCKS):
                span = slice(i * LANES, (i + 1) * LANES)
                update = product[:, span] * (diagonal[i] * norm)
                update_ref[step, among, span] = update.astype(bf16)
                weight = weight_ref[layer, among, span].astype(f32)
                new_ref[step, among, span] = (weight * kept[among] - update * moved[among]).astype(bf16)
            at = pl.ds(chunk * size, size)
            for number, (held, out) in enumerate(((update_ref, update_out), (new_ref, weight_out))):
                copy = pltpu.make_async_copy(
                    held.at[step, at], out.at[layer, at], leaving.at[number, step * CHUNKS + chunk]
                )
                copy.start()
                copies.append(copy)
    for copy in copies:
        copy.wait()


def apply_rows(steps, spread, places, seats, me, counts, tables, rows, weight, *outs):
    number = len(steps)
    layers, capacity, features = weight.shape
    smem = pl.BlockSpec(memory_space=pltpu.SMEM)
    vmem = pl.BlockSpec(memory_space=pltpu.VMEM)
    hbm = pl.BlockSpec(memory_space=pltpu.HBM)
    args = [me, counts] + list(tables) + list(rows) + [weight] + list(outs)
    shape = jax.ShapeDtypeStruct((layers, capacity, features), bf16)
    return pl.pallas_call(
        functools.partial(apply_kernel, steps, spread, places, seats, (len(tables), len(rows))),
        in_specs=[smem, smem] + [vmem] * (len(tables) + len(rows) + 1) + [hbm] * len(outs),
        out_specs=[hbm, hbm],
        out_shape=[shape, shape],
        scratch_shapes=[
            pltpu.VMEM((number, KV_RANK, KV_RANK), bf16),
            pltpu.VMEM((number, capacity, features), bf16),
            pltpu.VMEM((number, capacity, features), bf16),
            pltpu.SemaphoreType.DMA((2, number * CHUNKS)),
        ],
        input_output_aliases={len(args) - 2: 0, len(args) - 1: 1} if outs else {},
        compiler_params=params(),
        cost_estimate=pl.CostEstimate(
            flops=number * capacity * features * features * 2,
            bytes_accessed=number * capacity * features * 8,
            transcendentals=0,
        ),
        name="apply_rows",
    )(*args)


def local(dp_size, expert_size, grad_rows, momentum_rows, weight_rows, row_counts, logit_peaks):
    layers = grad_rows.shape[1]
    expert_bits = expert_size.bit_length() - 1
    bits = expert_bits - 1
    assert layers == expert_size == 1 << expert_bits and bits >= 2
    assert dp_size == 4 and dp_size * expert_size <= LANES
    dp = lax.axis_index("dp")
    expert = lax.axis_index("expert")
    counts = row_counts.reshape(layers)
    owner = ((dp >> 1) << (bits - 1)) | ((expert >> 1) & ((1 << (bits - 1)) - 1))
    me = jnp.stack([owner, expert & 1, dp * expert_size + expert]).astype(i32)
    owner_axes = [("expert", 1 << (p + 1)) for p in range(bits - 1)] + [("dp", 2)]
    copy_axes = [("dp", 1), ("expert", 1 << (expert_bits - 1))]
    sizes = {"dp": dp_size, "expert": expert_size}

    def over(x, axis_bit):
        axis, bit = axis_bit
        return lax.ppermute(x, axis, [(i, i ^ bit) for i in range(sizes[axis])])

    core_axis = ("expert", 1)
    grad, mom, peaks = grad_rows[0], momentum_rows[0], logit_peaks[0, 0]
    codes = lambda n: jax.ShapeDtypeStruct((n, HALF_CODE, LANES), i16)
    plain = lambda n: jax.ShapeDtypeStruct((n, HALF, LANES), f32)
    both = lambda n: jax.ShapeDtypeStruct((n, 2 * HALF, LANES), f32)
    every = list(range((1 << bits) - 1, 0, -1))
    orders = (list(range(bits - 1, -1, -1)), list(range(bits)))
    sent = [[r for r in range(1 << bits) if r >> orders[w][0] & 1] for w in range(2)]
    current = [[r for r in range(1 << bits) if r not in sent[w]] for w in range(2)]
    stays = [current[w][1:] for w in range(2)]
    message_of = [
        [(True, sent[w].index(r)) if r in sent[w] else (False, stays[w].index(r)) for r in every] for w in range(2)
    ]
    shapes = [shape for w in range(2) for shape in (codes(len(sent[w])), plain(len(stays[w])))]

    sources = (counts, grad, mom, peaks)
    rows_other, other = gram_parts([(r, False) for r in every], [both(len(every))], me, *sources)
    rows_own, own = gram_parts([(r, True) for r in every], [both(len(every))], me, *sources)
    out = list(
        local_call(functools.partial(first_kernel, message_of), shapes, "sum0", own, over(other, core_axis))
    )
    out[0], out[2], me_late = lax.optimization_barrier((out[0], out[2], me))
    rows_zero, *halves = gram_parts([(0, False), (0, True)], [plain(1)] * 4, me_late, *sources)
    late = halves[2:] + [over(x, core_axis) for x in halves[:2]]
    axes = [owner_axes[orders[w][0]] for w in range(2)]
    state = [out[1], over(out[0], axes[0]), out[3], over(out[2], axes[1])]
    for step in range(1, bits + 2):
        if step < bits:
            axes = [owner_axes[orders[w][step]] for w in range(2)]
            sends = [[k for k, r in enumerate(current[w]) if r >> orders[w][step] & 1] for w in range(2)]
            keeps = [[k for k in range(len(current[w])) if k not in sends[w]] for w in range(2)]
            current = [[current[w][k] for k in keeps[w]] for w in range(2)]
        else:
            axes = [copy_axes[step - bits], copy_axes[1 - (step - bits)]]
            sends = keeps = [[0], [0]]
        shapes = [s for w in range(2) for s in (codes(len(sends[w])), plain(len(keeps[w])))]
        kernel = functools.partial(sum_kernel, sends, keeps, bool(late))
        out = local_call(kernel, shapes, "sum" + str(step), *state, *late)
        late = []
        state = [out[1], over(out[0], axes[0]), out[3], over(out[2], axes[1])]
    table = iterations(*state)

    seats = (expert_size, KV_ROWS // dp_size)
    weight = weight_rows[0]
    full = lambda place: ((place, 0), (place, HEAD_P))

    def apply(picks, spread, tables, *outs):
        if picks[0][0] == 0:
            rows, places = [rows_zero], [(0, 1 if own_core else 0) for _, own_core in picks]
        else:
            rows = [rows_own, rows_other]
            places = [(0 if own_core else 1, every.index(r)) for r, own_core in picks]
        return apply_rows(picks, spread, places, seats, me, counts, tables, rows, weight, *outs)

    tables = {0: table}
    for position in range(bits - 1, -1, -1) if bits > 2 else ():
        for known in list(tables):
            tables[known | 1 << position] = over(tables[known], owner_axes[position])
    if bits == 2:
        tables[2], tables[1] = over(table, owner_axes[1]), over(table, owner_axes[0])
    pair = [table, over(table, core_axis)]
    outs = apply(((0, True), (0, False)), (full(0), full(1)), pair)
    if bits == 2:
        tables[1], tables[2], outs = lax.optimization_barrier((tables[1], tables[2], outs))
        tail = [over(tables[1][:HEAD_P], owner_axes[1]), over(tables[2][HEAD_P:], owner_axes[0])]
        near = [tables[1], tables[2]]
        near += [over(x, core_axis) for x in near]
        outs = apply(((1, True), (2, True), (1, False), (2, False)), tuple(full(k) for k in range(4)), near, *outs)
        tail, outs = lax.optimization_barrier((tail, outs))
        tail += [over(x, core_axis) for x in tail]
        spread = (((0, 0), (1, 0)), ((2, 0), (3, 0)))
        outs = apply(((3, True), (3, False)), spread, tail, *outs)
    else:
        for relative in range(1, 1 << bits):
            pair = [tables[relative], over(tables[relative], core_axis)]
            outs = apply(((relative, True), (relative, False)), (full(0), full(1)), pair, *outs)
    return (outs[0][None], outs[1][None])


def solution(mesh):
    return jax.shard_map(
        functools.partial(local, mesh.shape["dp"], mesh.shape["expert"]),
        mesh=mesh,
        in_specs=(
            P("dp", None, "expert", None),
            P("dp", None, "expert", None),
            P("dp", None, "expert", None),
            P("dp", None, "expert"),
            P("dp", "expert", None, None),
        ),
        out_specs=(P("dp", None, "expert", None), P("dp", None, "expert", None)),
        check_vma=False,
    )
```

time: 92 us -> 78.6 us (0.85)
  Pallas kernels: 42.1 us -> 35 us
  waiting for transfers between devices: 28.5 us -> 24.4 us
  local copies, waits for them, and re-layouts: 1.64 us -> 0.03 us
    pallas_call x5 -> x6, Pallas kernels: 28.1 us -> 22 us  [the longest x3 12.5 us: gram_parts(): pl.pallas_call(functools.partial(gram_kernel, picks), in_specs=[smem, hbm...]
    ppermute x18 -> x20, waiting for transfers between devices: 28.5 us -> 24.4 us  [over(): return lax.ppermute(x, axis, [(i, i ^ bit) for i in range(sizes[axis])])]
    unnamed x14 -> x6, local copies, waits for them, and re-layouts: 1.62 us -> 0.01 us
    pallas_call x1, Pallas kernels: 12.3 us -> 11.3 us  [iterations(): pl.pallas_call(iterate_kernel, in_specs=[pl.BlockSpec(memory_space=pltpu....]
    ppermute x18 -> x20, starting transfers between devices: 17.9 us -> 17.9 us  [over(): return lax.ppermute(x, axis, [(i, i ^ bit) for i in range(sizes[axis])])]
  transfers between devices with their start and end apart: 18 -> 20, of which waited for: 11 -> 13; matrix products, arithmetic and copies ran while one was open for 0% -> 0% of each run, Pallas kernels for 19% -> 19%
where the time goes in v3:
time: 78.6 us; the launch traced here: 78.4 us
  Pallas kernels  35 us (45%)
  waiting for transfers between devices  24.4 us (31%)
  starting transfers between devices  17.9 us (23%)
  between operations  0.97 us (1%)
    ppermute x20, waiting for transfers between devices, over(): return lax.ppermute(x, axis, [(i, i ^ bit) for i in range(sizes[axis])])  24.4 us
    ppermute x20, starting transfers between devices, over(): return lax.ppermute(x, axis, [(i, i ^ bit) for i in range(sizes[axis])])  17.9 us
    pallas_call x3, Pallas kernels, gram_parts(): pl.pallas_call(functools.partial(gram_kernel, picks), in_specs=[smem, hbm...  12.5 us
    pallas_call x1, Pallas kernels, iterations(): pl.pallas_call(iterate_kernel, in_specs=[pl.BlockSpec(memory_space=pltpu....  11.3 us
    pallas_call x3, Pallas kernels, apply_rows(): pl.pallas_call(functools.partial(apply_kernel, steps, spread, places, sea...  9.46 us
    pallas_call x4, Pallas kernels, local_call(): pl.pallas_call(kernel, in_specs=[pl.BlockSpec(memory_space=pltpu.VMEM)] *...  1.71 us
  transfers between devices with their start and end apart: 20, of which 13 were waited for; matrix products, arithmetic and copies ran while one was open for 0% of the time, Pallas kernels for 19%

profile of v3, /device:TPU:0, one launch (start us, length us, event | category | flops | bytes accessed | tf_op | source)
XLA Modules:
  0.0 78.4 jit_solution(5794959134408974270)
XLA Ops:
  0.7 4.7 %gram_parts.4 = (bf16[3,640,512]{2,1,0:T(8,128)(2,1)S(1)}, f32[3,1040,128]{2,1,0:T(8,128)S(1)}) custom-call(s32[3]{0:T(128)S(1)} %pad_add_fusion.me, s32[8]{0:T(128)} %bitcast.15, bf16[8,640,512]{2,1,0:T(8,128)(2,1)} %bitcast.21, bf16[8,640,512]{2,1,0:T(8,128)(2,1)} %bitcast.24, bf16[8,64]{1,0:T(8,128)(2,1)} %bitcast.29), custom_call_target="tpu_custom_call" | custom-call | flops 1006632960 | bytes 7495680 | tf_op jit(solution)/shard_map/gram_parts/pallas_call | solution.py:142
  5.9 4.7 %gram_parts.3 = (bf16[3,640,512]{2,1,0:T(8,128)(2,1)S(1)}, f32[3,1040,128]{2,1,0:T(8,128)S(1)}) custom-call(s32[3]{0:T(128)S(1)} %pad_add_fusion.me, s32[8]{0:T(128)} %bitcast.16, bf16[8,640,512]{2,1,0:T(8,128)(2,1)} %bitcast.22, bf16[8,640,512]{2,1,0:T(8,128)(2,1)} %bitcast.25, bf16[8,64]{1,0:T(8,128)(2,1)} %bitcast.30), custom_call_target="tpu_custom_call" | custom-call | flops 1006632960 | bytes 7495680 | tf_op jit(solution)/shard_map/gram_parts/pallas_call | solution.py:142
  11.1 2.6 %collective-permute-start.1 = (s16[2,528,128]{2,1,0:T(8,128)(2,1)S(1)}, s16[2,528,128]{2,1,0:T(8,128)(2,1)S(1)}, u32[]{:S(2)}, u32[]{:S(2)}) collective-permute-start(s16[2,528,128]{2,1,0:T(8,128)(2,1)S(1)} %get-tuple-element.49), channel_id=1, source_target_pairs={{0,16},{8,24},{16,0},{24,8},{1,17},{9,25},{17,1},{25,9},{2,18},{10... | collective-permute-start | bytes 811016 | tf_op jit(solution)/shard_map/ppermute | solution.py:511
  13.7 1.7 %collective-permute-start.2 = (s16[2,528,128]{2,1,0:T(8,128)(2,1)S(1)}, s16[2,528,128]{2,1,0:T(8,128)(2,1)S(1)}, u32[]{:S(2)}, u32[]{:S(2)}) collective-permute-start(s16[2,528,128]{2,1,0:T(8,128)(2,1)S(1)} %get-tuple-element.51), channel_id=1, source_target_pairs={{0,2},{1,3},{2,0},{3,1},{4,6},{5,7},{6,4},{7,5},{8,10},{9,11},{10,... | collective-permute-start | bytes 811016 | tf_op jit(solution)/shard_map/ppermute | solution.py:511
  15.4 3.2 %gram_parts.5 = (bf16[2,640,512]{2,1,0:T(8,128)(2,1)S(1)}, f32[1,520,128]{2,1,0:T(8,128)S(1)}, f32[1,520,128]{2,1,0:T(8,128)S(1)}, f32[1,520,128]{2,1,0:T(8,128)S(1)}, f32[1,520,128]{2,1,0:T(8,128)S(1)}) custom-call(s32[3]{0:T(128)S(1)} %pad_add_fusion.me, s32[8]{0:T(128)} %bitcast.17, bf16[8,640,512]{2,1,0:T(8,128)(2,1)} %bitcast.23, ...), custom_call_target="tpu_custom_call" | custom-call | flops 671088640 | bytes 4997120 | tf_op jit(solution)/shard_map/gram_parts/pallas_call | solution.py:142
  19.1 1.0 %collective-permute-done.3.refs_6_ = f32[1,520,128]{2,1,0:T(8,128)S(1)} collective-permute-done((f32[1,520,128]{2,1,0:T(8,128)S(1)}, f32[1,520,128]{2,1,0:T(8,128)S(1)}, u32[]{:S(2)}, u32[]{:S(2)}) %collective-permute-start.3) | collective-permute-done | bytes 266272 | tf_op jit(solution)/shard_map/ppermute | solution.py:511
  20.8 1.5 %collective-permute-done.2.refs_3_ = s16[2,528,128]{2,1,0:T(8,128)(2,1)S(1)} collective-permute-done((s16[2,528,128]{2,1,0:T(8,128)(2,1)S(1)}, s16[2,528,128]{2,1,0:T(8,128)(2,1)S(1)}, u32[]{:S(2)}, u32[]{:S(2)}) %collective-permute-start.2) | collective-permute-done | bytes 270368 | tf_op jit(solution)/shard_map/ppermute | solution.py:511
  22.8 1.6 %collective-permute-start.5 = (s16[1,528,128]{2,1,0:T(8,128)(2,1)S(1)}, s16[1,528,128]{2,1,0:T(8,128)(2,1)S(1)}, u32[]{:S(2)}, u32[]{:S(2)}) collective-permute-start(s16[1,528,128]{2,1,0:T(8,128)(2,1)S(1)} %get-tuple-element.58), channel_id=1, source_target_pairs={{0,2},{1,3},{2,0},{3,1},{4,6},{5,7},{6,4},{7,5},{8,10},{9,11},{10,... | collective-permute-start | bytes 405512 | tf_op jit(solution)/shard_map/ppermute | solution.py:511
  25.0 2.8 %collective-permute-done.5.refs_1_ = s16[1,528,128]{2,1,0:T(8,128)(2,1)S(1)} collective-permute-done((s16[1,528,128]{2,1,0:T(8,128)(2,1)S(1)}, s16[1,528,128]{2,1,0:T(8,128)(2,1)S(1)}, u32[]{:S(2)}, u32[]{:S(2)}) %collective-permute-start.5) | collective-permute-done | bytes 135200 | tf_op jit(solution)/shard_map/ppermute | solution.py:511
  27.8 1.6 %collective-permute-done.6.refs_3_ = s16[1,528,128]{2,1,0:T(8,128)(2,1)S(1)} collective-permute-done((s16[1,528,128]{2,1,0:T(8,128)(2,1)S(1)}, s16[1,528,128]{2,1,0:T(8,128)(2,1)S(1)}, u32[]{:S(2)}, u32[]{:S(2)}) %collective-permute-start.6) | collective-permute-done | bytes 135200 | tf_op jit(solution)/shard_map/ppermute | solution.py:511
  29.8 1.6 %collective-permute-start.7 = (s16[1,528,128]{2,1,0:T(8,128)(2,1)S(1)}, s16[1,528,128]{2,1,0:T(8,128)(2,1)S(1)}, u32[]{:S(2)}, u32[]{:S(2)}) collective-permute-start(s16[1,528,128]{2,1,0:T(8,128)(2,1)S(1)} %get-tuple-element.62), channel_id=1, source_target_pairs={{0,8},{8,0},{16,24},{24,16},{1,9},{9,1},{17,25},{25,17},{2,10},{10... | collective-permute-start | bytes 405512 | tf_op jit(solution)/shard_map/ppermute | solution.py:511
  31.3 2.6 %collective-permute-start.8 = (s16[1,528,128]{2,1,0:T(8,128)(2,1)S(1)}, s16[1,528,128]{2,1,0:T(8,128)(2,1)S(1)}, u32[]{:S(2)}, u32[]{:S(2)}) collective-permute-start(s16[1,528,128]{2,1,0:T(8,128)(2,1)S(1)} %get-tuple-element.64), channel_id=1, source_target_pairs={{0,4},{1,5},{2,6},{3,7},{4,0},{5,1},{6,2},{7,3},{8,12},{9,13},{10,... | collective-permute-start | bytes 405512 | tf_op jit(solution)/shard_map/ppermute | solution.py:511
  33.9 0.9 %collective-permute-done.7.refs_1_ = s16[1,528,128]{2,1,0:T(8,128)(2,1)S(1)} collective-permute-done((s16[1,528,128]{2,1,0:T(8,128)(2,1)S(1)}, s16[1,528,128]{2,1,0:T(8,128)(2,1)S(1)}, u32[]{:S(2)}, u32[]{:S(2)}) %collective-permute-start.7) | collective-permute-done | bytes 135200 | tf_op jit(solution)/shard_map/ppermute | solution.py:511
  34.9 3.7 %collective-permute-done.8.refs_3_ = s16[1,528,128]{2,1,0:T(8,128)(2,1)S(1)} collective-permute-done((s16[1,528,128]{2,1,0:T(8,128)(2,1)S(1)}, s16[1,528,128]{2,1,0:T(8,128)(2,1)S(1)}, u32[]{:S(2)}, u32[]{:S(2)}) %collective-permute-start.8) | collective-permute-done | bytes 135200 | tf_op jit(solution)/shard_map/ppermute | solution.py:511
  39.6 1.3 %collective-permute-start.9 = (s16[1,528,128]{2,1,0:T(8,128)(2,1)S(1)}, s16[1,528,128]{2,1,0:T(8,128)(2,1)S(1)}, u32[]{:S(2)}, u32[]{:S(2)}) collective-permute-start(s16[1,528,128]{2,1,0:T(8,128)(2,1)S(1)} %get-tuple-element.66), channel_id=1, source_target_pairs={{0,4},{1,5},{2,6},{3,7},{4,0},{5,1},{6,2},{7,3},{8,12},{9,13},{10,... | collective-permute-start | bytes 405512 | tf_op jit(solution)/shard_map/ppermute | solution.py:511
  40.9 3.1 %collective-permute-done.10.arrived_b = s16[1,528,128]{2,1,0:T(8,128)(2,1)S(1)} collective-permute-done((s16[1,528,128]{2,1,0:T(8,128)(2,1)S(1)}, s16[1,528,128]{2,1,0:T(8,128)(2,1)S(1)}, u32[]{:S(2)}, u32[]{:S(2)}) %collective-permute-start.10) | collective-permute-done | bytes 135200 | tf_op jit(solution)/shard_map/ppermute | solution.py:511
  44.0 2.6 %collective-permute-done.9.arrived_a = s16[1,528,128]{2,1,0:T(8,128)(2,1)S(1)} collective-permute-done((s16[1,528,128]{2,1,0:T(8,128)(2,1)S(1)}, s16[1,528,128]{2,1,0:T(8,128)(2,1)S(1)}, u32[]{:S(2)}, u32[]{:S(2)}) %collective-permute-start.9) | collective-permute-done | bytes 135200 | tf_op jit(solution)/shard_map/ppermute | solution.py:511
  46.6 11.3 %iterations.1.refs_0_ = bf16[1056,128]{1,0:T(8,128)(2,1)S(1)} custom-call(f32[1,520,128]{2,1,0:T(8,128)S(1)} %get-tuple-element.65.kept_a, s16[1,528,128]{2,1,0:T(8,128)(2,1)S(1)} %collective-permute-done.9.arrived_a, f32[1,520,128]{2,1,0:T(8,128)S(1)} %get-tuple-element.67.kept_b, s16[1,528,128]{2,1,0:T(8,128)(2,1)S(1)} %collective-permute-done.10.arrived_b), custom_call_target="tpu_custom_call" | custom-call | flops 12079595520 | bytes 798720 | tf_op jit(solution)/shard_map/iterations/pallas_call | solution.py:376
  59.6 2.7 %apply_rows.3 = (bf16[8,640,512]{2,1,0:T(8,128)(2,1)}, bf16[8,640,512]{2,1,0:T(8,128)(2,1)}) custom-call(s32[3]{0:T(128)S(1)} %pad_add_fusion.me, s32[8]{0:T(128)S(1)} %bitcast.18, bf16[1056,128]{1,0:T(8,128)(2,1)S(1)} %iterations.1.refs_0_, bf16[1056,128]{1,0:T(8,128)(2,1)S(1)} %collective-permute-done.13.refs_1_, ...), custom_call_target="tpu_custom_call" | custom-call | flops 671088640 | bytes 5242880 | tf_op jit(solution)/shard_map/apply_rows/pallas_call | solution.py:472
  62.3 4.6 %collective-permute-done.11.refs_0_ = bf16[1056,128]{1,0:T(8,128)(2,1)S(1)} collective-permute-done((bf16[1056,128]{1,0:T(8,128)(2,1)S(1)}, bf16[1056,128]{1,0:T(8,128)(2,1)S(1)}, u32[]{:S(2)}, u32[]{:S(2)}) %collective-permute-start.11) | collective-permute-done | bytes 270368 | tf_op jit(solution)/shard_map/ppermute | solution.py:511
  68.0 1.8 %collective-permute-start.15 = (bf16[512,128]{1,0:T(8,128)(2,1)S(1)}, bf16[512,128]{1,0:T(8,128)(2,1)S(1)}, u32[]{:S(2)}, u32[]{:S(2)}) collective-permute-start(bf16[512,128]{1,0:T(8,128)(2,1)S(1)} %slice.7), channel_id=1, source_target_pairs={{0,2},{1,3},{2,0},{3,1},{4,6},{5,7},{6,4},{7,5},{8,10},{9,11},{10,... | collective-permute-start | bytes 393224 | tf_op jit(solution)/shard_map/ppermute | solution.py:511
  69.8 4.0 %apply_rows.4 = (bf16[8,640,512]{2,1,0:T(8,128)(2,1)}, bf16[8,640,512]{2,1,0:T(8,128)(2,1)}) custom-call(s32[3]{0:T(128)S(1)} %pad_add_fusion.me, s32[8]{0:T(128)S(1)} %bitcast.19, bf16[1056,128]{1,0:T(8,128)(2,1)S(1)} %collective-permute-done.11.refs_0_, ...), custom_call_target="tpu_custom_call", output_to_operand_aliasing={{0}: (9, {}), {1}: (10, {})} | custom-call | flops 1342177280 | bytes 10485760 | tf_op jit(solution)/shard_map/apply_rows/pallas_call | solution.py:472
  74.5 1.0 %collective-permute-done.19.refs_3_ = bf16[512,128]{1,0:T(8,128)(2,1)S(1)} collective-permute-done((bf16[512,128]{1,0:T(8,128)(2,1)S(1)}, bf16[512,128]{1,0:T(8,128)(2,1)S(1)}, u32[]{:S(2)}, u32[]{:S(2)}) %collective-permute-start.19) | collective-permute-done | bytes 131104 | tf_op jit(solution)/shard_map/ppermute | solution.py:511
  75.5 2.7 %apply_rows.5 = (bf16[8,640,512]{2,1,0:T(8,128)(2,1)}, bf16[8,640,512]{2,1,0:T(8,128)(2,1)}) custom-call(s32[3]{0:T(128)S(1)} %pad_add_fusion.me, s32[8]{0:T(128)S(1)} %bitcast.20, bf16[544,128]{1,0:T(8,128)(2,1)S(1)} %collective-permute-done.14.refs_0_, ...), custom_call_target="tpu_custom_call", output_to_operand_aliasing={{0}: (9, {}), {1}: (10, {})} | custom-call | flops 671088640 | bytes 5242880 | tf_op jit(solution)/shard_map/apply_rows/pallas_call | solution.py:472
  (37 shorter events, 8.1 us)
Async XLA Ops:
  5.4 5.2 %collective-permute-start = (f32[3,1040,128]{2,1,0:T(8,128)S(1)}, f32[3,1040,128]{2,1,0:T(8,128)S(1)}, u32[]{:S(2)}, u32[]{:S(2)}) collective-permute-start(f32[3,1040,128]{2,1,0:T(8,128)S(1)} %get-tuple-element.45), channel_id=1, source_target_pairs={{0,1},{1,0},{2,3},{3,2},{4,5},{5,4},{6,7},{7,6},{8,9},{9,8},{10,11... | collective-permute-start | bytes 4792328 | tf_op jit(solution)/shard_map/ppermute | solution.py:511
  11.1 9.7 %collective-permute-start.1 = (s16[2,528,128]{2,1,0:T(8,128)(2,1)S(1)}, s16[2,528,128]{2,1,0:T(8,128)(2,1)S(1)}, u32[]{:S(2)}, u32[]{:S(2)}) collective-permute-start(s16[2,528,128]{2,1,0:T(8,128)(2,1)S(1)} %get-tuple-element.49), channel_id=1, source_target_pairs={{0,16},{8,24},{16,0},{24,8},{1,17},{9,25},{17,1},{25,9},{2,18},{10... | collective-permute-start | bytes 811016 | tf_op jit(solution)/shard_map/ppermute | solution.py:511
  13.7 8.6 %collective-permute-start.2 = (s16[2,528,128]{2,1,0:T(8,128)(2,1)S(1)}, s16[2,528,128]{2,1,0:T(8,128)(2,1)S(1)}, u32[]{:S(2)}, u32[]{:S(2)}) collective-permute-start(s16[2,528,128]{2,1,0:T(8,128)(2,1)S(1)} %get-tuple-element.51), channel_id=1, source_target_pairs={{0,2},{1,3},{2,0},{3,1},{4,6},{5,7},{6,4},{7,5},{8,10},{9,11},{10,... | collective-permute-start | bytes 811016 | tf_op jit(solution)/shard_map/ppermute | solution.py:511
  18.6 1.6 %collective-permute-start.3 = (f32[1,520,128]{2,1,0:T(8,128)S(1)}, f32[1,520,128]{2,1,0:T(8,128)S(1)}, u32[]{:S(2)}, u32[]{:S(2)}) collective-permute-start(f32[1,520,128]{2,1,0:T(8,128)S(1)} %get-tuple-element.55), channel_id=1, source_target_pairs={{0,1},{1,0},{2,3},{3,2},{4,5},{5,4},{6,7},{7,6},{8,9},{9,8},{10,11... | collective-permute-start | bytes 798728 | tf_op jit(solution)/shard_map/ppermute | solution.py:511
  18.6 1.9 %collective-permute-start.4 = (f32[1,520,128]{2,1,0:T(8,128)S(1)}, f32[1,520,128]{2,1,0:T(8,128)S(1)}, u32[]{:S(2)}, u32[]{:S(2)}) collective-permute-start(f32[1,520,128]{2,1,0:T(8,128)S(1)} %get-tuple-element.56), channel_id=1, source_target_pairs={{0,1},{1,0},{2,3},{3,2},{4,5},{5,4},{6,7},{7,6},{8,9},{9,8},{10,11... | collective-permute-start | bytes 798728 | tf_op jit(solution)/shard_map/ppermute | solution.py:511
  22.8 5.1 %collective-permute-start.5 = (s16[1,528,128]{2,1,0:T(8,128)(2,1)S(1)}, s16[1,528,128]{2,1,0:T(8,128)(2,1)S(1)}, u32[]{:S(2)}, u32[]{:S(2)}) collective-permute-start(s16[1,528,128]{2,1,0:T(8,128)(2,1)S(1)} %get-tuple-element.58), channel_id=1, source_target_pairs={{0,2},{1,3},{2,0},{3,1},{4,6},{5,7},{6,4},{7,5},{8,10},{9,11},{10,... | collective-permute-start | bytes 405512 | tf_op jit(solution)/shard_map/ppermute | solution.py:511
  24.4 5.0 %collective-permute-start.6 = (s16[1,528,128]{2,1,0:T(8,128)(2,1)S(1)}, s16[1,528,128]{2,1,0:T(8,128)(2,1)S(1)}, u32[]{:S(2)}, u32[]{:S(2)}) collective-permute-start(s16[1,528,128]{2,1,0:T(8,128)(2,1)S(1)} %get-tuple-element.60), channel_id=1, source_target_pairs={{0,16},{8,24},{16,0},{24,8},{1,17},{9,25},{17,1},{25,9},{2,18},{10... | collective-permute-start | bytes 405512 | tf_op jit(solution)/shard_map/ppermute | solution.py:511
  29.4 30.1 %slice-start = ((s8[5242880]{0:T(1024)(128)(4,1)}), s8[4194304]{0:T(1024)(128)(4,1)S(1)}, s32[]{:S(2)}) async-start(s8[5242880]{0:T(1024)(128)(4,1)} %bitcast.10), calls=%async_computation | async-start | bytes 8388608
  29.8 5.1 %collective-permute-start.7 = (s16[1,528,128]{2,1,0:T(8,128)(2,1)S(1)}, s16[1,528,128]{2,1,0:T(8,128)(2,1)S(1)}, u32[]{:S(2)}, u32[]{:S(2)}) collective-permute-start(s16[1,528,128]{2,1,0:T(8,128)(2,1)S(1)} %get-tuple-element.62), channel_id=1, source_target_pairs={{0,8},{8,0},{16,24},{24,16},{1,9},{9,1},{17,25},{25,17},{2,10},{10... | collective-permute-start | bytes 405512 | tf_op jit(solution)/shard_map/ppermute | solution.py:511
  31.3 7.3 %collective-permute-start.8 = (s16[1,528,128]{2,1,0:T(8,128)(2,1)S(1)}, s16[1,528,128]{2,1,0:T(8,128)(2,1)S(1)}, u32[]{:S(2)}, u32[]{:S(2)}) collective-permute-start(s16[1,528,128]{2,1,0:T(8,128)(2,1)S(1)} %get-tuple-element.64), channel_id=1, source_target_pairs={{0,4},{1,5},{2,6},{3,7},{4,0},{5,1},{6,2},{7,3},{8,12},{9,13},{10,... | collective-permute-start | bytes 405512 | tf_op jit(solution)/shard_map/ppermute | solution.py:511
  39.0 5.1 %collective-permute-start.10 = (s16[1,528,128]{2,1,0:T(8,128)(2,1)S(1)}, s16[1,528,128]{2,1,0:T(8,128)(2,1)S(1)}, u32[]{:S(2)}, u32[]{:S(2)}) collective-permute-start(s16[1,528,128]{2,1,0:T(8,128)(2,1)S(1)} %get-tuple-element.68), channel_id=1, source_target_pairs={{0,8},{8,0},{16,24},{24,16},{1,9},{9,1},{17,25},{25,17},{2,10},{10... | collective-permute-start | bytes 405512 | tf_op jit(solution)/shard_map/ppermute | solution.py:511
  39.6 7.0 %collective-permute-start.9 = (s16[1,528,128]{2,1,0:T(8,128)(2,1)S(1)}, s16[1,528,128]{2,1,0:T(8,128)(2,1)S(1)}, u32[]{:S(2)}, u32[]{:S(2)}) collective-permute-start(s16[1,528,128]{2,1,0:T(8,128)(2,1)S(1)} %get-tuple-element.66), channel_id=1, source_target_pairs={{0,4},{1,5},{2,6},{3,7},{4,0},{5,1},{6,2},{7,3},{8,12},{9,13},{10,... | collective-permute-start | bytes 405512 | tf_op jit(solution)/shard_map/ppermute | solution.py:511
  46.6 13.0 %slice-start.1 = ((s8[5242880]{0:T(1024)(128)(4,1)}), s8[1048576]{0:T(1024)(128)(4,1)S(1)}, s32[]{:S(2)}) async-start(s8[5242880]{0:T(1024)(128)(4,1)} %bitcast.10), calls=%async_computation.1 | async-start | bytes 2097152
  46.6 13.0 %copy-start = (s32[1,8,1]{1,2,0:T(1,128)S(1)}, s32[1,8,1]{1,2,0:T(1,128)}, u32[]{:S(2)}) copy-start(s32[1,8,1]{1,2,0:T(1,128)} %param.8) | copy-start | bytes 100
  57.9 1.6 %collective-permute-start.13 = (bf16[1056,128]{1,0:T(8,128)(2,1)S(1)}, bf16[1056,128]{1,0:T(8,128)(2,1)S(1)}, u32[]{:S(2)}, u32[]{:S(2)}) collective-permute-start(bf16[1056,128]{1,0:T(8,128)(2,1)S(1)} %iterations.1.refs_0_), channel_id=1, source_target_pairs={{0,1},{1,0},{2,3},{3,2},{4,5},{5,4},{6,7},{7,6},{8,9},{9,8},{10,11... | collective-permute-start | bytes 811016 | tf_op jit(solution)/shard_map/ppermute | solution.py:511
  58.0 8.9 %collective-permute-start.11 = (bf16[1056,128]{1,0:T(8,128)(2,1)S(1)}, bf16[1056,128]{1,0:T(8,128)(2,1)S(1)}, u32[]{:S(2)}, u32[]{:S(2)}) collective-permute-start(bf16[1056,128]{1,0:T(8,128)(2,1)S(1)} %iterations.1.refs_0_), channel_id=1, source_target_pairs={{0,2},{1,3},{2,0},{3,1},{4,6},{5,7},{6,4},{7,5},{8,10},{9,11},{10,... | collective-permute-start | bytes 811016 | tf_op jit(solution)/shard_map/ppermute | solution.py:511
  58.1 8.8 %collective-permute-start.12 = (bf16[1056,128]{1,0:T(8,128)(2,1)S(1)}, bf16[1056,128]{1,0:T(8,128)(2,1)S(1)}, u32[]{:S(2)}, u32[]{:S(2)}) collective-permute-start(bf16[1056,128]{1,0:T(8,128)(2,1)S(1)} %iterations.1.refs_0_), channel_id=1, source_target_pairs={{0,16},{8,24},{16,0},{24,8},{1,17},{9,25},{17,1},{25,9},{2,18},{10... | collective-permute-start | bytes 811016 | tf_op jit(solution)/shard_map/ppermute | solution.py:511
  66.9 2.9 %collective-permute-start.16 = (bf16[1056,128]{1,0:T(8,128)(2,1)S(1)}, bf16[1056,128]{1,0:T(8,128)(2,1)S(1)}, u32[]{:S(2)}, u32[]{:S(2)}) collective-permute-start(bf16[1056,128]{1,0:T(8,128)(2,1)S(1)} %collective-permute-done.11.refs_0_), channel_id=1, source_target_pairs={{0,1},{1,0},{2,3},{3,2},{4,5},{5,4},{6,7},{7,6},{8,9},{9,8},{10,11... | collective-permute-start | bytes 811016 | tf_op jit(solution)/shard_map/ppermute | solution.py:511
  66.9 2.9 %collective-permute-start.17 = (bf16[1056,128]{1,0:T(8,128)(2,1)S(1)}, bf16[1056,128]{1,0:T(8,128)(2,1)S(1)}, u32[]{:S(2)}, u32[]{:S(2)}) collective-permute-start(bf16[1056,128]{1,0:T(8,128)(2,1)S(1)} %collective-permute-done.12.refs_1_), channel_id=1, source_target_pairs={{0,1},{1,0},{2,3},{3,2},{4,5},{5,4},{6,7},{7,6},{8,9},{9,8},{10,11... | collective-permute-start | bytes 811016 | tf_op jit(solution)/shard_map/ppermute | solution.py:511
  67.4 6.4 %collective-permute-start.14 = (bf16[544,128]{1,0:T(8,128)(2,1)S(1)}, bf16[544,128]{1,0:T(8,128)(2,1)S(1)}, u32[]{:S(2)}, u32[]{:S(2)}) collective-permute-start(bf16[544,128]{1,0:T(8,128)(2,1)S(1)} %slice.6), channel_id=1, source_target_pairs={{0,16},{8,24},{16,0},{24,8},{1,17},{9,25},{17,1},{25,9},{2,18},{10... | collective-permute-start | bytes 417800 | tf_op jit(solution)/shard_map/ppermute | solution.py:511
  68.0 5.8 %collective-permute-start.15 = (bf16[512,128]{1,0:T(8,128)(2,1)S(1)}, bf16[512,128]{1,0:T(8,128)(2,1)S(1)}, u32[]{:S(2)}, u32[]{:S(2)}) collective-permute-start(bf16[512,128]{1,0:T(8,128)(2,1)S(1)} %slice.7), channel_id=1, source_target_pairs={{0,2},{1,3},{2,0},{3,1},{4,6},{5,7},{6,4},{7,5},{8,10},{9,11},{10,... | collective-permute-start | bytes 393224 | tf_op jit(solution)/shard_map/ppermute | solution.py:511
  73.9 1.6 %collective-permute-start.18 = (bf16[544,128]{1,0:T(8,128)(2,1)S(1)}, bf16[544,128]{1,0:T(8,128)(2,1)S(1)}, u32[]{:S(2)}, u32[]{:S(2)}) collective-permute-start(bf16[544,128]{1,0:T(8,128)(2,1)S(1)} %collective-permute-done.14.refs_0_), channel_id=1, source_target_pairs={{0,1},{1,0},{2,3},{3,2},{4,5},{5,4},{6,7},{7,6},{8,9},{9,8},{10,11... | collective-permute-start | bytes 417800 | tf_op jit(solution)/shard_map/ppermute | solution.py:511
  74.0 1.5 %collective-permute-start.19 = (bf16[512,128]{1,0:T(8,128)(2,1)S(1)}, bf16[512,128]{1,0:T(8,128)(2,1)S(1)}, u32[]{:S(2)}, u32[]{:S(2)}) collective-permute-start(bf16[512,128]{1,0:T(8,128)(2,1)S(1)} %collective-permute-done.15.refs_1_), channel_id=1, source_target_pairs={{0,1},{1,0},{2,3},{3,2},{4,5},{5,4},{6,7},{7,6},{8,9},{9,8},{10,11... | collective-permute-start | bytes 393224 | tf_op jit(solution)/shard_map/ppermute | solution.py:511

commit v4 on v3

v4 whole, which is shorter than its diff:
```python
import functools
import math

import jax
import jax.numpy as jnp
from jax import lax
from jax.experimental import pallas as pl
from jax.experimental.pallas import tpu as pltpu
from jax.sharding import PartitionSpec as P

KV_RANK = 512
NOPE = 128
VDIM = 128
NS_ITERS = 5
KV_ROWS = 16384

momentum_coef = 0.95
learn_rate = 0.02
decay_rate = 0.1
clip_limit = 100.0
coef_first = 3.4445
coef_second = -4.775
coef_third = 2.0315

f32 = jnp.float32
bf16 = jnp.bfloat16
i16 = jnp.int16
i32 = jnp.int32

LANES = 128
BLOCKS = KV_RANK // LANES
HALVES = (
    ((0, 1, True), (0, 1, False), (0, 2, False), (1, 2, False)),
    ((2, 3, True), (0, 3, False), (1, 3, False), (2, 3, False)),
)
AUX = 8
HALF = AUX + 4 * LANES
AUX_CODE = 16
HALF_CODE = AUX_CODE + 4 * LANES
AUX_P = 32
HEAD_P = AUX_P + 4 * LANES
ROWS_P = AUX_P + 8 * LANES
UNIT = 32000.0
CHUNKS = 2


SHORT = pl.CostEstimate(flops=1000, bytes_accessed=1000, transcendentals=0)


def params(mebibytes=40):
    return pltpu.CompilerParams(vmem_limit_bytes=mebibytes * 1024 * 1024)


def pinned(x):
    return pltpu.with_memory_space_constraint(x, pltpu.HBM)


def square_iotas():
    row = lax.broadcasted_iota(i32, (LANES, LANES), 0)
    col = lax.broadcasted_iota(i32, (LANES, LANES), 1)
    return row, col


def owner_bits(expert_size):
    return expert_size.bit_length() - 2


def place_of(expert_size):
    bits = owner_bits(expert_size)
    dp = lax.axis_index("dp").astype(i32)
    expert = lax.axis_index("expert").astype(i32)
    owner = ((dp >> 1) << (bits - 1)) | ((expert >> 1) & ((1 << (bits - 1)) - 1))
    return owner, expert & 1, dp * expert_size + expert


def layer_of(place, relative, own_core):
    core = place[1] if own_core else 1 - place[1]
    if isinstance(relative, tuple):
        relative = jnp.where(core == 0, relative[0], relative[1])
    return 2 * (place[0] ^ relative) + core


def gram_kernel(expert_size, picks, later, first, *refs):
    grad_ref, mom_ref = refs[:2]
    place = place_of(expert_size)
    if first:
        counts_ref, peaks_ref = refs[2:4]
        counts, peaks_buf, grad_buf, mom_buf, arrivals, own_arrivals, small_arrivals = refs[-7:]
        outs = refs[4:-7]
        facts_ref, outs = outs[0], outs[1:]
    else:
        facts_ref, grad_buf, mom_buf = refs[2:5]
        arrivals = refs[-1]
        outs = refs[5:-1]
    nes_ref, outs = outs[0], outs[1:]
    gram_refs, loads = outs[: 2 * len(picks)], outs[2 * len(picks) :]
    layers = [layer_of(place, *pick) for pick in picks]

    def copies_of(chosen, buffers, semaphores):
        return [
            pltpu.make_async_copy(source.at[layer], buffer.at[k], semaphores.at[n, k])
            for k, layer in enumerate(chosen)
            for n, (source, buffer) in enumerate(((grad_ref, buffers[0]), (mom_ref, buffers[1])))
        ]

    own_copies = copies_of(layers, (grad_buf, mom_buf), own_arrivals) if first else []
    small = []
    if first:
        small = [
            pltpu.make_async_copy(counts_ref, counts, small_arrivals.at[0]),
            pltpu.make_async_copy(peaks_ref, peaks_buf, small_arrivals.at[1]),
        ]
    late_copies = copies_of([layer_of(place, *pick) for pick in later], loads, arrivals) if later else []
    for copy in small + own_copies + late_copies:
        copy.start()
    row, col = square_iotas()
    line = lax.broadcasted_iota(i32, (AUX, LANES), 0)
    lane = lax.broadcasted_iota(i32, (AUX, LANES), 1)
    if first:
        for copy in small:
            copy.wait()
        every_peak = peaks_buf[...].astype(f32)
        every_peak = jnp.concatenate(
            [every_peak, jnp.zeros((every_peak.shape[0], LANES - every_peak.shape[1]), f32)], axis=1
        )
        for layer in range(every_peak.shape[0]):
            count = counts[layer].astype(f32)
            fact = jnp.where(line == 4, every_peak[layer : layer + 1], jnp.zeros((AUX, LANES), f32))
            fact = jnp.where((line == 6) | ((line == 5) & (lane == place[2])), count, fact)
            facts_ref[layer] = fact
    width = KV_RANK // 2
    dims = (((0,), (0,)), ((), ()))
    slot = lax.broadcasted_iota(i32, (grad_buf.shape[1], LANES), 0)

    def form_rows(k):
        for copy in own_copies[2 * k : 2 * k + 2]:
            copy.wait()
        live = slot < facts_ref[layers[k], 6:7, :].astype(i32)
        for i in range(BLOCKS):
            span = slice(i * LANES, (i + 1) * LANES)
            gradient = grad_buf[k, :, span].astype(f32)
            velocity = momentum_coef * mom_buf[k, :, span].astype(f32) + gradient
            nesterov = gradient + momentum_coef * velocity
            nes_ref[k, :, span] = jnp.where(live, nesterov, 0.0).astype(bf16)

    form_rows(0)
    for k, layer in enumerate(layers):
        if k + 1 < len(layers):
            form_rows(k + 1)
        rows = nes_ref[k]
        upper = lax.dot_general(rows[:, :width], rows, dims, preferred_element_type=f32)
        lower = lax.dot_general(rows[:, width:], rows[:, width:], dims, preferred_element_type=f32)

        def block(i, j):
            if i < 2:
                return upper[i * LANES : (i + 1) * LANES, j * LANES : (j + 1) * LANES]
            return lower[(i - 2) * LANES : (i - 1) * LANES, (j - 2) * LANES : (j - 1) * LANES]

        aux = jnp.where(line == 6, 0.0, facts_ref[layer])
        for i in range(BLOCKS):
            diagonal = jnp.sum(jnp.where(row == col, block(i, i), 0.0), axis=0, keepdims=True)
            aux = jnp.where(line == i, diagonal, aux)
        for which, entries in enumerate(HALVES):
            half = [aux]
            for i, j, triangle in entries:
                half.append(jnp.where(row <= col, block(i, i), block(j, j)) if triangle else block(i, j))
            store_half(gram_refs[2 * k + which], 0, half)
    for copy in late_copies:
        copy.wait()


def gram_parts(expert_size, picks, later, sources, facts=None, loaded=()):
    grad, mom, counts, peaks = sources
    layers, capacity, features = grad.shape
    first = facts is None
    number = len(picks)
    vmem = pl.BlockSpec(memory_space=pltpu.VMEM)
    hbm = pl.BlockSpec(memory_space=pltpu.HBM)
    rows = lambda n: jax.ShapeDtypeStruct((n, capacity, features), bf16)
    out_shapes = [jax.ShapeDtypeStruct((layers, AUX, LANES), f32)] if first else []
    out_shapes += [rows(number)] + [jax.ShapeDtypeStruct((1, HALF, LANES), f32)] * (2 * number)
    out_shapes += [rows(len(later))] * 2 if later else []
    args = [pinned(grad), pinned(mom)]
    args += [pinned(counts), pinned(peaks)] if first else [facts] + list(loaded)
    scratch = []
    if first:
        scratch += [pltpu.SMEM(counts.shape, i32), pltpu.VMEM(peaks.shape, bf16)]
        scratch += [pltpu.VMEM((number, capacity, features), bf16)] * 2
    scratch += [pltpu.SemaphoreType.DMA((2, max(len(later), 1)))]
    if first:
        scratch += [pltpu.SemaphoreType.DMA((2, number)), pltpu.SemaphoreType.DMA((2,))]
    out = pl.pallas_call(
        functools.partial(gram_kernel, expert_size, picks, later, first),
        in_specs=[hbm] * (4 if first else 2) + [vmem] * (0 if first else 3),
        out_specs=[vmem] * len(out_shapes),
        out_shape=out_shapes,
        scratch_shapes=scratch,
        compiler_params=params(),
        cost_estimate=SHORT,
        name="gram_parts",
    )(*args)
    if first:
        facts, out = out[0], out[1:]
    halves = [list(out[at : at + 2]) for at in range(1, 1 + 2 * number, 2)]
    return facts, out[0], halves, tuple(out[1 + 2 * number :])


def joined(first, second):
    line = lax.broadcasted_iota(i32, (AUX, LANES), 0)
    aux = jnp.where(line == 4, jnp.maximum(first[0], second[0]), first[0] + second[0])
    return [aux] + [x + y for x, y in zip(first[1:], second[1:])]


def load_half(ref, index, base=0):
    starts = [base + AUX + place * LANES for place in range(4)]
    return [ref[index, base : base + AUX, :]] + [ref[index, at : at + LANES, :] for at in starts]


def store_half(ref, index, half, base=0):
    ref[index, base : base + AUX, :] = half[0]
    for place in range(4):
        at = base + AUX + place * LANES
        ref[index, at : at + LANES, :] = half[1 + place]


def outer_scales(which, scale):
    row, col = square_iotas()
    across = [scale[g : g + 1] for g in range(BLOCKS)]
    down = {}

    def outer(i, j):
        if i not in down:
            down[i] = jnp.broadcast_to(across[i], (LANES, LANES)).T
        return down[i] * across[j]

    return [
        jnp.where(row <= col, outer(i, i), outer(j, j)) if triangle else outer(i, j)
        for i, j, triangle in HALVES[which]
    ]


def decoded(which, ref, index, base=0):
    line = lax.broadcasted_iota(i32, (AUX, LANES), 0)
    codes = ref[index, base : base + AUX_CODE, :].astype(i32).astype(f32)
    low, high = codes[0:AUX], codes[AUX:AUX_CODE]
    scale = jnp.where(line < 4, jnp.exp2(low) * jnp.sqrt(high * (1.0 / UNIT)), 0.0)
    aux = jnp.where(line < 4, scale * scale, jnp.where(line == 4, low * (1.0 / 64.0), low))
    half = [aux]
    for place, factor in enumerate(outer_scales(which, scale)):
        at = base + AUX_CODE + place * LANES
        half.append(ref[index, at : at + LANES, :].astype(i32).astype(f32) * (factor * (1.0 / UNIT)))
    return half


def encode(which, ref, index, half, base=0):
    line = lax.broadcasted_iota(i32, (AUX, LANES), 0)
    aux = half[0]
    diagonal = jnp.maximum(aux, 1e-30)
    power = jnp.ceil(0.5 * jnp.log2(diagonal))
    high = jnp.clip(jnp.floor(diagonal * jnp.exp2(-2.0 * power) * UNIT + 0.5), 1.0, 32767.0)
    low = jnp.where(line < 4, power, jnp.where(line == 4, jnp.floor(aux * 64.0 + 0.5), aux))
    high = jnp.where(line < 4, high, 0.0)
    ref[index, base : base + AUX_CODE, :] = jnp.concatenate([low, high], axis=0).astype(i32).astype(i16)
    inverse = jnp.where(line < 4, jnp.exp2(-power) * lax.rsqrt(high * (1.0 / UNIT)), 0.0)
    for place, factor in enumerate(outer_scales(which, inverse)):
        at = base + AUX_CODE + place * LANES
        value = jnp.floor(half[1 + place] * (factor * UNIT) + 0.5)
        value = jnp.clip(value, -32767.0, 32767.0)
        ref[index, at : at + LANES, :] = value.astype(i32).astype(i16)


def local_call(kernel, out_shapes, name, *args):
    return pl.pallas_call(
        kernel,
        in_specs=[pl.BlockSpec(memory_space=pltpu.VMEM)] * len(args),
        out_specs=[pl.BlockSpec(memory_space=pltpu.VMEM)] * len(out_shapes),
        out_shape=list(out_shapes),
        compiler_params=params(),
        cost_estimate=SHORT,
        name=name,
    )(*args)


def send_kernel(number, *refs):
    for k in range(number):
        own, partner, message = refs[4 * k : 4 * k + 2], refs[4 * k + 2 : 4 * k + 4], refs[4 * number + k]
        for which in range(2):
            half = joined(load_half(own[which], 0), load_half(partner[which], 0))
            encode(which, message, 0, half, which * HALF_CODE)


def gather_kernel(*refs):
    messages, outs, stay = refs[4:-3], refs[-3:-1], refs[-1]
    for which in range(2):
        half = joined(load_half(refs[which], 0), load_half(refs[2 + which], 0))
        for arrived in messages:
            half = joined(half, decoded(which, arrived, 0, which * HALF_CODE))
        encode(which, outs[which], 0, half)
        store_half(stay, 0, half, which * HALF)


def sum_kernel(kept, arrived_a, arrived_b, *refs):
    outs, stay = refs[:2], refs[2]
    for which, arrived in enumerate((arrived_a, arrived_b)):
        half = joined(load_half(kept, 0, which * HALF), decoded(which, arrived, 0))
        encode(which, outs[which], 0, half)
        store_half(stay, 0, half, which * HALF)


def mm(x, y):
    return jnp.dot(x, y, preferred_element_type=f32)


def wide(*parts):
    return jnp.concatenate(parts, axis=1)


def tall(*parts):
    return jnp.concatenate(parts, axis=0)


def parts_of(x):
    high = x.astype(bf16)
    return high, (x - high.astype(f32)).astype(bf16)


def unpack_symmetric(which, blocks, diagonal, store):
    row, col = square_iotas()
    for (i, j, triangle), block in zip(HALVES[which], blocks):
        other = block.T
        if triangle:
            first = jnp.where(row < col, block, other)
            second = jnp.where(row > col, block, other)
            store(i, i, jnp.where(row == col, diagonal(i), first))
            store(j, j, jnp.where(row == col, diagonal(j), second))
        else:
            store(i, j, block)
            store(j, i, other)


def iterate_kernel(kept, arrived_a, arrived_b, out_ref, gram_ref):
    row, col = square_iotas()

    def store(i, j, block):
        gram_ref[i * LANES : (i + 1) * LANES, j * LANES : (j + 1) * LANES] = block

    aux = None
    for which, arrived in enumerate((arrived_a, arrived_b)):
        half = joined(load_half(kept, 0, which * HALF), decoded(which, arrived, 0))
        if aux is None:
            aux = half[0]
        unpack_symmetric(which, half[1:], lambda g: aux[g : g + 1], store)
    line = lax.broadcasted_iota(i32, (AUX, LANES), 0)
    squares = jnp.sum(jnp.where(line < 4, aux, 0.0), axis=0, keepdims=True)
    squares = jnp.sum(squares, axis=1, keepdims=True)
    inverse = 1.0 / (jnp.sqrt(squares) + 1e-07)
    gram = gram_ref[...] * inverse * inverse
    full_row = lax.broadcasted_iota(i32, (KV_RANK, KV_RANK), 0)
    full_col = lax.broadcasted_iota(i32, (KV_RANK, KV_RANK), 1)
    product = None
    for repeat in range(NS_ITERS):
        high, low = parts_of(gram)
        if repeat >= 2:
            square = mm(wide(high, high, low), tall(high, low, high))
        else:
            square = mm(high, high)
        mixing = (coef_second * gram + coef_third * square).astype(bf16)
        if product is None:
            product = jnp.where(full_row == full_col, coef_first, 0.0) + mixing.astype(f32)
        else:
            product_high, product_low = parts_of(product)
            product = coef_first * product + mm(wide(product_high, product_low), tall(mixing, mixing))
        if repeat < NS_ITERS - 1:
            half = coef_first * gram + mm(wide(high, low), tall(mixing, mixing))
            half_high, half_low = parts_of(half)
            gram = coef_first * half + mm(wide(mixing, mixing), tall(half_high, half_low))
    gram_ref[...] = product
    at = AUX_P
    for entries in HALVES:
        for i, j, triangle in entries:
            load = lambda i, j: gram_ref[i * LANES : (i + 1) * LANES, j * LANES : (j + 1) * LANES]
            if triangle:
                block = jnp.where(row <= col, load(i, i), load(j, j))
                block = 0.5 * (block + jnp.where(row <= col, load(i, i).T, load(j, j).T))
            else:
                block = 0.5 * (load(i, j) + load(j, i).T)
            out_ref[at : at + LANES, :] = block.astype(bf16)
            at += LANES

    def three(x):
        high = x.astype(bf16).astype(f32)
        middle = (x - high).astype(bf16).astype(f32)
        return high, middle, x - high - middle

    lines = [[], [], []]
    for i in range(BLOCKS):
        block = gram_ref[i * LANES : (i + 1) * LANES, i * LANES : (i + 1) * LANES]
        diagonal = jnp.sum(jnp.where(row == col, block, 0.0), axis=0, keepdims=True)
        for lines_of, part in zip(lines, three(diagonal)):
            lines_of.append(part)
    peaks = aux[4:5]
    tallies = aux[5:6]
    tally_high = tallies.astype(bf16).astype(f32)
    norm = three(jnp.broadcast_to(inverse, (1, LANES)))
    stacked = lines[0] + lines[1] + lines[2] + [peaks, tally_high, tallies - tally_high] + list(norm)
    place = lax.broadcasted_iota(i32, (AUX_P, LANES), 0)
    table = jnp.zeros((AUX_P, LANES), f32)
    for number, one in enumerate(stacked):
        table = jnp.where(place == number, one, table)
    out_ref[0:AUX_P, :] = table.astype(bf16)


def iterations(*args):
    return pl.pallas_call(
        iterate_kernel,
        in_specs=[pl.BlockSpec(memory_space=pltpu.VMEM)] * 3,
        out_specs=pl.BlockSpec(memory_space=pltpu.VMEM),
        out_shape=jax.ShapeDtypeStruct((ROWS_P, LANES), bf16),
        scratch_shapes=[pltpu.VMEM((KV_RANK, KV_RANK), f32)],
        compiler_params=params(),
        cost_estimate=SHORT,
        name="iterations",
    )(*args)


def apply_kernel(steps, spread, places, seats, number_of, *refs):
    tables = refs[: number_of[0]]
    rows_in = refs[number_of[0] : sum(number_of)]
    weight_ref = refs[sum(number_of)]
    update_out, weight_out, mat_ref, update_ref, new_ref, leaving = refs[-6:]
    groups, rows_block = seats
    here = place_of(groups)
    dp = lax.axis_index("dp").astype(i32)
    capacity = weight_ref.shape[1]
    head_rows = NOPE + VDIM
    rms_scale = 0.2 * math.sqrt(max(KV_ROWS, KV_RANK))
    lane = lax.broadcasted_iota(i32, (1, LANES), 1)
    head_shift = head_rows.bit_length() - 1
    assert head_rows == 1 << head_shift and capacity % (16 * CHUNKS) == 0
    rows_of_slots = -(-capacity // LANES)
    slot = lax.broadcasted_iota(i32, (rows_of_slots, LANES), 0) * LANES
    slot = slot + lax.broadcasted_iota(i32, (rows_of_slots, LANES), 1)
    copies = []
    for step, pick in enumerate(steps):
        layer = layer_of(here, *pick)
        (place_a, start_a), (place_b, start_b) = spread[step]
        aux = tables[place_a][start_a : start_a + AUX_P, :].astype(f32)
        diagonal = [aux[i : i + 1] + aux[4 + i : 5 + i] + aux[8 + i : 9 + i] for i in range(BLOCKS)]
        inverse = [1.0 / line for line in diagonal]
        norm = (aux[15:16] + aux[16:17] + aux[17:18]) * rms_scale
        factor = jnp.sqrt(jnp.minimum(1.0, clip_limit / aux[12:13]))
        tallies = aux[13:14] + aux[14:15]

        def store(i, j, block):
            block = (block * inverse[j]).astype(bf16)
            mat_ref[step, i * LANES : (i + 1) * LANES, j * LANES : (j + 1) * LANES] = block

        for which, (place, start) in enumerate(((place_a, start_a + AUX_P), (place_b, start_b))):
            blocks = [
                tables[place][start + k * LANES : start + (k + 1) * LANES, :].astype(f32) for k in range(4)
            ]
            unpack_symmetric(which, blocks, lambda g: diagonal[g], store)
        lowest = dp * groups
        earlier = jnp.where((lane >= lowest) & (lane < here[2]), tallies, 0.0)
        base = jnp.sum(earlier, axis=1, keepdims=True).astype(i32) + dp * rows_block
        first_head = base >> head_shift
        row_index = base + slot
        head_of = row_index >> head_shift
        scale = jnp.ones(slot.shape, f32)
        for k in range((capacity - 1) // head_rows + 2):
            one = jnp.sum(jnp.where(lane == first_head + k, factor, 0.0), axis=1, keepdims=True)
            scale = jnp.where(head_of == first_head + k, one, scale)
        scale = jnp.where((row_index & (head_rows - 1)) < NOPE, scale, 1.0)
        count = jnp.sum(jnp.where(lane == here[2], tallies, 0.0), axis=1, keepdims=True).astype(i32)
        scale = jnp.where(slot < count, scale, 0.0)
        columns = [jnp.broadcast_to(scale[k : k + 1], (LANES, LANES)).T for k in range(slot.shape[0])]
        scale = jnp.concatenate(columns, axis=0)[:capacity]
        kept = scale * (1.0 - learn_rate * decay_rate)
        moved = scale * learn_rate
        source, index = places[step]
        if isinstance(index, tuple):
            core = here[1] if pick[1] else 1 - here[1]
            index = jnp.where(core == 0, index[0], index[1])
        for chunk in range(CHUNKS):
            size = capacity // CHUNKS
            among = slice(chunk * size, (chunk + 1) * size)
            product = mm(rows_in[source][index, among, :], mat_ref[step])
            for i in range(BLOCKS):
                span = slice(i * LANES, (i + 1) * LANES)
                update = product[:, span] * (diagonal[i] * norm)
                update_ref[step, among, span] = update.astype(bf16)
                weight = weight_ref[layer, among, span].astype(f32)
                new_ref[step, among, span] = (weight * kept[among] - update * moved[among]).astype(bf16)
            at = pl.ds(chunk * size, size)
            for number, (held, out) in enumerate(((update_ref, update_out), (new_ref, weight_out))):
                copy = pltpu.make_async_copy(
                    held.at[step, at], out.at[layer, at], leaving.at[number, step * CHUNKS + chunk]
                )
                copy.start()
                copies.append(copy)
    for copy in copies:
        copy.wait()


def apply_rows(steps, spread, places, seats, tables, rows, weight, *outs):
    number = len(steps)
    layers, capacity, features = weight.shape
    vmem = pl.BlockSpec(memory_space=pltpu.VMEM)
    hbm = pl.BlockSpec(memory_space=pltpu.HBM)
    args = list(tables) + list(rows) + [weight] + list(outs)
    shape = jax.ShapeDtypeStruct((layers, capacity, features), bf16)
    return pl.pallas_call(
        functools.partial(apply_kernel, steps, spread, places, seats, (len(tables), len(rows))),
        in_specs=[vmem] * (len(tables) + len(rows) + 1) + [hbm] * len(outs),
        out_specs=[hbm, hbm],
        out_shape=[shape, shape],
        scratch_shapes=[
            pltpu.VMEM((number, KV_RANK, KV_RANK), bf16),
            pltpu.VMEM((number, capacity, features), bf16),
            pltpu.VMEM((number, capacity, features), bf16),
            pltpu.SemaphoreType.DMA((2, number * CHUNKS)),
        ],
        input_output_aliases={len(args) - 2: 0, len(args) - 1: 1} if outs else {},
        compiler_params=params(),
        cost_estimate=SHORT,
        name="apply_rows",
    )(*args)


def local(dp_size, expert_size, grad_rows, momentum_rows, weight_rows, row_counts, logit_peaks):
    layers = grad_rows.shape[1]
    bits = owner_bits(expert_size)
    assert layers == expert_size == 2 << bits and bits >= 2
    assert dp_size == 4 and dp_size * expert_size <= LANES
    sources = (grad_rows[0], momentum_rows[0], row_counts.reshape(layers), logit_peaks[0, 0])

    def over(x, mask):
        everyone = range(dp_size * expert_size)
        return lax.ppermute(x, ("dp", "expert"), [(i, i ^ mask) for i in everyone])

    across_core = 1
    owner_masks = [2 << p for p in range(bits - 1)] + [2 * expert_size]
    copy_masks = [expert_size, expert_size // 2]

    def mask_of(relative):
        return sum(mask for p, mask in enumerate(owner_masks) if relative >> p & 1)

    def by_core(x, even, odd):
        everyone = range(dp_size * expert_size)
        return lax.ppermute(x, ("dp", "expert"), [(i, i ^ (odd if i & 1 else even)) for i in everyone])

    most = (1 << bits) - 1
    others = list(range(most - 1, 0, -1))
    turns = [
        [(most, False)],
        [(most, True)] + [(r, False) for r in others],
        [(r, True) for r in others],
        [(0, False), (0, True)],
    ]
    rows, partial, messages = {}, {}, []
    facts, loaded = None, ()
    message_shape = jax.ShapeDtypeStruct((1, 2 * HALF_CODE, LANES), i16)
    for number, turn in enumerate(turns):
        later = turns[number + 1] if number + 1 < len(turns) else []
        if messages and not later:
            loaded, messages[0] = lax.optimization_barrier((loaded, messages[0]))
        facts, made, grams, loaded = gram_parts(expert_size, turn, later, sources, facts, loaded)
        for index, (pick, gram) in enumerate(zip(turn, grams)):
            rows[pick] = (made, index)
            partial[pick] = gram if pick[1] else [over(half, across_core) for half in gram]
        ready = ([], [most], others, [])[number]
        if ready:
            sums = [half for r in ready for half in partial[r, True] + partial[r, False]]
            kernel = functools.partial(send_kernel, len(ready))
            made = local_call(kernel, [message_shape] * len(ready), "send", *sums)
            made, loaded = lax.optimization_barrier((made, loaded))
            messages += [over(message, mask_of(r)) for r, message in zip(ready, made)]
    codes = jax.ShapeDtypeStruct((1, HALF_CODE, LANES), i16)
    shapes = [codes, codes, jax.ShapeDtypeStruct((1, 2 * HALF, LANES), f32)]
    out = local_call(gather_kernel, shapes, "gather", *partial[0, True], *partial[0, False], *messages)
    state = [out[2], over(out[0], copy_masks[0]), over(out[1], copy_masks[1])]
    out = local_call(sum_kernel, shapes, "sum", *state)
    state = [out[2], over(out[0], copy_masks[1]), over(out[1], copy_masks[0])]
    table = iterations(*state)

    seats = (expert_size, KV_ROWS // dp_size)
    weight = weight_rows[0]
    full = lambda place: ((place, 0), (place, HEAD_P))

    def apply(picks, tables, *outs):
        arrays, places = [], []
        for relative, own_core in picks:
            found = [rows[r, own_core] for r in (relative if isinstance(relative, tuple) else (relative,))]
            if not any(array is found[0][0] for array in arrays):
                arrays.append(found[0][0])
            (source,) = [k for k, array in enumerate(arrays) if array is found[0][0]]
            assert all(made is arrays[source] for made, _ in found)
            indices = tuple(index for _, index in found)
            places.append((source, indices if len(indices) > 1 else indices[0]))
        spread = tuple(full(k) for k in range(len(tables)))
        return apply_rows(tuple(picks), spread, places, seats, tables, arrays, weight, *outs)

    if bits == 2:
        first = by_core(table, owner_masks[1], owner_masks[0])
        second = by_core(table, owner_masks[0], owner_masks[1])
        table, first, second = lax.optimization_barrier((table, first, second))
        last = by_core(second, owner_masks[1], owner_masks[0])
        known, relatives = [table, first, second], [0, (2, 1), (1, 2)]
        outs = apply([(r, True) for r in relatives], known)
        outs = apply([(r, False) for r in relatives], [over(x, across_core) for x in known], *outs)
        last, outs = lax.optimization_barrier((last, outs))
        outs = apply(((3, True), (3, False)), [last, over(last, across_core)], *outs)
    else:
        outs = apply(((0, True), (0, False)), [table, over(table, across_core)])
        tables = {0: table}
        for position in range(bits - 1, -1, -1):
            for known in list(tables):
                tables[known | 1 << position] = over(tables[known], owner_masks[position])
        for relative in range(1, 1 << bits):
            pair = [tables[relative], over(tables[relative], across_core)]
            outs = apply(((relative, True), (relative, False)), pair, *outs)
    return (outs[0][None], outs[1][None])


def solution(mesh):
    return jax.shard_map(
        functools.partial(local, mesh.shape["dp"], mesh.shape["expert"]),
        mesh=mesh,
        in_specs=(
            P("dp", None, "expert", None),
            P("dp", None, "expert", None),
            P("dp", None, "expert", None),
            P("dp", None, "expert"),
            P("dp", "expert", None, None),
        ),
        out_specs=(P("dp", None, "expert", None), P("dp", None, "expert", None)),
        check_vma=False,
    )
```

time: 78.6 us -> 76.6 us (0.975)
  Pallas kernels: 35 us -> 31.3 us
  waiting for transfers between devices: 24.4 us -> 27.8 us
  starting transfers between devices: 17.9 us -> 16.4 us
    ppermute x20 -> x22, waiting for transfers between devices: 24.4 us -> 27.8 us  [the longest x19 22.5 us: over(): return lax.ppermute(x, ('dp', 'expert'), [(i, i ^ mask) for i in everyone])]
    pallas_call x3 -> x4, Pallas kernels: 12.5 us -> 10.4 us  [gram_parts(): pl.pallas_call(functools.partial(gram_kernel, expert_size, picks, later,...]
    pallas_call x3, Pallas kernels: 9.46 us -> 7.84 us  [apply_rows(): pl.pallas_call(functools.partial(apply_kernel, steps, spread, places, sea...]
    ppermute x20 -> x22, starting transfers between devices: 17.9 us -> 16.4 us  [the longest x19 13 us: over(): return lax.ppermute(x, ('dp', 'expert'), [(i, i ^ mask) for i in everyone])]
  transfers between devices with their start and end apart: 20 -> 22, of which waited for: 13 -> 8; matrix products, arithmetic and copies ran while one was open for 0% -> 0% of each run, Pallas kernels for 19% -> 17%
where the time goes in v4:
time: 76.6 us; the launch traced here: 76.5 us
  Pallas kernels  31.3 us (41%)
  waiting for transfers between devices  27.8 us (36%)
  starting transfers between devices  16.4 us (21%)
  between operations  0.99 us (1%)
    ppermute x19, waiting for transfers between devices, over(): return lax.ppermute(x, ('dp', 'expert'), [(i, i ^ mask) for i in everyone])  22.5 us
    ppermute x19, starting transfers between devices, over(): return lax.ppermute(x, ('dp', 'expert'), [(i, i ^ mask) for i in everyone])  13 us
    pallas_call x1, Pallas kernels, iterations(): pl.pallas_call(iterate_kernel, in_specs=[pl.BlockSpec(memory_space=pltpu....  11.3 us
    pallas_call x4, Pallas kernels, gram_parts(): pl.pallas_call(functools.partial(gram_kernel, expert_size, picks, later,...  10.4 us
    pallas_call x3, Pallas kernels, apply_rows(): pl.pallas_call(functools.partial(apply_kernel, steps, spread, places, sea...  7.84 us
    ppermute x3, waiting for transfers between devices, by_core(): lax.ppermute(x, ('dp', 'expert'), [(i, i ^ (odd if i & 1 else even)) for...  5.23 us
    ppermute x3, starting transfers between devices, by_core(): lax.ppermute(x, ('dp', 'expert'), [(i, i ^ (odd if i & 1 else even)) for...  3.41 us
    pallas_call x4, Pallas kernels, local_call(): pl.pallas_call(kernel, in_specs=[pl.BlockSpec(memory_space=pltpu.VMEM)] *...  1.73 us
  transfers between devices with their start and end apart: 22, of which 8 were waited for; matrix products, arithmetic and copies ran while one was open for 0% of the time, Pallas kernels for 17%

profile of v4, /device:TPU:0, one launch (start us, length us, event | category | flops | bytes accessed | tf_op | source)
XLA Modules:
  0.0 76.5 jit_solution(14652557888660402063)
XLA Ops:
  0.6 3.1 %gram_parts.4 = (f32[8,8,128]{2,1,0:T(8,128)S(1)}, bf16[1,640,512]{2,1,0:T(8,128)(2,1)S(1)}, f32[1,520,128]{2,1,0:T(8,128)S(1)}, f32[1,520,128]{2,1,0:T(8,128)S(...) custom-call(bf16[8,640,512]{2,1,0:T(8,128)(2,1)} %bitcast.12, bf16[8,640,512]{2,1,0:T(8,128)(2,1)} %bitcast.16, ...), custom_call_target="tpu_custom_call" | custom-call | flops 1000 | bytes 1000 | tf_op jit(solution)/shard_map/gram_parts/pallas_call | solution.py:192
  4.4 3.2 %gram_parts.5 = (bf16[3,640,512]{2,1,0:T(8,128)(2,1)S(1)}, f32[1,520,128]{2,1,0:T(8,128)S(1)}, f32[1,520,128]{2,1,0:T(8,128)S(1)}, f32[1,520,128]{2,1,0:T(8,128)...) custom-call(bf16[8,640,512]{2,1,0:T(8,128)(2,1)} %bitcast.13, ...), custom_call_target="tpu_custom_call" | custom-call | flops 1000 | bytes 1000 | tf_op jit(solution)/shard_map/gram_parts/pallas_call | solution.py:192
  9.0 4.0 %collective-permute-start.6 = (s16[1,1056,128]{2,1,0:T(8,128)(2,1)S(1)}, s16[1,1056,128]{2,1,0:T(8,128)(2,1)S(1)}, u32[]{:S(2)}, u32[]{:S(2)}) collective-permute-start(s16[1,1056,128]{2,1,0:T(8,128)(2,1)S(1)} %send.2), channel_id=1, source_target_pairs={{0,18},{1,19},{2,16},{3,17},{4,22},{5,23},{6,20},{7,21},{8,26},{9,... | collective-permute-start | bytes 811016 | tf_op jit(solution)/shard_map/ppermute | solution.py:539
  13.0 2.8 %gram_parts.6 = (bf16[2,640,512]{2,1,0:T(8,128)(2,1)S(1)}, f32[1,520,128]{2,1,0:T(8,128)S(1)}, f32[1,520,128]{2,1,0:T(8,128)S(1)}, f32[1,520,128]{2,1,0:T(8,128)...) custom-call(bf16[8,640,512]{2,1,0:T(8,128)(2,1)} %bitcast.14, ...), custom_call_target="tpu_custom_call" | custom-call | flops 1000 | bytes 1000 | tf_op jit(solution)/shard_map/gram_parts/pallas_call | solution.py:192
  16.3 0.6 collective-permute-start.9
  17.0 2.9 %collective-permute-done.6.refs_4_ = s16[1,1056,128]{2,1,0:T(8,128)(2,1)S(1)} collective-permute-done((s16[1,1056,128]{2,1,0:T(8,128)(2,1)S(1)}, s16[1,1056,128]{2,1,0:T(8,128)(2,1)S(1)}, u32[]{:S(2)}, u32[]{:S(2)}) %collective-permute-start.6) | collective-permute-done | bytes 270368 | tf_op jit(solution)/shard_map/ppermute | solution.py:539
  19.9 1.3 %gram_parts.7 = (bf16[2,640,512]{2,1,0:T(8,128)(2,1)S(1)}, f32[1,520,128]{2,1,0:T(8,128)S(1)}, f32[1,520,128]{2,1,0:T(8,128)S(1)}, f32[1,520,128]{2,1,0:T(8,128)S(1)}, f32[1,520,128]{2,1,0:T(8,128)S(1)}) custom-call(bf16[8,640,512]{2,1,0:T(8,128)(2,1)} %bitcast.15, bf16[8,640,512]{2,1,0:T(8,128)(2,1)} %bitcast.19, ...), custom_call_target="tpu_custom_call" | custom-call | flops 1000 | bytes 1000 | tf_op jit(solution)/shard_map/gram_parts/pallas_call | solution.py:192
  21.7 3.8 %collective-permute-done.9.refs_5_ = s16[1,1056,128]{2,1,0:T(8,128)(2,1)S(1)} collective-permute-done((s16[1,1056,128]{2,1,0:T(8,128)(2,1)S(1)}, s16[1,1056,128]{2,1,0:T(8,128)(2,1)S(1)}, u32[]{:S(2)}, u32[]{:S(2)}) %collective-permute-start.9) | collective-permute-done | bytes 270368 | tf_op jit(solution)/shard_map/ppermute | solution.py:539
  25.7 0.6 gather.1
  26.3 1.6 %collective-permute-start.11 = (s16[1,528,128]{2,1,0:T(8,128)(2,1)S(1)}, s16[1,528,128]{2,1,0:T(8,128)(2,1)S(1)}, u32[]{:S(2)}, u32[]{:S(2)}) collective-permute-start(s16[1,528,128]{2,1,0:T(8,128)(2,1)S(1)} %get-tuple-element.95), channel_id=1, source_target_pairs={{0,8},{1,9},{2,10},{3,11},{4,12},{5,13},{6,14},{7,15},{8,0},{9,1},... | collective-permute-start | bytes 405512 | tf_op jit(solution)/shard_map/ppermute | solution.py:539
  27.8 2.6 %collective-permute-start.12 = (s16[1,528,128]{2,1,0:T(8,128)(2,1)S(1)}, s16[1,528,128]{2,1,0:T(8,128)(2,1)S(1)}, u32[]{:S(2)}, u32[]{:S(2)}) collective-permute-start(s16[1,528,128]{2,1,0:T(8,128)(2,1)S(1)} %get-tuple-element.96), channel_id=1, source_target_pairs={{0,4},{1,5},{2,6},{3,7},{4,0},{5,1},{6,2},{7,3},{8,12},{9,13},{10,... | collective-permute-start | bytes 405512 | tf_op jit(solution)/shard_map/ppermute | solution.py:539
  30.4 1.1 %collective-permute-done.11.arrived_a = s16[1,528,128]{2,1,0:T(8,128)(2,1)S(1)} collective-permute-done((s16[1,528,128]{2,1,0:T(8,128)(2,1)S(1)}, s16[1,528,128]{2,1,0:T(8,128)(2,1)S(1)}, u32[]{:S(2)}, u32[]{:S(2)}) %collective-permute-start.11) | collective-permute-done | bytes 135200 | tf_op jit(solution)/shard_map/ppermute | solution.py:539
  31.6 5.2 %collective-permute-done.12.arrived_b = s16[1,528,128]{2,1,0:T(8,128)(2,1)S(1)} collective-permute-done((s16[1,528,128]{2,1,0:T(8,128)(2,1)S(1)}, s16[1,528,128]{2,1,0:T(8,128)(2,1)S(1)}, u32[]{:S(2)}, u32[]{:S(2)}) %collective-permute-start.12) | collective-permute-done | bytes 135200 | tf_op jit(solution)/shard_map/ppermute | solution.py:539
  37.8 8.1 %collective-permute-done.13.arrived_a = s16[1,528,128]{2,1,0:T(8,128)(2,1)S(1)} collective-permute-done((s16[1,528,128]{2,1,0:T(8,128)(2,1)S(1)}, s16[1,528,128]{2,1,0:T(8,128)(2,1)S(1)}, u32[]{:S(2)}, u32[]{:S(2)}) %collective-permute-start.13) | collective-permute-done | bytes 135200 | tf_op jit(solution)/shard_map/ppermute | solution.py:539
  45.9 11.3 %iterations.1.refs_0_ = bf16[1056,128]{1,0:T(8,128)(2,1)S(1)} custom-call(f32[1,1040,128]{2,1,0:T(8,128)S(1)} %get-tuple-element.97.kept, s16[1,528,128]{2,1,0:T(8,128)(2,1)S(1)} %collective-permute-done.13.arrived_a, s16[1,528,128]{2,1,0:T(8,128)(2,1)S(1)} %collective-permute-done.14.arrived_b), custom_call_target="tpu_custom_call" | custom-call | flops 1000 | bytes 1000 | tf_op jit(solution)/shard_map/iterations/pallas_call | solution.py:414
  57.3 0.6 collective-permute-start.16
  57.9 1.5 %collective-permute-start.15 = (bf16[1056,128]{1,0:T(8,128)(2,1)S(1)}, bf16[1056,128]{1,0:T(8,128)(2,1)S(1)}, u32[]{:S(2)}, u32[]{:S(2)}) collective-permute-start(bf16[1056,128]{1,0:T(8,128)(2,1)S(1)} %iterations.1.refs_0_), channel_id=1, source_target_pairs={{0,16},{1,3},{2,18},{3,1},{4,20},{5,7},{6,22},{7,5},{8,24},{9,11},... | collective-permute-start | bytes 811016 | tf_op jit(solution)/shard_map/ppermute | solution.py:550
  59.4 5.2 %collective-permute-done.16.refs_2_ = bf16[1056,128]{1,0:T(8,128)(2,1)S(1)} collective-permute-done((bf16[1056,128]{1,0:T(8,128)(2,1)S(1)}, bf16[1056,128]{1,0:T(8,128)(2,1)S(1)}, u32[]{:S(2)}, u32[]{:S(2)}) %collective-permute-start.16) | collective-permute-done | bytes 270368 | tf_op jit(solution)/shard_map/ppermute | solution.py:550
  65.2 1.2 %collective-permute-start.17 = (bf16[1056,128]{1,0:T(8,128)(2,1)S(1)}, bf16[1056,128]{1,0:T(8,128)(2,1)S(1)}, u32[]{:S(2)}, u32[]{:S(2)}) collective-permute-start(bf16[1056,128]{1,0:T(8,128)(2,1)S(1)} %collective-permute-done.16.refs_2_), channel_id=1, source_target_pairs={{0,16},{1,3},{2,18},{3,1},{4,20},{5,7},{6,22},{7,5},{8,24},{9,11},... | collective-permute-start | bytes 811016 | tf_op jit(solution)/shard_map/ppermute | solution.py:550
  66.4 2.8 %apply_rows.3 = (bf16[8,640,512]{2,1,0:T(8,128)(2,1)}, bf16[8,640,512]{2,1,0:T(8,128)(2,1)}) custom-call(bf16[1056,128]{1,0:T(8,128)(2,1)S(1)} %iterations.1.refs_0_, bf16[1056,128]{1,0:T(8,128)(2,1)S(1)} %collective-permute-done.15.refs_1_, bf16[1056,128]{1,0:T(8,128)(2,1)S(1)} %collective-permute-done.16.refs_2_, ...), custom_call_target="tpu_custom_call" | custom-call | flops 1000 | bytes 1000 | tf_op jit(solution)/shard_map/apply_rows/pallas_call | solution.py:512
  69.3 2.8 %apply_rows.4 = (bf16[8,640,512]{2,1,0:T(8,128)(2,1)}, bf16[8,640,512]{2,1,0:T(8,128)(2,1)}) custom-call(bf16[1056,128]{1,0:T(8,128)(2,1)S(1)} %collective-permute-done.18.refs_0_, bf16[1056,128]{1,0:T(8,128)(2,1)S(1)} %collective-permute-done.19.refs_1_, ...), custom_call_target="tpu_custom_call", output_to_operand_aliasing={{0}: (6, {}), {1}: (7, {})} | custom-call | flops 1000 | bytes 1000 | tf_op jit(solution)/shard_map/apply_rows/pallas_call | solution.py:512
  72.2 0.8 %collective-permute-start.21 = (bf16[1056,128]{1,0:T(8,128)(2,1)S(1)}, bf16[1056,128]{1,0:T(8,128)(2,1)S(1)}, u32[]{:S(2)}, u32[]{:S(2)}) collective-permute-start(bf16[1056,128]{1,0:T(8,128)(2,1)S(1)} %collective-permute-done.17.refs_0_), channel_id=1, source_target_pairs={{0,1},{1,0},{2,3},{3,2},{4,5},{5,4},{6,7},{7,6},{8,9},{9,8},{10,11... | collective-permute-start | bytes 811016 | tf_op jit(solution)/shard_map/ppermute | solution.py:539
  73.0 1.2 %collective-permute-done.21.refs_1_ = bf16[1056,128]{1,0:T(8,128)(2,1)S(1)} collective-permute-done((bf16[1056,128]{1,0:T(8,128)(2,1)S(1)}, bf16[1056,128]{1,0:T(8,128)(2,1)S(1)}, u32[]{:S(2)}, u32[]{:S(2)}) %collective-permute-start.21) | collective-permute-done | bytes 270368 | tf_op jit(solution)/shard_map/ppermute | solution.py:539
  74.1 2.2 %apply_rows.5 = (bf16[8,640,512]{2,1,0:T(8,128)(2,1)}, bf16[8,640,512]{2,1,0:T(8,128)(2,1)}) custom-call(bf16[1056,128]{1,0:T(8,128)(2,1)S(1)} %collective-permute-done.17.refs_0_, bf16[1056,128]{1,0:T(8,128)(2,1)S(1)} %collective-permute-done.21.refs_1_, ...), custom_call_target="tpu_custom_call", output_to_operand_aliasing={{0}: (5, {}), {1}: (6, {})} | custom-call | flops 1000 | bytes 1000 | tf_op jit(solution)/shard_map/apply_rows/pallas_call | solution.py:512
  (37 shorter events, 4.8 us)
Async XLA Ops:
  3.8 4.8 %collective-permute-start = (f32[1,520,128]{2,1,0:T(8,128)S(1)}, f32[1,520,128]{2,1,0:T(8,128)S(1)}, u32[]{:S(2)}, u32[]{:S(2)}) collective-permute-start(f32[1,520,128]{2,1,0:T(8,128)S(1)} %get-tuple-element.64), channel_id=1, source_target_pairs={{0,1},{1,0},{2,3},{3,2},{4,5},{5,4},{6,7},{7,6},{8,9},{9,8},{10,11... | collective-permute-start | bytes 798728 | tf_op jit(solution)/shard_map/ppermute | solution.py:539
  4.3 4.4 %collective-permute-start.1 = (f32[1,520,128]{2,1,0:T(8,128)S(1)}, f32[1,520,128]{2,1,0:T(8,128)S(1)}, u32[]{:S(2)}, u32[]{:S(2)}) collective-permute-start(f32[1,520,128]{2,1,0:T(8,128)S(1)} %get-tuple-element.65), channel_id=1, source_target_pairs={{0,1},{1,0},{2,3},{3,2},{4,5},{5,4},{6,7},{7,6},{8,9},{9,8},{10,11... | collective-permute-start | bytes 798728 | tf_op jit(solution)/shard_map/ppermute | solution.py:539
  7.6 8.2 %collective-permute-start.2 = (f32[1,520,128]{2,1,0:T(8,128)S(1)}, f32[1,520,128]{2,1,0:T(8,128)S(1)}, u32[]{:S(2)}, u32[]{:S(2)}) collective-permute-start(f32[1,520,128]{2,1,0:T(8,128)S(1)} %get-tuple-element.72), channel_id=1, source_target_pairs={{0,1},{1,0},{2,3},{3,2},{4,5},{5,4},{6,7},{7,6},{8,9},{9,8},{10,11... | collective-permute-start | bytes 798728 | tf_op jit(solution)/shard_map/ppermute | solution.py:539
  8.1 7.7 %collective-permute-start.3 = (f32[1,520,128]{2,1,0:T(8,128)S(1)}, f32[1,520,128]{2,1,0:T(8,128)S(1)}, u32[]{:S(2)}, u32[]{:S(2)}) collective-permute-start(f32[1,520,128]{2,1,0:T(8,128)S(1)} %get-tuple-element.73), channel_id=1, source_target_pairs={{0,1},{1,0},{2,3},{3,2},{4,5},{5,4},{6,7},{7,6},{8,9},{9,8},{10,11... | collective-permute-start | bytes 798728 | tf_op jit(solution)/shard_map/ppermute | solution.py:539
  8.1 7.6 %collective-permute-start.4 = (f32[1,520,128]{2,1,0:T(8,128)S(1)}, f32[1,520,128]{2,1,0:T(8,128)S(1)}, u32[]{:S(2)}, u32[]{:S(2)}) collective-permute-start(f32[1,520,128]{2,1,0:T(8,128)S(1)} %get-tuple-element.76), channel_id=1, source_target_pairs={{0,1},{1,0},{2,3},{3,2},{4,5},{5,4},{6,7},{7,6},{8,9},{9,8},{10,11... | collective-permute-start | bytes 798728 | tf_op jit(solution)/shard_map/ppermute | solution.py:539
  8.6 7.2 %collective-permute-start.5 = (f32[1,520,128]{2,1,0:T(8,128)S(1)}, f32[1,520,128]{2,1,0:T(8,128)S(1)}, u32[]{:S(2)}, u32[]{:S(2)}) collective-permute-start(f32[1,520,128]{2,1,0:T(8,128)S(1)} %get-tuple-element.77), channel_id=1, source_target_pairs={{0,1},{1,0},{2,3},{3,2},{4,5},{5,4},{6,7},{7,6},{8,9},{9,8},{10,11... | collective-permute-start | bytes 798728 | tf_op jit(solution)/shard_map/ppermute | solution.py:539
  9.0 10.9 %collective-permute-start.6 = (s16[1,1056,128]{2,1,0:T(8,128)(2,1)S(1)}, s16[1,1056,128]{2,1,0:T(8,128)(2,1)S(1)}, u32[]{:S(2)}, u32[]{:S(2)}) collective-permute-start(s16[1,1056,128]{2,1,0:T(8,128)(2,1)S(1)} %send.2), channel_id=1, source_target_pairs={{0,18},{1,19},{2,16},{3,17},{4,22},{5,23},{6,20},{7,21},{8,26},{9,... | collective-permute-start | bytes 811016 | tf_op jit(solution)/shard_map/ppermute | solution.py:539
  16.3 50.1 %slice-start = ((s8[5242880]{0:T(1024)(128)(4,1)}), s8[4194304]{0:T(1024)(128)(4,1)S(1)}, s32[]{:S(2)}) async-start(s8[5242880]{0:T(1024)(128)(4,1)} %bitcast.7), calls=%async_computation | async-start | bytes 8388608
  16.3 50.1 %slice-start.1 = ((s8[5242880]{0:T(1024)(128)(4,1)}), s8[1048576]{0:T(1024)(128)(4,1)S(1)}, s32[]{:S(2)}) async-start(s8[5242880]{0:T(1024)(128)(4,1)} %bitcast.7), calls=%async_computation.1 | async-start | bytes 2097152
  16.3 9.2 %collective-permute-start.9 = (s16[1,1056,128]{2,1,0:T(8,128)(2,1)S(1)}, s16[1,1056,128]{2,1,0:T(8,128)(2,1)S(1)}, u32[]{:S(2)}, u32[]{:S(2)}) collective-permute-start(s16[1,1056,128]{2,1,0:T(8,128)(2,1)S(1)} %get-tuple-element.92), channel_id=1, source_target_pairs={{0,16},{1,17},{2,18},{3,19},{4,20},{5,21},{6,22},{7,23},{8,24},{9,... | collective-permute-start | bytes 811016 | tf_op jit(solution)/shard_map/ppermute | solution.py:539
  16.9 8.8 %collective-permute-start.10 = (s16[1,1056,128]{2,1,0:T(8,128)(2,1)S(1)}, s16[1,1056,128]{2,1,0:T(8,128)(2,1)S(1)}, u32[]{:S(2)}, u32[]{:S(2)}) collective-permute-start(s16[1,1056,128]{2,1,0:T(8,128)(2,1)S(1)} %get-tuple-element.93), channel_id=1, source_target_pairs={{0,2},{1,3},{2,0},{3,1},{4,6},{5,7},{6,4},{7,5},{8,10},{9,11},{10,... | collective-permute-start | bytes 811016 | tf_op jit(solution)/shard_map/ppermute | solution.py:539
  21.2 4.5 %collective-permute-start.7 = (f32[1,520,128]{2,1,0:T(8,128)S(1)}, f32[1,520,128]{2,1,0:T(8,128)S(1)}, u32[]{:S(2)}, u32[]{:S(2)}) collective-permute-start(f32[1,520,128]{2,1,0:T(8,128)S(1)} %get-tuple-element.89), channel_id=1, source_target_pairs={{0,1},{1,0},{2,3},{3,2},{4,5},{5,4},{6,7},{7,6},{8,9},{9,8},{10,11... | collective-permute-start | bytes 798728 | tf_op jit(solution)/shard_map/ppermute | solution.py:539
  21.2 4.4 %collective-permute-start.8 = (f32[1,520,128]{2,1,0:T(8,128)S(1)}, f32[1,520,128]{2,1,0:T(8,128)S(1)}, u32[]{:S(2)}, u32[]{:S(2)}) collective-permute-start(f32[1,520,128]{2,1,0:T(8,128)S(1)} %get-tuple-element.90), channel_id=1, source_target_pairs={{0,1},{1,0},{2,3},{3,2},{4,5},{5,4},{6,7},{7,6},{8,9},{9,8},{10,11... | collective-permute-start | bytes 798728 | tf_op jit(solution)/shard_map/ppermute | solution.py:539
  26.3 5.3 %collective-permute-start.11 = (s16[1,528,128]{2,1,0:T(8,128)(2,1)S(1)}, s16[1,528,128]{2,1,0:T(8,128)(2,1)S(1)}, u32[]{:S(2)}, u32[]{:S(2)}) collective-permute-start(s16[1,528,128]{2,1,0:T(8,128)(2,1)S(1)} %get-tuple-element.95), channel_id=1, source_target_pairs={{0,8},{1,9},{2,10},{3,11},{4,12},{5,13},{6,14},{7,15},{8,0},{9,1},... | collective-permute-start | bytes 405512 | tf_op jit(solution)/shard_map/ppermute | solution.py:539
  27.8 8.9 %collective-permute-start.12 = (s16[1,528,128]{2,1,0:T(8,128)(2,1)S(1)}, s16[1,528,128]{2,1,0:T(8,128)(2,1)S(1)}, u32[]{:S(2)}, u32[]{:S(2)}) collective-permute-start(s16[1,528,128]{2,1,0:T(8,128)(2,1)S(1)} %get-tuple-element.96), channel_id=1, source_target_pairs={{0,4},{1,5},{2,6},{3,7},{4,0},{5,1},{6,2},{7,3},{8,12},{9,13},{10,... | collective-permute-start | bytes 405512 | tf_op jit(solution)/shard_map/ppermute | solution.py:539
  37.2 8.8 %collective-permute-start.13 = (s16[1,528,128]{2,1,0:T(8,128)(2,1)S(1)}, s16[1,528,128]{2,1,0:T(8,128)(2,1)S(1)}, u32[]{:S(2)}, u32[]{:S(2)}) collective-permute-start(s16[1,528,128]{2,1,0:T(8,128)(2,1)S(1)} %get-tuple-element.98), channel_id=1, source_target_pairs={{0,4},{1,5},{2,6},{3,7},{4,0},{5,1},{6,2},{7,3},{8,12},{9,13},{10,... | collective-permute-start | bytes 405512 | tf_op jit(solution)/shard_map/ppermute | solution.py:539
  37.2 8.7 %collective-permute-start.14 = (s16[1,528,128]{2,1,0:T(8,128)(2,1)S(1)}, s16[1,528,128]{2,1,0:T(8,128)(2,1)S(1)}, u32[]{:S(2)}, u32[]{:S(2)}) collective-permute-start(s16[1,528,128]{2,1,0:T(8,128)(2,1)S(1)} %get-tuple-element.99), channel_id=1, source_target_pairs={{0,8},{1,9},{2,10},{3,11},{4,12},{5,13},{6,14},{7,15},{8,0},{9,1},... | collective-permute-start | bytes 405512 | tf_op jit(solution)/shard_map/ppermute | solution.py:539
  57.3 7.4 %collective-permute-start.16 = (bf16[1056,128]{1,0:T(8,128)(2,1)S(1)}, bf16[1056,128]{1,0:T(8,128)(2,1)S(1)}, u32[]{:S(2)}, u32[]{:S(2)}) collective-permute-start(bf16[1056,128]{1,0:T(8,128)(2,1)S(1)} %iterations.1.refs_0_), channel_id=1, source_target_pairs={{0,2},{1,17},{2,0},{3,19},{4,6},{5,21},{6,4},{7,23},{8,10},{9,25},... | collective-permute-start | bytes 811016 | tf_op jit(solution)/shard_map/ppermute | solution.py:550
  57.9 6.8 %collective-permute-start.15 = (bf16[1056,128]{1,0:T(8,128)(2,1)S(1)}, bf16[1056,128]{1,0:T(8,128)(2,1)S(1)}, u32[]{:S(2)}, u32[]{:S(2)}) collective-permute-start(bf16[1056,128]{1,0:T(8,128)(2,1)S(1)} %iterations.1.refs_0_), channel_id=1, source_target_pairs={{0,16},{1,3},{2,18},{3,1},{4,20},{5,7},{6,22},{7,5},{8,24},{9,11},... | collective-permute-start | bytes 811016 | tf_op jit(solution)/shard_map/ppermute | solution.py:550
  64.7 4.6 %collective-permute-start.18 = (bf16[1056,128]{1,0:T(8,128)(2,1)S(1)}, bf16[1056,128]{1,0:T(8,128)(2,1)S(1)}, u32[]{:S(2)}, u32[]{:S(2)}) collective-permute-start(bf16[1056,128]{1,0:T(8,128)(2,1)S(1)} %iterations.1.refs_0_), channel_id=1, source_target_pairs={{0,1},{1,0},{2,3},{3,2},{4,5},{5,4},{6,7},{7,6},{8,9},{9,8},{10,11... | collective-permute-start | bytes 811016 | tf_op jit(solution)/shard_map/ppermute | solution.py:539
  64.7 4.6 %collective-permute-start.19 = (bf16[1056,128]{1,0:T(8,128)(2,1)S(1)}, bf16[1056,128]{1,0:T(8,128)(2,1)S(1)}, u32[]{:S(2)}, u32[]{:S(2)}) collective-permute-start(bf16[1056,128]{1,0:T(8,128)(2,1)S(1)} %collective-permute-done.15.refs_1_), channel_id=1, source_target_pairs={{0,1},{1,0},{2,3},{3,2},{4,5},{5,4},{6,7},{7,6},{8,9},{9,8},{10,11... | collective-permute-start | bytes 811016 | tf_op jit(solution)/shard_map/ppermute | solution.py:539
  65.2 4.1 %collective-permute-start.20 = (bf16[1056,128]{1,0:T(8,128)(2,1)S(1)}, bf16[1056,128]{1,0:T(8,128)(2,1)S(1)}, u32[]{:S(2)}, u32[]{:S(2)}) collective-permute-start(bf16[1056,128]{1,0:T(8,128)(2,1)S(1)} %collective-permute-done.16.refs_2_), channel_id=1, source_target_pairs={{0,1},{1,0},{2,3},{3,2},{4,5},{5,4},{6,7},{7,6},{8,9},{9,8},{10,11... | collective-permute-start | bytes 811016 | tf_op jit(solution)/shard_map/ppermute | solution.py:539
  65.2 7.0 %collective-permute-start.17 = (bf16[1056,128]{1,0:T(8,128)(2,1)S(1)}, bf16[1056,128]{1,0:T(8,128)(2,1)S(1)}, u32[]{:S(2)}, u32[]{:S(2)}) collective-permute-start(bf16[1056,128]{1,0:T(8,128)(2,1)S(1)} %collective-permute-done.16.refs_2_), channel_id=1, source_target_pairs={{0,16},{1,3},{2,18},{3,1},{4,20},{5,7},{6,22},{7,5},{8,24},{9,11},... | collective-permute-start | bytes 811016 | tf_op jit(solution)/shard_map/ppermute | solution.py:550
  72.2 2.0 %collective-permute-start.21 = (bf16[1056,128]{1,0:T(8,128)(2,1)S(1)}, bf16[1056,128]{1,0:T(8,128)(2,1)S(1)}, u32[]{:S(2)}, u32[]{:S(2)}) collective-permute-start(bf16[1056,128]{1,0:T(8,128)(2,1)S(1)} %collective-permute-done.17.refs_0_), channel_id=1, source_target_pairs={{0,1},{1,0},{2,3},{3,2},{4,5},{5,4},{6,7},{7,6},{8,9},{9,8},{10,11... | collective-permute-start | bytes 811016 | tf_op jit(solution)/shard_map/ppermute | solution.py:539

commit v5 on v4

--- a/solution.py
+++ b/solution.py
@@ -80,20 +80,24 @@
     return 2 * (place[0] ^ relative) + core
 
 
-def gram_kernel(expert_size, picks, later, first, *refs):
-    grad_ref, mom_ref = refs[:2]
+def gram_kernel(expert_size, picks, later, first, loaded, *refs):
+    refs = list(refs)
+    take = lambda n: [refs.pop(0) for _ in range(n)]
+    grad_ref, mom_ref = take(2)
+    if first:
+        counts_ref, peaks_ref = take(2)
+    else:
+        (facts_ref,) = take(1)
+    given = take(2 if loaded else 0)
+    if first:
+        (facts_ref,) = take(1)
+    (nes_ref,) = take(1)
+    gram_refs = take(2 * len(picks))
+    loads = take(2 if later else 0)
+    if first:
+        counts, peaks_buf, small_arrivals = take(3)
+    late_arrivals, own_arrivals, own_grad, own_mom = take(4)
     place = place_of(expert_size)
-    if first:
-        counts_ref, peaks_ref = refs[2:4]
-        counts, peaks_buf, grad_buf, mom_buf, arrivals, own_arrivals, small_arrivals = refs[-7:]
-        outs = refs[4:-7]
-        facts_ref, outs = outs[0], outs[1:]
-    else:
-        facts_ref, grad_buf, mom_buf = refs[2:5]
-        arrivals = refs[-1]
-        outs = refs[5:-1]
-    nes_ref, outs = outs[0], outs[1:]
-    gram_refs, loads = outs[: 2 * len(picks)], outs[2 * len(picks) :]
     layers = [layer_of(place, *pick) for pick in picks]
 
     def copies_of(chosen, buffers, semaphores):
@@ -103,14 +107,14 @@
             for n, (source, buffer) in enumerate(((grad_ref, buffers[0]), (mom_ref, buffers[1])))
         ]
 
-    own_copies = copies_of(layers, (grad_buf, mom_buf), own_arrivals) if first else []
+    own_copies = copies_of(layers[loaded:], (own_grad, own_mom), own_arrivals)
     small = []
     if first:
         small = [
             pltpu.make_async_copy(counts_ref, counts, small_arrivals.at[0]),
             pltpu.make_async_copy(peaks_ref, peaks_buf, small_arrivals.at[1]),
         ]
-    late_copies = copies_of([layer_of(place, *pick) for pick in later], loads, arrivals) if later else []
+    late_copies = copies_of([layer_of(place, *pick) for pick in later], loads, late_arrivals) if later else []
     for copy in small + own_copies + late_copies:
         copy.start()
     row, col = square_iotas()
@@ -130,16 +134,18 @@
             facts_ref[layer] = fact
     width = KV_RANK // 2
     dims = (((0,), (0,)), ((), ()))
-    slot = lax.broadcasted_iota(i32, (grad_buf.shape[1], LANES), 0)
+    slot = lax.broadcasted_iota(i32, (nes_ref.shape[1], LANES), 0)
 
     def form_rows(k):
-        for copy in own_copies[2 * k : 2 * k + 2]:
-            copy.wait()
+        (grad_buf, mom_buf), at = (given, k) if k < loaded else ((own_grad, own_mom), k - loaded)
+        if k >= loaded:
+            for copy in own_copies[2 * at : 2 * at + 2]:
+                copy.wait()
         live = slot < facts_ref[layers[k], 6:7, :].astype(i32)
         for i in range(BLOCKS):
             span = slice(i * LANES, (i + 1) * LANES)
-            gradient = grad_buf[k, :, span].astype(f32)
-            velocity = momentum_coef * mom_buf[k, :, span].astype(f32) + gradient
+            gradient = grad_buf[at, :, span].astype(f32)
+            velocity = momentum_coef * mom_buf[at, :, span].astype(f32) + gradient
             nesterov = gradient + momentum_coef * velocity
             nes_ref[k, :, span] = jnp.where(live, nesterov, 0.0).astype(bf16)
 
@@ -182,16 +188,16 @@
     out_shapes += [rows(len(later))] * 2 if later else []
     args = [pinned(grad), pinned(mom)]
     args += [pinned(counts), pinned(peaks)] if first else [facts] + list(loaded)
+    known = loaded[0].shape[0] if loaded else 0
+    own = max(number - known, 1)
     scratch = []
     if first:
-        scratch += [pltpu.SMEM(counts.shape, i32), pltpu.VMEM(peaks.shape, bf16)]
-        scratch += [pltpu.VMEM((number, capacity, features), bf16)] * 2
-    scratch += [pltpu.SemaphoreType.DMA((2, max(len(later), 1)))]
-    if first:
-        scratch += [pltpu.SemaphoreType.DMA((2, number)), pltpu.SemaphoreType.DMA((2,))]
+        scratch += [pltpu.SMEM(counts.shape, i32), pltpu.VMEM(peaks.shape, bf16), pltpu.SemaphoreType.DMA((2,))]
+    scratch += [pltpu.SemaphoreType.DMA((2, max(len(later), 1))), pltpu.SemaphoreType.DMA((2, own))]
+    scratch += [pltpu.VMEM((own, capacity, features), bf16)] * 2
     out = pl.pallas_call(
-        functools.partial(gram_kernel, expert_size, picks, later, first),
-        in_specs=[hbm] * (4 if first else 2) + [vmem] * (0 if first else 3),
+        functools.partial(gram_kernel, expert_size, picks, later, first, known),
+        in_specs=[hbm] * (4 if first else 2) + [vmem] * (0 if first else 1) + [vmem] * len(loaded),
         out_specs=[vmem] * len(out_shapes),
         out_shape=out_shapes,
         scratch_shapes=scratch,
@@ -357,6 +363,7 @@
     gram = gram_ref[...] * inverse * inverse
     full_row = lax.broadcasted_iota(i32, (KV_RANK, KV_RANK), 0)
     full_col = lax.broadcasted_iota(i32, (KV_RANK, KV_RANK), 1)
+    on_diagonal = full_row == full_col
     product = None
     for repeat in range(NS_ITERS):
         high, low = parts_of(gram)
@@ -366,10 +373,11 @@
             square = mm(high, high)
         mixing = (coef_second * gram + coef_third * square).astype(bf16)
         if product is None:
-            product = jnp.where(full_row == full_col, coef_first, 0.0) + mixing.astype(f32)
+            product = jnp.where(on_diagonal, coef_first, 0.0) + mixing.astype(f32)
         else:
-            product_high, product_low = parts_of(product)
-            product = coef_first * product + mm(wide(product_high, product_low), tall(mixing, mixing))
+            diagonal = jnp.sum(jnp.where(on_diagonal, product, 0.0), axis=0, keepdims=True)
+            rest = jnp.where(on_diagonal, 0.0, product).astype(bf16)
+            product = coef_first * product + (mm(mixing, rest) + mixing.astype(f32) * diagonal)
         if repeat < NS_ITERS - 1:
             half = coef_first * gram + mm(wide(high, low), tall(mixing, mixing))
             half_high, half_low = parts_of(half)
@@ -561,7 +569,7 @@
     facts, loaded = None, ()
     message_shape = jax.ShapeDtypeStruct((1, 2 * HALF_CODE, LANES), i16)
     for number, turn in enumerate(turns):
-        later = turns[number + 1] if number + 1 < len(turns) else []
+        later = turns[number + 1][:2] if number + 1 < len(turns) else []
         if messages and not later:
             loaded, messages[0] = lax.optimization_barrier((loaded, messages[0]))
         facts, made, grams, loaded = gram_parts(expert_size, turn, later, sources, facts, loaded)
@@ -603,13 +611,16 @@
     if bits == 2:
         first = by_core(table, owner_masks[1], owner_masks[0])
         second = by_core(table, owner_masks[0], owner_masks[1])
-        table, first, second = lax.optimization_barrier((table, first, second))
+        outs = apply([(0, True)], [table])
+        table, first, second, outs = lax.optimization_barrier((table, first, second, outs))
         last = by_core(second, owner_masks[1], owner_masks[0])
-        known, relatives = [table, first, second], [0, (2, 1), (1, 2)]
-        outs = apply([(r, True) for r in relatives], known)
-        outs = apply([(r, False) for r in relatives], [over(x, across_core) for x in known], *outs)
+        near = [(2, 1), (1, 2)]
+        outs = apply([(r, True) for r in near], [first, second], *outs)
+        crossed = [over(x, across_core) for x in (table, first, second)]
+        outs = apply([(r, False) for r in [0] + near], crossed, *outs)
         last, outs = lax.optimization_barrier((last, outs))
-        outs = apply(((3, True), (3, False)), [last, over(last, across_core)], *outs)
+        outs = apply([(3, True)], [last], *outs)
+        outs = apply([(3, False)], [over(last, across_core)], *outs)
     else:
         outs = apply(((0, True), (0, False)), [table, over(table, across_core)])
         tables = {0: table}

time: 76.6 us -> 74.4 us (0.971)
  waiting for transfers between devices: 27.8 us -> 24.6 us
    ppermute x19, waiting for transfers between devices: 22.5 us -> 20 us  [over(): return lax.ppermute(x, ('dp', 'expert'), [(i, i ^ mask) for i in everyone])]
    pallas_call x3 -> x5, Pallas kernels: 7.84 us -> 9.94 us  [apply_rows(): pl.pallas_call(functools.partial(apply_kernel, steps, spread, places, sea...]
    pallas_call x1, Pallas kernels: 11.3 us -> 10.1 us  [iterations(): pl.pallas_call(iterate_kernel, in_specs=[pl.BlockSpec(memory_space=pltpu....]
    ppermute x3, starting transfers between devices: 3.41 us -> 4.27 us  [by_core(): lax.ppermute(x, ('dp', 'expert'), [(i, i ^ (odd if i & 1 else even)) for...]
  transfers between devices with their start and end apart: 22 -> 22, of which waited for: 8 -> 8; matrix products, arithmetic and copies ran while one was open for 0% -> 0% of each run, Pallas kernels for 17% -> 21%
where the time goes in v5:
time: 74.4 us; the launch traced here: 74.1 us
  Pallas kernels  31.9 us (43%)
  waiting for transfers between devices  24.6 us (33%)
  starting transfers between devices  16.7 us (22%)
  between operations  1 us (1%)
    ppermute x19, waiting for transfers between devices, over(): return lax.ppermute(x, ('dp', 'expert'), [(i, i ^ mask) for i in everyone])  20 us
    ppermute x19, starting transfers between devices, over(): return lax.ppermute(x, ('dp', 'expert'), [(i, i ^ mask) for i in everyone])  12.4 us
    pallas_call x4, Pallas kernels, gram_parts(): pl.pallas_call(functools.partial(gram_kernel, expert_size, picks, later,...  10.1 us
    pallas_call x1, Pallas kernels, iterations(): pl.pallas_call(iterate_kernel, in_specs=[pl.BlockSpec(memory_space=pltpu....  10.1 us
    pallas_call x5, Pallas kernels, apply_rows(): pl.pallas_call(functools.partial(apply_kernel, steps, spread, places, sea...  9.94 us
    ppermute x3, waiting for transfers between devices, by_core(): lax.ppermute(x, ('dp', 'expert'), [(i, i ^ (odd if i & 1 else even)) for...  4.57 us
    ppermute x3, starting transfers between devices, by_core(): lax.ppermute(x, ('dp', 'expert'), [(i, i ^ (odd if i & 1 else even)) for...  4.27 us
    pallas_call x4, Pallas kernels, local_call(): pl.pallas_call(kernel, in_specs=[pl.BlockSpec(memory_space=pltpu.VMEM)] *...  1.73 us
  transfers between devices with their start and end apart: 22, of which 8 were waited for; matrix products, arithmetic and copies ran while one was open for 0% of the time, Pallas kernels for 21%

profile of v5, /device:TPU:0, one launch (start us, length us, event | category | flops | bytes accessed | tf_op | source)
XLA Modules:
  0.0 74.1 jit_solution(9489395424251036570)
XLA Ops:
  0.6 2.7 %gram_parts.4 = (f32[8,8,128]{2,1,0:T(8,128)S(1)}, bf16[1,640,512]{2,1,0:T(8,128)(2,1)S(1)}, f32[1,520,128]{2,1,0:T(8,128)S(1)}, f32[1,520,128]{2,1,0:T(8,128)S(...) custom-call(bf16[8,640,512]{2,1,0:T(8,128)(2,1)} %bitcast.14, bf16[8,640,512]{2,1,0:T(8,128)(2,1)} %bitcast.18, ...), custom_call_target="tpu_custom_call" | custom-call | flops 1000 | bytes 1000 | tf_op jit(solution)/shard_map/gram_parts/pallas_call | solution.py:198
  3.9 3.4 %gram_parts.5 = (bf16[3,640,512]{2,1,0:T(8,128)(2,1)S(1)}, f32[1,520,128]{2,1,0:T(8,128)S(1)}, f32[1,520,128]{2,1,0:T(8,128)S(1)}, f32[1,520,128]{2,1,0:T(8,128)...) custom-call(bf16[8,640,512]{2,1,0:T(8,128)(2,1)} %bitcast.15, ...), custom_call_target="tpu_custom_call" | custom-call | flops 1000 | bytes 1000 | tf_op jit(solution)/shard_map/gram_parts/pallas_call | solution.py:198
  8.7 4.0 %collective-permute-start.6 = (s16[1,1056,128]{2,1,0:T(8,128)(2,1)S(1)}, s16[1,1056,128]{2,1,0:T(8,128)(2,1)S(1)}, u32[]{:S(2)}, u32[]{:S(2)}) collective-permute-start(s16[1,1056,128]{2,1,0:T(8,128)(2,1)S(1)} %send.2), channel_id=1, source_target_pairs={{0,18},{1,19},{2,16},{3,17},{4,22},{5,23},{6,20},{7,21},{8,26},{9,... | collective-permute-start | bytes 811016 | tf_op jit(solution)/shard_map/ppermute | solution.py:547
  12.7 2.8 %gram_parts.6 = (bf16[2,640,512]{2,1,0:T(8,128)(2,1)S(1)}, f32[1,520,128]{2,1,0:T(8,128)S(1)}, f32[1,520,128]{2,1,0:T(8,128)S(1)}, f32[1,520,128]{2,1,0:T(8,128)...) custom-call(bf16[8,640,512]{2,1,0:T(8,128)(2,1)} %bitcast.16, ...), custom_call_target="tpu_custom_call" | custom-call | flops 1000 | bytes 1000 | tf_op jit(solution)/shard_map/gram_parts/pallas_call | solution.py:198
  16.7 3.3 %collective-permute-done.6.refs_4_ = s16[1,1056,128]{2,1,0:T(8,128)(2,1)S(1)} collective-permute-done((s16[1,1056,128]{2,1,0:T(8,128)(2,1)S(1)}, s16[1,1056,128]{2,1,0:T(8,128)(2,1)S(1)}, u32[]{:S(2)}, u32[]{:S(2)}) %collective-permute-start.6) | collective-permute-done | bytes 270368 | tf_op jit(solution)/shard_map/ppermute | solution.py:547
  20.0 1.3 %gram_parts.7 = (bf16[2,640,512]{2,1,0:T(8,128)(2,1)S(1)}, f32[1,520,128]{2,1,0:T(8,128)S(1)}, f32[1,520,128]{2,1,0:T(8,128)S(1)}, f32[1,520,128]{2,1,0:T(8,128)S(1)}, f32[1,520,128]{2,1,0:T(8,128)S(1)}) custom-call(bf16[8,640,512]{2,1,0:T(8,128)(2,1)} %bitcast.17, bf16[8,640,512]{2,1,0:T(8,128)(2,1)} %bitcast.21, ...), custom_call_target="tpu_custom_call" | custom-call | flops 1000 | bytes 1000 | tf_op jit(solution)/shard_map/gram_parts/pallas_call | solution.py:198
  21.9 3.5 %collective-permute-done.10.refs_6_ = s16[1,1056,128]{2,1,0:T(8,128)(2,1)S(1)} collective-permute-done((s16[1,1056,128]{2,1,0:T(8,128)(2,1)S(1)}, s16[1,1056,128]{2,1,0:T(8,128)(2,1)S(1)}, u32[]{:S(2)}, u32[]{:S(2)}) %collective-permute-start.10) | collective-permute-done | bytes 270368 | tf_op jit(solution)/shard_map/ppermute | solution.py:547
  25.4 0.6 gather.1
  26.0 1.6 %collective-permute-start.11 = (s16[1,528,128]{2,1,0:T(8,128)(2,1)S(1)}, s16[1,528,128]{2,1,0:T(8,128)(2,1)S(1)}, u32[]{:S(2)}, u32[]{:S(2)}) collective-permute-start(s16[1,528,128]{2,1,0:T(8,128)(2,1)S(1)} %get-tuple-element.101), channel_id=1, source_target_pairs={{0,8},{1,9},{2,10},{3,11},{4,12},{5,13},{6,14},{7,15},{8,0},{9,1},... | collective-permute-start | bytes 405512 | tf_op jit(solution)/shard_map/ppermute | solution.py:547
  27.6 2.6 %collective-permute-start.12 = (s16[1,528,128]{2,1,0:T(8,128)(2,1)S(1)}, s16[1,528,128]{2,1,0:T(8,128)(2,1)S(1)}, u32[]{:S(2)}, u32[]{:S(2)}) collective-permute-start(s16[1,528,128]{2,1,0:T(8,128)(2,1)S(1)} %get-tuple-element.102), channel_id=1, source_target_pairs={{0,4},{1,5},{2,6},{3,7},{4,0},{5,1},{6,2},{7,3},{8,12},{9,13},{10,... | collective-permute-start | bytes 405512 | tf_op jit(solution)/shard_map/ppermute | solution.py:547
  30.2 0.9 %collective-permute-done.11.arrived_a = s16[1,528,128]{2,1,0:T(8,128)(2,1)S(1)} collective-permute-done((s16[1,528,128]{2,1,0:T(8,128)(2,1)S(1)}, s16[1,528,128]{2,1,0:T(8,128)(2,1)S(1)}, u32[]{:S(2)}, u32[]{:S(2)}) %collective-permute-start.11) | collective-permute-done | bytes 135200 | tf_op jit(solution)/shard_map/ppermute | solution.py:547
  31.1 4.8 %collective-permute-done.12.arrived_b = s16[1,528,128]{2,1,0:T(8,128)(2,1)S(1)} collective-permute-done((s16[1,528,128]{2,1,0:T(8,128)(2,1)S(1)}, s16[1,528,128]{2,1,0:T(8,128)(2,1)S(1)}, u32[]{:S(2)}, u32[]{:S(2)}) %collective-permute-start.12) | collective-permute-done | bytes 135200 | tf_op jit(solution)/shard_map/ppermute | solution.py:547
  37.1 7.5 %collective-permute-done.13.arrived_a = s16[1,528,128]{2,1,0:T(8,128)(2,1)S(1)} collective-permute-done((s16[1,528,128]{2,1,0:T(8,128)(2,1)S(1)}, s16[1,528,128]{2,1,0:T(8,128)(2,1)S(1)}, u32[]{:S(2)}, u32[]{:S(2)}) %collective-permute-start.13) | collective-permute-done | bytes 135200 | tf_op jit(solution)/shard_map/ppermute | solution.py:547
  44.5 10.1 %iterations.1.refs_0_ = bf16[1056,128]{1,0:T(8,128)(2,1)S(1)} custom-call(f32[1,1040,128]{2,1,0:T(8,128)S(1)} %get-tuple-element.103.kept, s16[1,528,128]{2,1,0:T(8,128)(2,1)S(1)} %collective-permute-done.13.arrived_a, s16[1,528,128]{2,1,0:T(8,128)(2,1)S(1)} %collective-permute-done.14.arrived_b), custom_call_target="tpu_custom_call" | custom-call | flops 1000 | bytes 1000 | tf_op jit(solution)/shard_map/iterations/pallas_call | solution.py:422
  54.6 2.6 %collective-permute-start.15 = (bf16[1056,128]{1,0:T(8,128)(2,1)S(1)}, bf16[1056,128]{1,0:T(8,128)(2,1)S(1)}, u32[]{:S(2)}, u32[]{:S(2)}) collective-permute-start(bf16[1056,128]{1,0:T(8,128)(2,1)S(1)} %iterations.1.refs_0_), channel_id=1, source_target_pairs={{0,16},{1,3},{2,18},{3,1},{4,20},{5,7},{6,22},{7,5},{8,24},{9,11},... | collective-permute-start | bytes 811016 | tf_op jit(solution)/shard_map/ppermute | solution.py:558
  57.2 0.6 collective-permute-start.16
  57.8 1.6 %apply_rows.5 = (bf16[8,640,512]{2,1,0:T(8,128)(2,1)}, bf16[8,640,512]{2,1,0:T(8,128)(2,1)}) custom-call(bf16[1056,128]{1,0:T(8,128)(2,1)S(1)} %iterations.1.refs_0_, bf16[2,640,512]{2,1,0:T(8,128)(2,1)S(1)} %get-tuple-element.106.refs_1_.refs_3_, bf16[8,640,512]{2,1,0:T(8,128)(2,1)S(1)} %bitcast.9), custom_call_target="tpu_custom_call" | custom-call | flops 1000 | bytes 1000 | tf_op jit(solution)/shard_map/apply_rows/pallas_call | solution.py:520
  59.4 3.6 %collective-permute-done.15.refs_0_ = bf16[1056,128]{1,0:T(8,128)(2,1)S(1)} collective-permute-done((bf16[1056,128]{1,0:T(8,128)(2,1)S(1)}, bf16[1056,128]{1,0:T(8,128)(2,1)S(1)}, u32[]{:S(2)}, u32[]{:S(2)}) %collective-permute-start.15) | collective-permute-done | bytes 270368 | tf_op jit(solution)/shard_map/ppermute | solution.py:558
  63.0 0.7 collective-permute-done.16.refs_1_
  64.2 1.1 %collective-permute-start.17 = (bf16[1056,128]{1,0:T(8,128)(2,1)S(1)}, bf16[1056,128]{1,0:T(8,128)(2,1)S(1)}, u32[]{:S(2)}, u32[]{:S(2)}) collective-permute-start(bf16[1056,128]{1,0:T(8,128)(2,1)S(1)} %collective-permute-done.16.refs_1_), channel_id=1, source_target_pairs={{0,16},{1,3},{2,18},{3,1},{4,20},{5,7},{6,22},{7,5},{8,24},{9,11},... | collective-permute-start | bytes 811016 | tf_op jit(solution)/shard_map/ppermute | solution.py:558
  65.3 2.2 %apply_rows.6 = (bf16[8,640,512]{2,1,0:T(8,128)(2,1)}, bf16[8,640,512]{2,1,0:T(8,128)(2,1)}) custom-call(bf16[1056,128]{1,0:T(8,128)(2,1)S(1)} %collective-permute-done.15.refs_0_, bf16[1056,128]{1,0:T(8,128)(2,1)S(1)} %collective-permute-done.16.refs_1_, ...), custom_call_target="tpu_custom_call", output_to_operand_aliasing={{0}: (4, {}), {1}: (5, {})} | custom-call | flops 1000 | bytes 1000 | tf_op jit(solution)/shard_map/apply_rows/pallas_call | solution.py:520
  67.5 2.8 %apply_rows.7 = (bf16[8,640,512]{2,1,0:T(8,128)(2,1)}, bf16[8,640,512]{2,1,0:T(8,128)(2,1)}) custom-call(bf16[1056,128]{1,0:T(8,128)(2,1)S(1)} %collective-permute-done.18.refs_0_, bf16[1056,128]{1,0:T(8,128)(2,1)S(1)} %collective-permute-done.19.refs_1_, ...), custom_call_target="tpu_custom_call", output_to_operand_aliasing={{0}: (6, {}), {1}: (7, {})} | custom-call | flops 1000 | bytes 1000 | tf_op jit(solution)/shard_map/apply_rows/pallas_call | solution.py:520
  70.6 1.6 %apply_rows.8 = (bf16[8,640,512]{2,1,0:T(8,128)(2,1)}, bf16[8,640,512]{2,1,0:T(8,128)(2,1)}) custom-call(bf16[1056,128]{1,0:T(8,128)(2,1)S(1)} %collective-permute-done.17.refs_0_, bf16[3,640,512]{2,1,0:T(8,128)(2,1)S(1)} %get-tuple-element.112.refs_4_.refs_1_, bf16[8,640,512]{2,1,0:T(8,128)(2,1)S(1)} %bitcast.12, ...), custom_call_target="tpu_custom_call", output_to_operand_aliasing={{0}: (3, {}), {1}: (4, {})} | custom-call | flops 1000 | bytes 1000 | tf_op jit(solution)/shard_map/apply_rows/pallas_call | solution.py:520
  72.3 1.6 %apply_rows.9 = (bf16[8,640,512]{2,1,0:T(8,128)(2,1)}, bf16[8,640,512]{2,1,0:T(8,128)(2,1)}) custom-call(bf16[1056,128]{1,0:T(8,128)(2,1)S(1)} %collective-permute-done.21.refs_0_, bf16[1,640,512]{2,1,0:T(8,128)(2,1)S(1)} %get-tuple-element.121.refs_1_, bf16[8,640,512]{2,1,0:T(8,128)(2,1)S(1)} %bitcast.13, ...), custom_call_target="tpu_custom_call", output_to_operand_aliasing={{0}: (3, {}), {1}: (4, {})} | custom-call | flops 1000 | bytes 1000 | tf_op jit(solution)/shard_map/apply_rows/pallas_call | solution.py:520
  (39 shorter events, 5.7 us)
Async XLA Ops:
  3.3 5.0 %collective-permute-start = (f32[1,520,128]{2,1,0:T(8,128)S(1)}, f32[1,520,128]{2,1,0:T(8,128)S(1)}, u32[]{:S(2)}, u32[]{:S(2)}) collective-permute-start(f32[1,520,128]{2,1,0:T(8,128)S(1)} %get-tuple-element.70), channel_id=1, source_target_pairs={{0,1},{1,0},{2,3},{3,2},{4,5},{5,4},{6,7},{7,6},{8,9},{9,8},{10,11... | collective-permute-start | bytes 798728 | tf_op jit(solution)/shard_map/ppermute | solution.py:547
  3.9 4.5 %collective-permute-start.1 = (f32[1,520,128]{2,1,0:T(8,128)S(1)}, f32[1,520,128]{2,1,0:T(8,128)S(1)}, u32[]{:S(2)}, u32[]{:S(2)}) collective-permute-start(f32[1,520,128]{2,1,0:T(8,128)S(1)} %get-tuple-element.71), channel_id=1, source_target_pairs={{0,1},{1,0},{2,3},{3,2},{4,5},{5,4},{6,7},{7,6},{8,9},{9,8},{10,11... | collective-permute-start | bytes 798728 | tf_op jit(solution)/shard_map/ppermute | solution.py:547
  7.3 8.2 %collective-permute-start.2 = (f32[1,520,128]{2,1,0:T(8,128)S(1)}, f32[1,520,128]{2,1,0:T(8,128)S(1)}, u32[]{:S(2)}, u32[]{:S(2)}) collective-permute-start(f32[1,520,128]{2,1,0:T(8,128)S(1)} %get-tuple-element.78), channel_id=1, source_target_pairs={{0,1},{1,0},{2,3},{3,2},{4,5},{5,4},{6,7},{7,6},{8,9},{9,8},{10,11... | collective-permute-start | bytes 798728 | tf_op jit(solution)/shard_map/ppermute | solution.py:547
  7.8 7.7 %collective-permute-start.3 = (f32[1,520,128]{2,1,0:T(8,128)S(1)}, f32[1,520,128]{2,1,0:T(8,128)S(1)}, u32[]{:S(2)}, u32[]{:S(2)}) collective-permute-start(f32[1,520,128]{2,1,0:T(8,128)S(1)} %get-tuple-element.79), channel_id=1, source_target_pairs={{0,1},{1,0},{2,3},{3,2},{4,5},{5,4},{6,7},{7,6},{8,9},{9,8},{10,11... | collective-permute-start | bytes 798728 | tf_op jit(solution)/shard_map/ppermute | solution.py:547
  7.9 7.7 %collective-permute-start.4 = (f32[1,520,128]{2,1,0:T(8,128)S(1)}, f32[1,520,128]{2,1,0:T(8,128)S(1)}, u32[]{:S(2)}, u32[]{:S(2)}) collective-permute-start(f32[1,520,128]{2,1,0:T(8,128)S(1)} %get-tuple-element.82), channel_id=1, source_target_pairs={{0,1},{1,0},{2,3},{3,2},{4,5},{5,4},{6,7},{7,6},{8,9},{9,8},{10,11... | collective-permute-start | bytes 798728 | tf_op jit(solution)/shard_map/ppermute | solution.py:547
  8.3 7.2 %collective-permute-start.5 = (f32[1,520,128]{2,1,0:T(8,128)S(1)}, f32[1,520,128]{2,1,0:T(8,128)S(1)}, u32[]{:S(2)}, u32[]{:S(2)}) collective-permute-start(f32[1,520,128]{2,1,0:T(8,128)S(1)} %get-tuple-element.83), channel_id=1, source_target_pairs={{0,1},{1,0},{2,3},{3,2},{4,5},{5,4},{6,7},{7,6},{8,9},{9,8},{10,11... | collective-permute-start | bytes 798728 | tf_op jit(solution)/shard_map/ppermute | solution.py:547
  8.7 11.3 %collective-permute-start.6 = (s16[1,1056,128]{2,1,0:T(8,128)(2,1)S(1)}, s16[1,1056,128]{2,1,0:T(8,128)(2,1)S(1)}, u32[]{:S(2)}, u32[]{:S(2)}) collective-permute-start(s16[1,1056,128]{2,1,0:T(8,128)(2,1)S(1)} %send.2), channel_id=1, source_target_pairs={{0,18},{1,19},{2,16},{3,17},{4,22},{5,23},{6,20},{7,21},{8,26},{9,... | collective-permute-start | bytes 811016 | tf_op jit(solution)/shard_map/ppermute | solution.py:547
  16.0 41.8 %slice-start = ((s8[5242880]{0:T(1024)(128)(4,1)}), s8[4194304]{0:T(1024)(128)(4,1)S(1)}, s32[]{:S(2)}) async-start(s8[5242880]{0:T(1024)(128)(4,1)} %bitcast.7), calls=%async_computation | async-start | bytes 8388608
  16.0 41.7 %slice-start.1 = ((s8[5242880]{0:T(1024)(128)(4,1)}), s8[1048576]{0:T(1024)(128)(4,1)S(1)}, s32[]{:S(2)}) async-start(s8[5242880]{0:T(1024)(128)(4,1)} %bitcast.7), calls=%async_computation.1 | async-start | bytes 2097152
  16.1 9.3 %collective-permute-start.10 = (s16[1,1056,128]{2,1,0:T(8,128)(2,1)S(1)}, s16[1,1056,128]{2,1,0:T(8,128)(2,1)S(1)}, u32[]{:S(2)}, u32[]{:S(2)}) collective-permute-start(s16[1,1056,128]{2,1,0:T(8,128)(2,1)S(1)} %get-tuple-element.99), channel_id=1, source_target_pairs={{0,2},{1,3},{2,0},{3,1},{4,6},{5,7},{6,4},{7,5},{8,10},{9,11},{10,... | collective-permute-start | bytes 811016 | tf_op jit(solution)/shard_map/ppermute | solution.py:547
  16.6 8.8 %collective-permute-start.9 = (s16[1,1056,128]{2,1,0:T(8,128)(2,1)S(1)}, s16[1,1056,128]{2,1,0:T(8,128)(2,1)S(1)}, u32[]{:S(2)}, u32[]{:S(2)}) collective-permute-start(s16[1,1056,128]{2,1,0:T(8,128)(2,1)S(1)} %get-tuple-element.98), channel_id=1, source_target_pairs={{0,16},{1,17},{2,18},{3,19},{4,20},{5,21},{6,22},{7,23},{8,24},{9,... | collective-permute-start | bytes 811016 | tf_op jit(solution)/shard_map/ppermute | solution.py:547
  21.3 4.1 %collective-permute-start.7 = (f32[1,520,128]{2,1,0:T(8,128)S(1)}, f32[1,520,128]{2,1,0:T(8,128)S(1)}, u32[]{:S(2)}, u32[]{:S(2)}) collective-permute-start(f32[1,520,128]{2,1,0:T(8,128)S(1)} %get-tuple-element.95), channel_id=1, source_target_pairs={{0,1},{1,0},{2,3},{3,2},{4,5},{5,4},{6,7},{7,6},{8,9},{9,8},{10,11... | collective-permute-start | bytes 798728 | tf_op jit(solution)/shard_map/ppermute | solution.py:547
  21.4 4.0 %collective-permute-start.8 = (f32[1,520,128]{2,1,0:T(8,128)S(1)}, f32[1,520,128]{2,1,0:T(8,128)S(1)}, u32[]{:S(2)}, u32[]{:S(2)}) collective-permute-start(f32[1,520,128]{2,1,0:T(8,128)S(1)} %get-tuple-element.96), channel_id=1, source_target_pairs={{0,1},{1,0},{2,3},{3,2},{4,5},{5,4},{6,7},{7,6},{8,9},{9,8},{10,11... | collective-permute-start | bytes 798728 | tf_op jit(solution)/shard_map/ppermute | solution.py:547
  26.0 5.1 %collective-permute-start.11 = (s16[1,528,128]{2,1,0:T(8,128)(2,1)S(1)}, s16[1,528,128]{2,1,0:T(8,128)(2,1)S(1)}, u32[]{:S(2)}, u32[]{:S(2)}) collective-permute-start(s16[1,528,128]{2,1,0:T(8,128)(2,1)S(1)} %get-tuple-element.101), channel_id=1, source_target_pairs={{0,8},{1,9},{2,10},{3,11},{4,12},{5,13},{6,14},{7,15},{8,0},{9,1},... | collective-permute-start | bytes 405512 | tf_op jit(solution)/shard_map/ppermute | solution.py:547
  27.6 8.3 %collective-permute-start.12 = (s16[1,528,128]{2,1,0:T(8,128)(2,1)S(1)}, s16[1,528,128]{2,1,0:T(8,128)(2,1)S(1)}, u32[]{:S(2)}, u32[]{:S(2)}) collective-permute-start(s16[1,528,128]{2,1,0:T(8,128)(2,1)S(1)} %get-tuple-element.102), channel_id=1, source_target_pairs={{0,4},{1,5},{2,6},{3,7},{4,0},{5,1},{6,2},{7,3},{8,12},{9,13},{10,... | collective-permute-start | bytes 405512 | tf_op jit(solution)/shard_map/ppermute | solution.py:547
  36.2 8.3 %collective-permute-start.13 = (s16[1,528,128]{2,1,0:T(8,128)(2,1)S(1)}, s16[1,528,128]{2,1,0:T(8,128)(2,1)S(1)}, u32[]{:S(2)}, u32[]{:S(2)}) collective-permute-start(s16[1,528,128]{2,1,0:T(8,128)(2,1)S(1)} %get-tuple-element.104), channel_id=1, source_target_pairs={{0,4},{1,5},{2,6},{3,7},{4,0},{5,1},{6,2},{7,3},{8,12},{9,13},{10,... | collective-permute-start | bytes 405512 | tf_op jit(solution)/shard_map/ppermute | solution.py:547
  36.5 8.0 %collective-permute-start.14 = (s16[1,528,128]{2,1,0:T(8,128)(2,1)S(1)}, s16[1,528,128]{2,1,0:T(8,128)(2,1)S(1)}, u32[]{:S(2)}, u32[]{:S(2)}) collective-permute-start(s16[1,528,128]{2,1,0:T(8,128)(2,1)S(1)} %get-tuple-element.105), channel_id=1, source_target_pairs={{0,8},{1,9},{2,10},{3,11},{4,12},{5,13},{6,14},{7,15},{8,0},{9,1},... | collective-permute-start | bytes 405512 | tf_op jit(solution)/shard_map/ppermute | solution.py:547
  54.6 8.4 %collective-permute-start.15 = (bf16[1056,128]{1,0:T(8,128)(2,1)S(1)}, bf16[1056,128]{1,0:T(8,128)(2,1)S(1)}, u32[]{:S(2)}, u32[]{:S(2)}) collective-permute-start(bf16[1056,128]{1,0:T(8,128)(2,1)S(1)} %iterations.1.refs_0_), channel_id=1, source_target_pairs={{0,16},{1,3},{2,18},{3,1},{4,20},{5,7},{6,22},{7,5},{8,24},{9,11},... | collective-permute-start | bytes 811016 | tf_op jit(solution)/shard_map/ppermute | solution.py:558
  57.2 6.5 %collective-permute-start.16 = (bf16[1056,128]{1,0:T(8,128)(2,1)S(1)}, bf16[1056,128]{1,0:T(8,128)(2,1)S(1)}, u32[]{:S(2)}, u32[]{:S(2)}) collective-permute-start(bf16[1056,128]{1,0:T(8,128)(2,1)S(1)} %iterations.1.refs_0_), channel_id=1, source_target_pairs={{0,2},{1,17},{2,0},{3,19},{4,6},{5,21},{6,4},{7,23},{8,10},{9,25},... | collective-permute-start | bytes 811016 | tf_op jit(solution)/shard_map/ppermute | solution.py:558
  63.7 3.8 %collective-permute-start.18 = (bf16[1056,128]{1,0:T(8,128)(2,1)S(1)}, bf16[1056,128]{1,0:T(8,128)(2,1)S(1)}, u32[]{:S(2)}, u32[]{:S(2)}) collective-permute-start(bf16[1056,128]{1,0:T(8,128)(2,1)S(1)} %iterations.1.refs_0_), channel_id=1, source_target_pairs={{0,1},{1,0},{2,3},{3,2},{4,5},{5,4},{6,7},{7,6},{8,9},{9,8},{10,11... | collective-permute-start | bytes 811016 | tf_op jit(solution)/shard_map/ppermute | solution.py:547
  63.7 3.8 %collective-permute-start.19 = (bf16[1056,128]{1,0:T(8,128)(2,1)S(1)}, bf16[1056,128]{1,0:T(8,128)(2,1)S(1)}, u32[]{:S(2)}, u32[]{:S(2)}) collective-permute-start(bf16[1056,128]{1,0:T(8,128)(2,1)S(1)} %collective-permute-done.15.refs_0_), channel_id=1, source_target_pairs={{0,1},{1,0},{2,3},{3,2},{4,5},{5,4},{6,7},{7,6},{8,9},{9,8},{10,11... | collective-permute-start | bytes 811016 | tf_op jit(solution)/shard_map/ppermute | solution.py:547
  64.2 3.3 %collective-permute-start.20 = (bf16[1056,128]{1,0:T(8,128)(2,1)S(1)}, bf16[1056,128]{1,0:T(8,128)(2,1)S(1)}, u32[]{:S(2)}, u32[]{:S(2)}) collective-permute-start(bf16[1056,128]{1,0:T(8,128)(2,1)S(1)} %collective-permute-done.16.refs_1_), channel_id=1, source_target_pairs={{0,1},{1,0},{2,3},{3,2},{4,5},{5,4},{6,7},{7,6},{8,9},{9,8},{10,11... | collective-permute-start | bytes 811016 | tf_op jit(solution)/shard_map/ppermute | solution.py:547
  64.2 6.5 %collective-permute-start.17 = (bf16[1056,128]{1,0:T(8,128)(2,1)S(1)}, bf16[1056,128]{1,0:T(8,128)(2,1)S(1)}, u32[]{:S(2)}, u32[]{:S(2)}) collective-permute-start(bf16[1056,128]{1,0:T(8,128)(2,1)S(1)} %collective-permute-done.16.refs_1_), channel_id=1, source_target_pairs={{0,16},{1,3},{2,18},{3,1},{4,20},{5,7},{6,22},{7,5},{8,24},{9,11},... | collective-permute-start | bytes 811016 | tf_op jit(solution)/shard_map/ppermute | solution.py:558
  70.6 1.7 %collective-permute-start.21 = (bf16[1056,128]{1,0:T(8,128)(2,1)S(1)}, bf16[1056,128]{1,0:T(8,128)(2,1)S(1)}, u32[]{:S(2)}, u32[]{:S(2)}) collective-permute-start(bf16[1056,128]{1,0:T(8,128)(2,1)S(1)} %collective-permute-done.17.refs_0_), channel_id=1, source_target_pairs={{0,1},{1,0},{2,3},{3,2},{4,5},{5,4},{6,7},{7,6},{8,9},{9,8},{10,11... | collective-permute-start | bytes 811016 | tf_op jit(solution)/shard_map/ppermute | solution.py:547

commit v6 on v5

--- a/solution.py
+++ b/solution.py
@@ -41,7 +41,10 @@
 HEAD_P = AUX_P + 4 * LANES
 ROWS_P = AUX_P + 8 * LANES
 UNIT = 32000.0
-CHUNKS = 2
+
+
+def chunks_of(capacity):
+    return 4 if capacity % 64 == 0 else 2 if capacity % 32 == 0 else 1
 
 
 SHORT = pl.CostEstimate(flops=1000, bytes_accessed=1000, transcendentals=0)
@@ -317,19 +320,6 @@
     return jnp.dot(x, y, preferred_element_type=f32)
 
 
-def wide(*parts):
-    return jnp.concatenate(parts, axis=1)
-
-
-def tall(*parts):
-    return jnp.concatenate(parts, axis=0)
-
-
-def parts_of(x):
-    high = x.astype(bf16)
-    return high, (x - high.astype(f32)).astype(bf16)
-
-
 def unpack_symmetric(which, blocks, diagonal, store):
     row, col = square_iotas()
     for (i, j, triangle), block in zip(HALVES[which], blocks):
@@ -364,24 +354,30 @@
     full_row = lax.broadcasted_iota(i32, (KV_RANK, KV_RANK), 0)
     full_col = lax.broadcasted_iota(i32, (KV_RANK, KV_RANK), 1)
     on_diagonal = full_row == full_col
+    def diagonal_of(x):
+        return jnp.sum(jnp.where(on_diagonal, x, 0.0), axis=0, keepdims=True)
+
+    def rest_of(x):
+        return jnp.where(on_diagonal, 0.0, x).astype(bf16)
+
     product = None
     for repeat in range(NS_ITERS):
-        high, low = parts_of(gram)
-        if repeat >= 2:
-            square = mm(wide(high, high, low), tall(high, low, high))
+        diagonal = diagonal_of(gram)
+        columns = [diagonal[:, i * LANES : (i + 1) * LANES] for i in range(BLOCKS)]
+        down = jnp.concatenate([jnp.broadcast_to(one, (LANES, LANES)).T for one in columns], axis=0)
+        down = jnp.concatenate([down] * BLOCKS, axis=1)
+        rest = rest_of(gram)
+        square = mm(rest, rest) + jnp.where(on_diagonal, diagonal * diagonal, gram * (down + diagonal))
+        mixing = (coef_second * gram + coef_third * square).astype(bf16)
+        mixing_wide = mixing.astype(f32)
+        if product is None:
+            product = jnp.where(on_diagonal, coef_first, 0.0) + mixing_wide
         else:
-            square = mm(high, high)
-        mixing = (coef_second * gram + coef_third * square).astype(bf16)
-        if product is None:
-            product = jnp.where(on_diagonal, coef_first, 0.0) + mixing.astype(f32)
-        else:
-            diagonal = jnp.sum(jnp.where(on_diagonal, product, 0.0), axis=0, keepdims=True)
-            rest = jnp.where(on_diagonal, 0.0, product).astype(bf16)
-            product = coef_first * product + (mm(mixing, rest) + mixing.astype(f32) * diagonal)
+            moved = mm(mixing, rest_of(product)) + mixing_wide * diagonal_of(product)
+            product = coef_first * product + moved
         if repeat < NS_ITERS - 1:
-            half = coef_first * gram + mm(wide(high, low), tall(mixing, mixing))
-            half_high, half_low = parts_of(half)
-            gram = coef_first * half + mm(wide(mixing, mixing), tall(half_high, half_low))
+            half = coef_first * gram + (mm(rest, mixing) + mixing_wide * down)
+            gram = coef_first * half + (mm(mixing, rest_of(half)) + mixing_wide * diagonal_of(half))
     gram_ref[...] = product
     at = AUX_P
     for entries in HALVES:
@@ -444,7 +440,8 @@
     rms_scale = 0.2 * math.sqrt(max(KV_ROWS, KV_RANK))
     lane = lax.broadcasted_iota(i32, (1, LANES), 1)
     head_shift = head_rows.bit_length() - 1
-    assert head_rows == 1 << head_shift and capacity % (16 * CHUNKS) == 0
+    chunks = chunks_of(capacity)
+    assert head_rows == 1 << head_shift and capacity % (16 * chunks) == 0
     rows_of_slots = -(-capacity // LANES)
     slot = lax.broadcasted_iota(i32, (rows_of_slots, LANES), 0) * LANES
     slot = slot + lax.broadcasted_iota(i32, (rows_of_slots, LANES), 1)
@@ -489,8 +486,8 @@
         if isinstance(index, tuple):
             core = here[1] if pick[1] else 1 - here[1]
             index = jnp.where(core == 0, index[0], index[1])
-        for chunk in range(CHUNKS):
-            size = capacity // CHUNKS
+        for chunk in range(chunks):
+            size = capacity // chunks
             among = slice(chunk * size, (chunk + 1) * size)
             product = mm(rows_in[source][index, among, :], mat_ref[step])
             for i in range(BLOCKS):
@@ -502,7 +499,7 @@
             at = pl.ds(chunk * size, size)
             for number, (held, out) in enumerate(((update_ref, update_out), (new_ref, weight_out))):
                 copy = pltpu.make_async_copy(
-                    held.at[step, at], out.at[layer, at], leaving.at[number, step * CHUNKS + chunk]
+                    held.at[step, at], out.at[layer, at], leaving.at[number, step * chunks + chunk]
                 )
                 copy.start()
                 copies.append(copy)
@@ -526,7 +523,7 @@
             pltpu.VMEM((number, KV_RANK, KV_RANK), bf16),
             pltpu.VMEM((number, capacity, features), bf16),
             pltpu.VMEM((number, capacity, features), bf16),
-            pltpu.SemaphoreType.DMA((2, number * CHUNKS)),
+            pltpu.SemaphoreType.DMA((2, number * chunks_of(capacity))),
         ],
         input_output_aliases={len(args) - 2: 0, len(args) - 1: 1} if outs else {},
         compiler_params=params(),

time: 74.4 us -> 71.2 us (0.957)
  Pallas kernels: 31.9 us -> 28.7 us
    pallas_call x1, Pallas kernels: 10.1 us -> 7.04 us  [iterations(): pl.pallas_call(iterate_kernel, in_specs=[pl.BlockSpec(memory_space=pltpu....]
  transfers between devices with their start and end apart: 22 -> 22, of which waited for: 8 -> 8; matrix products, arithmetic and copies ran while one was open for 0% -> 0% of each run, Pallas kernels for 21% -> 22%
where the time goes in v6:
time: 71.2 us; the launch traced here: 71 us
  Pallas kernels  28.7 us (40%)
  waiting for transfers between devices  24.6 us (35%)
  starting transfers between devices  16.6 us (23%)
  between operations  1 us (1%)
    ppermute x19, waiting for transfers between devices, over(): return lax.ppermute(x, ('dp', 'expert'), [(i, i ^ mask) for i in everyone])  20 us
    ppermute x19, starting transfers between devices, over(): return lax.ppermute(x, ('dp', 'expert'), [(i, i ^ mask) for i in everyone])  12.4 us
    pallas_call x4, Pallas kernels, gram_parts(): pl.pallas_call(functools.partial(gram_kernel, expert_size, picks, later,...  10.1 us
    pallas_call x5, Pallas kernels, apply_rows(): pl.pallas_call(functools.partial(apply_kernel, steps, spread, places, sea...  9.77 us
    pallas_call x1, Pallas kernels, iterations(): pl.pallas_call(iterate_kernel, in_specs=[pl.BlockSpec(memory_space=pltpu....  7.04 us
    ppermute x3, waiting for transfers between devices, by_core(): lax.ppermute(x, ('dp', 'expert'), [(i, i ^ (odd if i & 1 else even)) for...  4.65 us
    ppermute x3, starting transfers between devices, by_core(): lax.ppermute(x, ('dp', 'expert'), [(i, i ^ (odd if i & 1 else even)) for...  4.23 us
    pallas_call x4, Pallas kernels, local_call(): pl.pallas_call(kernel, in_specs=[pl.BlockSpec(memory_space=pltpu.VMEM)] *...  1.73 us
  transfers between devices with their start and end apart: 22, of which 8 were waited for; matrix products, arithmetic and copies ran while one was open for 0% of the time, Pallas kernels for 22%

profile of v6, /device:TPU:0, one launch (start us, length us, event | category | flops | bytes accessed | tf_op | source)
XLA Modules:
  0.0 71.0 jit_solution(10819375101928572423)
XLA Ops:
  0.6 2.7 %gram_parts.4 = (f32[8,8,128]{2,1,0:T(8,128)S(1)}, bf16[1,640,512]{2,1,0:T(8,128)(2,1)S(1)}, f32[1,520,128]{2,1,0:T(8,128)S(1)}, f32[1,520,128]{2,1,0:T(8,128)S(...) custom-call(bf16[8,640,512]{2,1,0:T(8,128)(2,1)} %bitcast.14, bf16[8,640,512]{2,1,0:T(8,128)(2,1)} %bitcast.18, ...), custom_call_target="tpu_custom_call" | custom-call | flops 1000 | bytes 1000 | tf_op jit(solution)/shard_map/gram_parts/pallas_call | solution.py:201
  3.9 3.4 %gram_parts.5 = (bf16[3,640,512]{2,1,0:T(8,128)(2,1)S(1)}, f32[1,520,128]{2,1,0:T(8,128)S(1)}, f32[1,520,128]{2,1,0:T(8,128)S(1)}, f32[1,520,128]{2,1,0:T(8,128)...) custom-call(bf16[8,640,512]{2,1,0:T(8,128)(2,1)} %bitcast.15, ...), custom_call_target="tpu_custom_call" | custom-call | flops 1000 | bytes 1000 | tf_op jit(solution)/shard_map/gram_parts/pallas_call | solution.py:201
  8.7 4.0 %collective-permute-start.6 = (s16[1,1056,128]{2,1,0:T(8,128)(2,1)S(1)}, s16[1,1056,128]{2,1,0:T(8,128)(2,1)S(1)}, u32[]{:S(2)}, u32[]{:S(2)}) collective-permute-start(s16[1,1056,128]{2,1,0:T(8,128)(2,1)S(1)} %send.2), channel_id=1, source_target_pairs={{0,18},{1,19},{2,16},{3,17},{4,22},{5,23},{6,20},{7,21},{8,26},{9,... | collective-permute-start | bytes 811016 | tf_op jit(solution)/shard_map/ppermute | solution.py:544
  12.7 2.8 %gram_parts.6 = (bf16[2,640,512]{2,1,0:T(8,128)(2,1)S(1)}, f32[1,520,128]{2,1,0:T(8,128)S(1)}, f32[1,520,128]{2,1,0:T(8,128)S(1)}, f32[1,520,128]{2,1,0:T(8,128)...) custom-call(bf16[8,640,512]{2,1,0:T(8,128)(2,1)} %bitcast.16, ...), custom_call_target="tpu_custom_call" | custom-call | flops 1000 | bytes 1000 | tf_op jit(solution)/shard_map/gram_parts/pallas_call | solution.py:201
  16.7 3.3 %collective-permute-done.6.refs_4_ = s16[1,1056,128]{2,1,0:T(8,128)(2,1)S(1)} collective-permute-done((s16[1,1056,128]{2,1,0:T(8,128)(2,1)S(1)}, s16[1,1056,128]{2,1,0:T(8,128)(2,1)S(1)}, u32[]{:S(2)}, u32[]{:S(2)}) %collective-permute-start.6) | collective-permute-done | bytes 270368 | tf_op jit(solution)/shard_map/ppermute | solution.py:544
  20.0 1.3 %gram_parts.7 = (bf16[2,640,512]{2,1,0:T(8,128)(2,1)S(1)}, f32[1,520,128]{2,1,0:T(8,128)S(1)}, f32[1,520,128]{2,1,0:T(8,128)S(1)}, f32[1,520,128]{2,1,0:T(8,128)S(1)}, f32[1,520,128]{2,1,0:T(8,128)S(1)}) custom-call(bf16[8,640,512]{2,1,0:T(8,128)(2,1)} %bitcast.17, bf16[8,640,512]{2,1,0:T(8,128)(2,1)} %bitcast.21, ...), custom_call_target="tpu_custom_call" | custom-call | flops 1000 | bytes 1000 | tf_op jit(solution)/shard_map/gram_parts/pallas_call | solution.py:201
  21.9 3.5 %collective-permute-done.10.refs_6_ = s16[1,1056,128]{2,1,0:T(8,128)(2,1)S(1)} collective-permute-done((s16[1,1056,128]{2,1,0:T(8,128)(2,1)S(1)}, s16[1,1056,128]{2,1,0:T(8,128)(2,1)S(1)}, u32[]{:S(2)}, u32[]{:S(2)}) %collective-permute-start.10) | collective-permute-done | bytes 270368 | tf_op jit(solution)/shard_map/ppermute | solution.py:544
  25.4 0.6 gather.1
  26.0 1.6 %collective-permute-start.11 = (s16[1,528,128]{2,1,0:T(8,128)(2,1)S(1)}, s16[1,528,128]{2,1,0:T(8,128)(2,1)S(1)}, u32[]{:S(2)}, u32[]{:S(2)}) collective-permute-start(s16[1,528,128]{2,1,0:T(8,128)(2,1)S(1)} %get-tuple-element.101), channel_id=1, source_target_pairs={{0,8},{1,9},{2,10},{3,11},{4,12},{5,13},{6,14},{7,15},{8,0},{9,1},... | collective-permute-start | bytes 405512 | tf_op jit(solution)/shard_map/ppermute | solution.py:544
  27.6 2.6 %collective-permute-start.12 = (s16[1,528,128]{2,1,0:T(8,128)(2,1)S(1)}, s16[1,528,128]{2,1,0:T(8,128)(2,1)S(1)}, u32[]{:S(2)}, u32[]{:S(2)}) collective-permute-start(s16[1,528,128]{2,1,0:T(8,128)(2,1)S(1)} %get-tuple-element.102), channel_id=1, source_target_pairs={{0,4},{1,5},{2,6},{3,7},{4,0},{5,1},{6,2},{7,3},{8,12},{9,13},{10,... | collective-permute-start | bytes 405512 | tf_op jit(solution)/shard_map/ppermute | solution.py:544
  30.2 0.9 %collective-permute-done.11.arrived_a = s16[1,528,128]{2,1,0:T(8,128)(2,1)S(1)} collective-permute-done((s16[1,528,128]{2,1,0:T(8,128)(2,1)S(1)}, s16[1,528,128]{2,1,0:T(8,128)(2,1)S(1)}, u32[]{:S(2)}, u32[]{:S(2)}) %collective-permute-start.11) | collective-permute-done | bytes 135200 | tf_op jit(solution)/shard_map/ppermute | solution.py:544
  31.1 4.8 %collective-permute-done.12.arrived_b = s16[1,528,128]{2,1,0:T(8,128)(2,1)S(1)} collective-permute-done((s16[1,528,128]{2,1,0:T(8,128)(2,1)S(1)}, s16[1,528,128]{2,1,0:T(8,128)(2,1)S(1)}, u32[]{:S(2)}, u32[]{:S(2)}) %collective-permute-start.12) | collective-permute-done | bytes 135200 | tf_op jit(solution)/shard_map/ppermute | solution.py:544
  36.5 0.5 collective-permute-start.14
  37.1 7.5 %collective-permute-done.13.arrived_a = s16[1,528,128]{2,1,0:T(8,128)(2,1)S(1)} collective-permute-done((s16[1,528,128]{2,1,0:T(8,128)(2,1)S(1)}, s16[1,528,128]{2,1,0:T(8,128)(2,1)S(1)}, u32[]{:S(2)}, u32[]{:S(2)}) %collective-permute-start.13) | collective-permute-done | bytes 135200 | tf_op jit(solution)/shard_map/ppermute | solution.py:544
  44.5 7.0 %iterations.1.refs_0_ = bf16[1056,128]{1,0:T(8,128)(2,1)S(1)} custom-call(f32[1,1040,128]{2,1,0:T(8,128)S(1)} %get-tuple-element.103.kept, s16[1,528,128]{2,1,0:T(8,128)(2,1)S(1)} %collective-permute-done.13.arrived_a, s16[1,528,128]{2,1,0:T(8,128)(2,1)S(1)} %collective-permute-done.14.arrived_b), custom_call_target="tpu_custom_call" | custom-call | flops 1000 | bytes 1000 | tf_op jit(solution)/shard_map/iterations/pallas_call | solution.py:418
  51.6 2.7 %collective-permute-start.15 = (bf16[1056,128]{1,0:T(8,128)(2,1)S(1)}, bf16[1056,128]{1,0:T(8,128)(2,1)S(1)}, u32[]{:S(2)}, u32[]{:S(2)}) collective-permute-start(bf16[1056,128]{1,0:T(8,128)(2,1)S(1)} %iterations.1.refs_0_), channel_id=1, source_target_pairs={{0,16},{1,3},{2,18},{3,1},{4,20},{5,7},{6,22},{7,5},{8,24},{9,11},... | collective-permute-start | bytes 811016 | tf_op jit(solution)/shard_map/ppermute | solution.py:555
  54.8 1.6 %apply_rows.5 = (bf16[8,640,512]{2,1,0:T(8,128)(2,1)}, bf16[8,640,512]{2,1,0:T(8,128)(2,1)}) custom-call(bf16[1056,128]{1,0:T(8,128)(2,1)S(1)} %iterations.1.refs_0_, bf16[2,640,512]{2,1,0:T(8,128)(2,1)S(1)} %get-tuple-element.106.refs_1_.refs_3_, bf16[8,640,512]{2,1,0:T(8,128)(2,1)S(1)} %bitcast.9), custom_call_target="tpu_custom_call" | custom-call | flops 1000 | bytes 1000 | tf_op jit(solution)/shard_map/apply_rows/pallas_call | solution.py:517
  56.3 3.6 %collective-permute-done.15.refs_0_ = bf16[1056,128]{1,0:T(8,128)(2,1)S(1)} collective-permute-done((bf16[1056,128]{1,0:T(8,128)(2,1)S(1)}, bf16[1056,128]{1,0:T(8,128)(2,1)S(1)}, u32[]{:S(2)}, u32[]{:S(2)}) %collective-permute-start.15) | collective-permute-done | bytes 270368 | tf_op jit(solution)/shard_map/ppermute | solution.py:555
  60.0 0.7 collective-permute-done.16.refs_1_
  61.2 1.0 %collective-permute-start.17 = (bf16[1056,128]{1,0:T(8,128)(2,1)S(1)}, bf16[1056,128]{1,0:T(8,128)(2,1)S(1)}, u32[]{:S(2)}, u32[]{:S(2)}) collective-permute-start(bf16[1056,128]{1,0:T(8,128)(2,1)S(1)} %collective-permute-done.16.refs_1_), channel_id=1, source_target_pairs={{0,16},{1,3},{2,18},{3,1},{4,20},{5,7},{6,22},{7,5},{8,24},{9,11},... | collective-permute-start | bytes 811016 | tf_op jit(solution)/shard_map/ppermute | solution.py:555
  62.2 2.2 %apply_rows.6 = (bf16[8,640,512]{2,1,0:T(8,128)(2,1)}, bf16[8,640,512]{2,1,0:T(8,128)(2,1)}) custom-call(bf16[1056,128]{1,0:T(8,128)(2,1)S(1)} %collective-permute-done.15.refs_0_, bf16[1056,128]{1,0:T(8,128)(2,1)S(1)} %collective-permute-done.16.refs_1_, ...), custom_call_target="tpu_custom_call", output_to_operand_aliasing={{0}: (4, {}), {1}: (5, {})} | custom-call | flops 1000 | bytes 1000 | tf_op jit(solution)/shard_map/apply_rows/pallas_call | solution.py:517
  64.5 2.9 %apply_rows.7 = (bf16[8,640,512]{2,1,0:T(8,128)(2,1)}, bf16[8,640,512]{2,1,0:T(8,128)(2,1)}) custom-call(bf16[1056,128]{1,0:T(8,128)(2,1)S(1)} %collective-permute-done.18.refs_0_, bf16[1056,128]{1,0:T(8,128)(2,1)S(1)} %collective-permute-done.19.refs_1_, ...), custom_call_target="tpu_custom_call", output_to_operand_aliasing={{0}: (6, {}), {1}: (7, {})} | custom-call | flops 1000 | bytes 1000 | tf_op jit(solution)/shard_map/apply_rows/pallas_call | solution.py:517
  67.7 1.6 %apply_rows.8 = (bf16[8,640,512]{2,1,0:T(8,128)(2,1)}, bf16[8,640,512]{2,1,0:T(8,128)(2,1)}) custom-call(bf16[1056,128]{1,0:T(8,128)(2,1)S(1)} %collective-permute-done.17.refs_0_, bf16[3,640,512]{2,1,0:T(8,128)(2,1)S(1)} %get-tuple-element.112.refs_4_.refs_1_, bf16[8,640,512]{2,1,0:T(8,128)(2,1)S(1)} %bitcast.12, ...), custom_call_target="tpu_custom_call", output_to_operand_aliasing={{0}: (3, {}), {1}: (4, {})} | custom-call | flops 1000 | bytes 1000 | tf_op jit(solution)/shard_map/apply_rows/pallas_call | solution.py:517
  69.2 1.6 %apply_rows.9 = (bf16[8,640,512]{2,1,0:T(8,128)(2,1)}, bf16[8,640,512]{2,1,0:T(8,128)(2,1)}) custom-call(bf16[1056,128]{1,0:T(8,128)(2,1)S(1)} %collective-permute-done.21.refs_0_, bf16[1,640,512]{2,1,0:T(8,128)(2,1)S(1)} %get-tuple-element.121.refs_1_, bf16[8,640,512]{2,1,0:T(8,128)(2,1)S(1)} %bitcast.13, ...), custom_call_target="tpu_custom_call", output_to_operand_aliasing={{0}: (3, {}), {1}: (4, {})} | custom-call | flops 1000 | bytes 1000 | tf_op jit(solution)/shard_map/apply_rows/pallas_call | solution.py:517
  (39 shorter events, 5.7 us)
Async XLA Ops:
  3.3 5.0 %collective-permute-start = (f32[1,520,128]{2,1,0:T(8,128)S(1)}, f32[1,520,128]{2,1,0:T(8,128)S(1)}, u32[]{:S(2)}, u32[]{:S(2)}) collective-permute-start(f32[1,520,128]{2,1,0:T(8,128)S(1)} %get-tuple-element.70), channel_id=1, source_target_pairs={{0,1},{1,0},{2,3},{3,2},{4,5},{5,4},{6,7},{7,6},{8,9},{9,8},{10,11... | collective-permute-start | bytes 798728 | tf_op jit(solution)/shard_map/ppermute | solution.py:544
  3.9 4.5 %collective-permute-start.1 = (f32[1,520,128]{2,1,0:T(8,128)S(1)}, f32[1,520,128]{2,1,0:T(8,128)S(1)}, u32[]{:S(2)}, u32[]{:S(2)}) collective-permute-start(f32[1,520,128]{2,1,0:T(8,128)S(1)} %get-tuple-element.71), channel_id=1, source_target_pairs={{0,1},{1,0},{2,3},{3,2},{4,5},{5,4},{6,7},{7,6},{8,9},{9,8},{10,11... | collective-permute-start | bytes 798728 | tf_op jit(solution)/shard_map/ppermute | solution.py:544
  7.3 8.2 %collective-permute-start.2 = (f32[1,520,128]{2,1,0:T(8,128)S(1)}, f32[1,520,128]{2,1,0:T(8,128)S(1)}, u32[]{:S(2)}, u32[]{:S(2)}) collective-permute-start(f32[1,520,128]{2,1,0:T(8,128)S(1)} %get-tuple-element.78), channel_id=1, source_target_pairs={{0,1},{1,0},{2,3},{3,2},{4,5},{5,4},{6,7},{7,6},{8,9},{9,8},{10,11... | collective-permute-start | bytes 798728 | tf_op jit(solution)/shard_map/ppermute | solution.py:544
  7.8 7.7 %collective-permute-start.3 = (f32[1,520,128]{2,1,0:T(8,128)S(1)}, f32[1,520,128]{2,1,0:T(8,128)S(1)}, u32[]{:S(2)}, u32[]{:S(2)}) collective-permute-start(f32[1,520,128]{2,1,0:T(8,128)S(1)} %get-tuple-element.79), channel_id=1, source_target_pairs={{0,1},{1,0},{2,3},{3,2},{4,5},{5,4},{6,7},{7,6},{8,9},{9,8},{10,11... | collective-permute-start | bytes 798728 | tf_op jit(solution)/shard_map/ppermute | solution.py:544
  7.9 7.7 %collective-permute-start.4 = (f32[1,520,128]{2,1,0:T(8,128)S(1)}, f32[1,520,128]{2,1,0:T(8,128)S(1)}, u32[]{:S(2)}, u32[]{:S(2)}) collective-permute-start(f32[1,520,128]{2,1,0:T(8,128)S(1)} %get-tuple-element.82), channel_id=1, source_target_pairs={{0,1},{1,0},{2,3},{3,2},{4,5},{5,4},{6,7},{7,6},{8,9},{9,8},{10,11... | collective-permute-start | bytes 798728 | tf_op jit(solution)/shard_map/ppermute | solution.py:544
  8.3 7.2 %collective-permute-start.5 = (f32[1,520,128]{2,1,0:T(8,128)S(1)}, f32[1,520,128]{2,1,0:T(8,128)S(1)}, u32[]{:S(2)}, u32[]{:S(2)}) collective-permute-start(f32[1,520,128]{2,1,0:T(8,128)S(1)} %get-tuple-element.83), channel_id=1, source_target_pairs={{0,1},{1,0},{2,3},{3,2},{4,5},{5,4},{6,7},{7,6},{8,9},{9,8},{10,11... | collective-permute-start | bytes 798728 | tf_op jit(solution)/shard_map/ppermute | solution.py:544
  8.7 11.3 %collective-permute-start.6 = (s16[1,1056,128]{2,1,0:T(8,128)(2,1)S(1)}, s16[1,1056,128]{2,1,0:T(8,128)(2,1)S(1)}, u32[]{:S(2)}, u32[]{:S(2)}) collective-permute-start(s16[1,1056,128]{2,1,0:T(8,128)(2,1)S(1)} %send.2), channel_id=1, source_target_pairs={{0,18},{1,19},{2,16},{3,17},{4,22},{5,23},{6,20},{7,21},{8,26},{9,... | collective-permute-start | bytes 811016 | tf_op jit(solution)/shard_map/ppermute | solution.py:544
  16.0 38.7 %slice-start = ((s8[5242880]{0:T(1024)(128)(4,1)}), s8[4194304]{0:T(1024)(128)(4,1)S(1)}, s32[]{:S(2)}) async-start(s8[5242880]{0:T(1024)(128)(4,1)} %bitcast.7), calls=%async_computation | async-start | bytes 8388608
  16.0 38.7 %slice-start.1 = ((s8[5242880]{0:T(1024)(128)(4,1)}), s8[1048576]{0:T(1024)(128)(4,1)S(1)}, s32[]{:S(2)}) async-start(s8[5242880]{0:T(1024)(128)(4,1)} %bitcast.7), calls=%async_computation.1 | async-start | bytes 2097152
  16.1 9.3 %collective-permute-start.10 = (s16[1,1056,128]{2,1,0:T(8,128)(2,1)S(1)}, s16[1,1056,128]{2,1,0:T(8,128)(2,1)S(1)}, u32[]{:S(2)}, u32[]{:S(2)}) collective-permute-start(s16[1,1056,128]{2,1,0:T(8,128)(2,1)S(1)} %get-tuple-element.99), channel_id=1, source_target_pairs={{0,2},{1,3},{2,0},{3,1},{4,6},{5,7},{6,4},{7,5},{8,10},{9,11},{10,... | collective-permute-start | bytes 811016 | tf_op jit(solution)/shard_map/ppermute | solution.py:544
  16.6 8.8 %collective-permute-start.9 = (s16[1,1056,128]{2,1,0:T(8,128)(2,1)S(1)}, s16[1,1056,128]{2,1,0:T(8,128)(2,1)S(1)}, u32[]{:S(2)}, u32[]{:S(2)}) collective-permute-start(s16[1,1056,128]{2,1,0:T(8,128)(2,1)S(1)} %get-tuple-element.98), channel_id=1, source_target_pairs={{0,16},{1,17},{2,18},{3,19},{4,20},{5,21},{6,22},{7,23},{8,24},{9,... | collective-permute-start | bytes 811016 | tf_op jit(solution)/shard_map/ppermute | solution.py:544
  21.3 4.1 %collective-permute-start.7 = (f32[1,520,128]{2,1,0:T(8,128)S(1)}, f32[1,520,128]{2,1,0:T(8,128)S(1)}, u32[]{:S(2)}, u32[]{:S(2)}) collective-permute-start(f32[1,520,128]{2,1,0:T(8,128)S(1)} %get-tuple-element.95), channel_id=1, source_target_pairs={{0,1},{1,0},{2,3},{3,2},{4,5},{5,4},{6,7},{7,6},{8,9},{9,8},{10,11... | collective-permute-start | bytes 798728 | tf_op jit(solution)/shard_map/ppermute | solution.py:544
  21.4 4.0 %collective-permute-start.8 = (f32[1,520,128]{2,1,0:T(8,128)S(1)}, f32[1,520,128]{2,1,0:T(8,128)S(1)}, u32[]{:S(2)}, u32[]{:S(2)}) collective-permute-start(f32[1,520,128]{2,1,0:T(8,128)S(1)} %get-tuple-element.96), channel_id=1, source_target_pairs={{0,1},{1,0},{2,3},{3,2},{4,5},{5,4},{6,7},{7,6},{8,9},{9,8},{10,11... | collective-permute-start | bytes 798728 | tf_op jit(solution)/shard_map/ppermute | solution.py:544
  26.0 5.1 %collective-permute-start.11 = (s16[1,528,128]{2,1,0:T(8,128)(2,1)S(1)}, s16[1,528,128]{2,1,0:T(8,128)(2,1)S(1)}, u32[]{:S(2)}, u32[]{:S(2)}) collective-permute-start(s16[1,528,128]{2,1,0:T(8,128)(2,1)S(1)} %get-tuple-element.101), channel_id=1, source_target_pairs={{0,8},{1,9},{2,10},{3,11},{4,12},{5,13},{6,14},{7,15},{8,0},{9,1},... | collective-permute-start | bytes 405512 | tf_op jit(solution)/shard_map/ppermute | solution.py:544
  27.6 8.3 %collective-permute-start.12 = (s16[1,528,128]{2,1,0:T(8,128)(2,1)S(1)}, s16[1,528,128]{2,1,0:T(8,128)(2,1)S(1)}, u32[]{:S(2)}, u32[]{:S(2)}) collective-permute-start(s16[1,528,128]{2,1,0:T(8,128)(2,1)S(1)} %get-tuple-element.102), channel_id=1, source_target_pairs={{0,4},{1,5},{2,6},{3,7},{4,0},{5,1},{6,2},{7,3},{8,12},{9,13},{10,... | collective-permute-start | bytes 405512 | tf_op jit(solution)/shard_map/ppermute | solution.py:544
  36.2 8.3 %collective-permute-start.13 = (s16[1,528,128]{2,1,0:T(8,128)(2,1)S(1)}, s16[1,528,128]{2,1,0:T(8,128)(2,1)S(1)}, u32[]{:S(2)}, u32[]{:S(2)}) collective-permute-start(s16[1,528,128]{2,1,0:T(8,128)(2,1)S(1)} %get-tuple-element.104), channel_id=1, source_target_pairs={{0,4},{1,5},{2,6},{3,7},{4,0},{5,1},{6,2},{7,3},{8,12},{9,13},{10,... | collective-permute-start | bytes 405512 | tf_op jit(solution)/shard_map/ppermute | solution.py:544
  36.5 8.0 %collective-permute-start.14 = (s16[1,528,128]{2,1,0:T(8,128)(2,1)S(1)}, s16[1,528,128]{2,1,0:T(8,128)(2,1)S(1)}, u32[]{:S(2)}, u32[]{:S(2)}) collective-permute-start(s16[1,528,128]{2,1,0:T(8,128)(2,1)S(1)} %get-tuple-element.105), channel_id=1, source_target_pairs={{0,8},{1,9},{2,10},{3,11},{4,12},{5,13},{6,14},{7,15},{8,0},{9,1},... | collective-permute-start | bytes 405512 | tf_op jit(solution)/shard_map/ppermute | solution.py:544
  51.6 8.4 %collective-permute-start.15 = (bf16[1056,128]{1,0:T(8,128)(2,1)S(1)}, bf16[1056,128]{1,0:T(8,128)(2,1)S(1)}, u32[]{:S(2)}, u32[]{:S(2)}) collective-permute-start(bf16[1056,128]{1,0:T(8,128)(2,1)S(1)} %iterations.1.refs_0_), channel_id=1, source_target_pairs={{0,16},{1,3},{2,18},{3,1},{4,20},{5,7},{6,22},{7,5},{8,24},{9,11},... | collective-permute-start | bytes 811016 | tf_op jit(solution)/shard_map/ppermute | solution.py:555
  54.2 6.5 %collective-permute-start.16 = (bf16[1056,128]{1,0:T(8,128)(2,1)S(1)}, bf16[1056,128]{1,0:T(8,128)(2,1)S(1)}, u32[]{:S(2)}, u32[]{:S(2)}) collective-permute-start(bf16[1056,128]{1,0:T(8,128)(2,1)S(1)} %iterations.1.refs_0_), channel_id=1, source_target_pairs={{0,2},{1,17},{2,0},{3,19},{4,6},{5,21},{6,4},{7,23},{8,10},{9,25},... | collective-permute-start | bytes 811016 | tf_op jit(solution)/shard_map/ppermute | solution.py:555
  60.7 3.8 %collective-permute-start.18 = (bf16[1056,128]{1,0:T(8,128)(2,1)S(1)}, bf16[1056,128]{1,0:T(8,128)(2,1)S(1)}, u32[]{:S(2)}, u32[]{:S(2)}) collective-permute-start(bf16[1056,128]{1,0:T(8,128)(2,1)S(1)} %iterations.1.refs_0_), channel_id=1, source_target_pairs={{0,1},{1,0},{2,3},{3,2},{4,5},{5,4},{6,7},{7,6},{8,9},{9,8},{10,11... | collective-permute-start | bytes 811016 | tf_op jit(solution)/shard_map/ppermute | solution.py:544
  60.7 3.8 %collective-permute-start.19 = (bf16[1056,128]{1,0:T(8,128)(2,1)S(1)}, bf16[1056,128]{1,0:T(8,128)(2,1)S(1)}, u32[]{:S(2)}, u32[]{:S(2)}) collective-permute-start(bf16[1056,128]{1,0:T(8,128)(2,1)S(1)} %collective-permute-done.15.refs_0_), channel_id=1, source_target_pairs={{0,1},{1,0},{2,3},{3,2},{4,5},{5,4},{6,7},{7,6},{8,9},{9,8},{10,11... | collective-permute-start | bytes 811016 | tf_op jit(solution)/shard_map/ppermute | solution.py:544
  61.2 3.3 %collective-permute-start.20 = (bf16[1056,128]{1,0:T(8,128)(2,1)S(1)}, bf16[1056,128]{1,0:T(8,128)(2,1)S(1)}, u32[]{:S(2)}, u32[]{:S(2)}) collective-permute-start(bf16[1056,128]{1,0:T(8,128)(2,1)S(1)} %collective-permute-done.16.refs_1_), channel_id=1, source_target_pairs={{0,1},{1,0},{2,3},{3,2},{4,5},{5,4},{6,7},{7,6},{8,9},{9,8},{10,11... | collective-permute-start | bytes 811016 | tf_op jit(solution)/shard_map/ppermute | solution.py:544
  61.2 6.5 %collective-permute-start.17 = (bf16[1056,128]{1,0:T(8,128)(2,1)S(1)}, bf16[1056,128]{1,0:T(8,128)(2,1)S(1)}, u32[]{:S(2)}, u32[]{:S(2)}) collective-permute-start(bf16[1056,128]{1,0:T(8,128)(2,1)S(1)} %collective-permute-done.16.refs_1_), channel_id=1, source_target_pairs={{0,16},{1,3},{2,18},{3,1},{4,20},{5,7},{6,22},{7,5},{8,24},{9,11},... | collective-permute-start | bytes 811016 | tf_op jit(solution)/shard_map/ppermute | solution.py:555
  67.7 1.6 %collective-permute-start.21 = (bf16[1056,128]{1,0:T(8,128)(2,1)S(1)}, bf16[1056,128]{1,0:T(8,128)(2,1)S(1)}, u32[]{:S(2)}, u32[]{:S(2)}) collective-permute-start(bf16[1056,128]{1,0:T(8,128)(2,1)S(1)} %collective-permute-done.17.refs_0_), channel_id=1, source_target_pairs={{0,1},{1,0},{2,3},{3,2},{4,5},{5,4},{6,7},{7,6},{8,9},{9,8},{10,11... | collective-permute-start | bytes 811016 | tf_op jit(solution)/shard_map/ppermute | solution.py:544

commit v7 on v6

--- a/solution.py
+++ b/solution.py
@@ -83,7 +83,7 @@
     return 2 * (place[0] ^ relative) + core
 
 
-def gram_kernel(expert_size, picks, later, first, loaded, *refs):
+def gram_kernel(expert_size, picks, later, first, where, *refs):
     refs = list(refs)
     take = lambda n: [refs.pop(0) for _ in range(n)]
     grad_ref, mom_ref = take(2)
@@ -91,7 +91,7 @@
         counts_ref, peaks_ref = take(2)
     else:
         (facts_ref,) = take(1)
-    given = take(2 if loaded else 0)
+    given = [take(2) for _ in range(1 + max([spot[0] for spot in where if spot] + [-1]))]
     if first:
         (facts_ref,) = take(1)
     (nes_ref,) = take(1)
@@ -110,7 +110,8 @@
             for n, (source, buffer) in enumerate(((grad_ref, buffers[0]), (mom_ref, buffers[1])))
         ]
 
-    own_copies = copies_of(layers[loaded:], (own_grad, own_mom), own_arrivals)
+    own = [k for k, spot in enumerate(where) if not spot]
+    own_copies = copies_of([layers[k] for k in own], (own_grad, own_mom), own_arrivals)
     small = []
     if first:
         small = [
@@ -140,8 +141,10 @@
     slot = lax.broadcasted_iota(i32, (nes_ref.shape[1], LANES), 0)
 
     def form_rows(k):
-        (grad_buf, mom_buf), at = (given, k) if k < loaded else ((own_grad, own_mom), k - loaded)
-        if k >= loaded:
+        if where[k]:
+            (grad_buf, mom_buf), at = given[where[k][0]], where[k][1]
+        else:
+            (grad_buf, mom_buf), at = (own_grad, own_mom), own.index(k)
             for copy in own_copies[2 * at : 2 * at + 2]:
                 copy.wait()
         live = slot < facts_ref[layers[k], 6:7, :].astype(i32)
@@ -178,7 +181,16 @@
         copy.wait()
 
 
-def gram_parts(expert_size, picks, later, sources, facts=None, loaded=()):
+def gram_parts(expert_size, picks, later, sources, facts, loaded):
+    pairs, where = [], []
+    for pick in picks:
+        spot = None
+        if pick in loaded:
+            grad_rows, mom_rows, index = loaded[pick]
+            if not any(pair[0] is grad_rows for pair in pairs):
+                pairs.append((grad_rows, mom_rows))
+            spot = [k for k, pair in enumerate(pairs) if pair[0] is grad_rows][0], index
+        where.append(spot)
     grad, mom, counts, peaks = sources
     layers, capacity, features = grad.shape
     first = facts is None
@@ -190,17 +202,17 @@
     out_shapes += [rows(number)] + [jax.ShapeDtypeStruct((1, HALF, LANES), f32)] * (2 * number)
     out_shapes += [rows(len(later))] * 2 if later else []
     args = [pinned(grad), pinned(mom)]
-    args += [pinned(counts), pinned(peaks)] if first else [facts] + list(loaded)
-    known = loaded[0].shape[0] if loaded else 0
-    own = max(number - known, 1)
+    args += [pinned(counts), pinned(peaks)] if first else [facts]
+    args += [array for pair in pairs for array in pair]
+    own = max(where.count(None), 1)
     scratch = []
     if first:
         scratch += [pltpu.SMEM(counts.shape, i32), pltpu.VMEM(peaks.shape, bf16), pltpu.SemaphoreType.DMA((2,))]
     scratch += [pltpu.SemaphoreType.DMA((2, max(len(later), 1))), pltpu.SemaphoreType.DMA((2, own))]
     scratch += [pltpu.VMEM((own, capacity, features), bf16)] * 2
     out = pl.pallas_call(
-        functools.partial(gram_kernel, expert_size, picks, later, first, known),
-        in_specs=[hbm] * (4 if first else 2) + [vmem] * (0 if first else 1) + [vmem] * len(loaded),
+        functools.partial(gram_kernel, expert_size, picks, later, first, where),
+        in_specs=[hbm] * (4 if first else 2) + [vmem] * (0 if first else 1) + [vmem] * (2 * len(pairs)),
         out_specs=[vmem] * len(out_shapes),
         out_shape=out_shapes,
         scratch_shapes=scratch,
@@ -211,7 +223,9 @@
     if first:
         facts, out = out[0], out[1:]
     halves = [list(out[at : at + 2]) for at in range(1, 1 + 2 * number, 2)]
-    return facts, out[0], halves, tuple(out[1 + 2 * number :])
+    loads = out[1 + 2 * number :]
+    loaded = loaded | {pick: (loads[0], loads[1], k) for k, pick in enumerate(later)}
+    return facts, out[0], halves, loaded
 
 
 def joined(first, second):
@@ -558,27 +572,38 @@
     others = list(range(most - 1, 0, -1))
     turns = [
         [(most, False)],
-        [(most, True)] + [(r, False) for r in others],
+        [(most, True)],
+        [(r, False) for r in others],
         [(r, True) for r in others],
         [(0, False), (0, True)],
     ]
+    ahead = [turns[1] + turns[2][:1], turns[2][1:2], turns[3][:2], turns[4], []]
     rows, partial, messages = {}, {}, []
-    facts, loaded = None, ()
+    facts, loaded = None, {}
     message_shape = jax.ShapeDtypeStruct((1, 2 * HALF_CODE, LANES), i16)
+
+    def after(loaded, arrays):
+        kept = []
+        for first_array, second_array, _ in loaded.values():
+            if not any(first_array is pair[0] for pair in kept):
+                kept.append((first_array, second_array))
+        held, arrays = lax.optimization_barrier((kept, arrays))
+        number_of = lambda array: [k for k, pair in enumerate(kept) if pair[0] is array][0]
+        return {pick: (*held[number_of(g)], index) for pick, (g, _, index) in loaded.items()}, arrays
+
     for number, turn in enumerate(turns):
-        later = turns[number + 1][:2] if number + 1 < len(turns) else []
-        if messages and not later:
-            loaded, messages[0] = lax.optimization_barrier((loaded, messages[0]))
-        facts, made, grams, loaded = gram_parts(expert_size, turn, later, sources, facts, loaded)
+        facts, made, grams, loaded = gram_parts(expert_size, turn, ahead[number], sources, facts, loaded)
         for index, (pick, gram) in enumerate(zip(turn, grams)):
             rows[pick] = (made, index)
             partial[pick] = gram if pick[1] else [over(half, across_core) for half in gram]
-        ready = ([], [most], others, [])[number]
+        ready = ([], [most], [], others, [])[number]
         if ready:
             sums = [half for r in ready for half in partial[r, True] + partial[r, False]]
+            if messages:
+                sums, messages[0] = lax.optimization_barrier((sums, messages[0]))
             kernel = functools.partial(send_kernel, len(ready))
             made = local_call(kernel, [message_shape] * len(ready), "send", *sums)
-            made, loaded = lax.optimization_barrier((made, loaded))
+            loaded, made = after(loaded, made)
             messages += [over(message, mask_of(r)) for r, message in zip(ready, made)]
     codes = jax.ShapeDtypeStruct((1, HALF_CODE, LANES), i16)
     shapes = [codes, codes, jax.ShapeDtypeStruct((1, 2 * HALF, LANES), f32)]

time: 71.2 us -> 69.6 us (0.978)
  waiting for transfers between devices: 24.6 us -> 16.4 us
  starting transfers between devices: 16.6 us -> 22.6 us
    ppermute x19, waiting for transfers between devices: 20 us -> 13.5 us  [over(): return lax.ppermute(x, ('dp', 'expert'), [(i, i ^ mask) for i in everyone])]
    ppermute x19, starting transfers between devices: 12.4 us -> 16.3 us  [over(): return lax.ppermute(x, ('dp', 'expert'), [(i, i ^ mask) for i in everyone])]
    ppermute x3, starting transfers between devices: 4.23 us -> 6.25 us  [by_core(): lax.ppermute(x, ('dp', 'expert'), [(i, i ^ (odd if i & 1 else even)) for...]
    ppermute x3, waiting for transfers between devices: 4.65 us -> 2.86 us  [by_core(): lax.ppermute(x, ('dp', 'expert'), [(i, i ^ (odd if i & 1 else even)) for...]
    pallas_call x4 -> x5, Pallas kernels: 10.1 us -> 10.9 us  [gram_parts(): pl.pallas_call(functools.partial(gram_kernel, expert_size, picks, later,...]
  transfers between devices with their start and end apart: 22 -> 22, of which waited for: 8 -> 12; matrix products, arithmetic and copies ran while one was open for 0% -> 0% of each run, Pallas kernels for 22% -> 24%
where the time goes in v7:
time: 69.6 us; the launch traced here: 69.4 us
  Pallas kernels  29.4 us (42%)
  starting transfers between devices  22.6 us (32%)
  waiting for transfers between devices  16.4 us (24%)
  between operations  1.02 us (1%)
    ppermute x19, starting transfers between devices, over(): return lax.ppermute(x, ('dp', 'expert'), [(i, i ^ mask) for i in everyone])  16.3 us
    ppermute x19, waiting for transfers between devices, over(): return lax.ppermute(x, ('dp', 'expert'), [(i, i ^ mask) for i in everyone])  13.5 us
    pallas_call x5, Pallas kernels, gram_parts(): pl.pallas_call(functools.partial(gram_kernel, expert_size, picks, later,...  10.9 us
    pallas_call x5, Pallas kernels, apply_rows(): pl.pallas_call(functools.partial(apply_kernel, steps, spread, places, sea...  9.78 us
    pallas_call x1, Pallas kernels, iterations(): pl.pallas_call(iterate_kernel, in_specs=[pl.BlockSpec(memory_space=pltpu....  7.03 us
    ppermute x3, starting transfers between devices, by_core(): lax.ppermute(x, ('dp', 'expert'), [(i, i ^ (odd if i & 1 else even)) for...  6.25 us
    ppermute x3, waiting for transfers between devices, by_core(): lax.ppermute(x, ('dp', 'expert'), [(i, i ^ (odd if i & 1 else even)) for...  2.86 us
    pallas_call x4, Pallas kernels, local_call(): pl.pallas_call(kernel, in_specs=[pl.BlockSpec(memory_space=pltpu.VMEM)] *...  1.72 us
  transfers between devices with their start and end apart: 22, of which 12 were waited for; matrix products, arithmetic and copies ran while one was open for 0% of the time, Pallas kernels for 24%

profile of v7, /device:TPU:0, one launch (start us, length us, event | category | flops | bytes accessed | tf_op | source)
XLA Modules:
  0.0 69.4 jit_solution(9384806681569177310)
XLA Ops:
  0.6 2.7 %gram_parts.5 = (f32[8,8,128]{2,1,0:T(8,128)S(1)}, bf16[1,640,512]{2,1,0:T(8,128)(2,1)S(1)}, f32[1,520,128]{2,1,0:T(8,128)S(1)}, f32[1,520,128]{2,1,0:T(8,128)S(...) custom-call(bf16[8,640,512]{2,1,0:T(8,128)(2,1)} %bitcast.14, bf16[8,640,512]{2,1,0:T(8,128)(2,1)} %bitcast.19, ...), custom_call_target="tpu_custom_call" | custom-call | flops 1000 | bytes 1000 | tf_op jit(solution)/shard_map/gram_parts/pallas_call | solution.py:213
  3.9 1.3 %gram_parts.6 = (bf16[1,640,512]{2,1,0:T(8,128)(2,1)S(1)}, f32[1,520,128]{2,1,0:T(8,128)S(1)}, f32[1,520,128]{2,1,0:T(8,128)S(1)}, bf16[1,640,512]{2,1,0:T(8,128)(2,1)S(1)}, bf16[1,640,512]{2,1,0:T(8,128)(2,1)S(1)}) custom-call(bf16[8,640,512]{2,1,0:T(8,128)(2,1)} %bitcast.15, bf16[8,640,512]{2,1,0:T(8,128)(2,1)} %bitcast.20, ...), custom_call_target="tpu_custom_call" | custom-call | flops 1000 | bytes 1000 | tf_op jit(solution)/shard_map/gram_parts/pallas_call | solution.py:213
  5.7 4.0 %collective-permute-start.6 = (s16[1,1056,128]{2,1,0:T(8,128)(2,1)S(1)}, s16[1,1056,128]{2,1,0:T(8,128)(2,1)S(1)}, u32[]{:S(2)}, u32[]{:S(2)}) collective-permute-start(s16[1,1056,128]{2,1,0:T(8,128)(2,1)S(1)} %send.2), channel_id=1, source_target_pairs={{0,18},{1,19},{2,16},{3,17},{4,22},{5,23},{6,20},{7,21},{8,26},{9,... | collective-permute-start | bytes 811016 | tf_op jit(solution)/shard_map/ppermute | solution.py:558
  9.7 2.7 %gram_parts.7 = (bf16[2,640,512]{2,1,0:T(8,128)(2,1)S(1)}, f32[1,520,128]{2,1,0:T(8,128)S(1)}, f32[1,520,128]{2,1,0:T(8,128)S(1)}, f32[1,520,128]{2,1,0:T(8,128)...) custom-call(bf16[8,640,512]{2,1,0:T(8,128)(2,1)} %bitcast.16, ...), custom_call_target="tpu_custom_call" | custom-call | flops 1000 | bytes 1000 | tf_op jit(solution)/shard_map/gram_parts/pallas_call | solution.py:213
  13.5 2.8 %gram_parts.8 = (bf16[2,640,512]{2,1,0:T(8,128)(2,1)S(1)}, f32[1,520,128]{2,1,0:T(8,128)S(1)}, f32[1,520,128]{2,1,0:T(8,128)S(1)}, f32[1,520,128]{2,1,0:T(8,128)...) custom-call(bf16[8,640,512]{2,1,0:T(8,128)(2,1)} %bitcast.17, ...), custom_call_target="tpu_custom_call" | custom-call | flops 1000 | bytes 1000 | tf_op jit(solution)/shard_map/gram_parts/pallas_call | solution.py:213
  16.9 1.7 %collective-permute-start.10 = (s16[1,1056,128]{2,1,0:T(8,128)(2,1)S(1)}, s16[1,1056,128]{2,1,0:T(8,128)(2,1)S(1)}, u32[]{:S(2)}, u32[]{:S(2)}) collective-permute-start(s16[1,1056,128]{2,1,0:T(8,128)(2,1)S(1)} %get-tuple-element.120), channel_id=1, source_target_pairs={{0,2},{1,3},{2,0},{3,1},{4,6},{5,7},{6,4},{7,5},{8,10},{9,11},{10,... | collective-permute-start | bytes 811016 | tf_op jit(solution)/shard_map/ppermute | solution.py:558
  18.7 1.5 %collective-permute-start.9 = (s16[1,1056,128]{2,1,0:T(8,128)(2,1)S(1)}, s16[1,1056,128]{2,1,0:T(8,128)(2,1)S(1)}, u32[]{:S(2)}, u32[]{:S(2)}) collective-permute-start(s16[1,1056,128]{2,1,0:T(8,128)(2,1)S(1)} %get-tuple-element.119), channel_id=1, source_target_pairs={{0,16},{1,17},{2,18},{3,19},{4,20},{5,21},{6,22},{7,23},{8,24},{9,... | collective-permute-start | bytes 811016 | tf_op jit(solution)/shard_map/ppermute | solution.py:558
  20.2 1.3 %gram_parts.9 = (bf16[2,640,512]{2,1,0:T(8,128)(2,1)S(1)}, f32[1,520,128]{2,1,0:T(8,128)S(1)}, f32[1,520,128]{2,1,0:T(8,128)S(1)}, f32[1,520,128]{2,1,0:T(8,128)S(1)}, f32[1,520,128]{2,1,0:T(8,128)S(1)}) custom-call(bf16[8,640,512]{2,1,0:T(8,128)(2,1)} %bitcast.18, bf16[8,640,512]{2,1,0:T(8,128)(2,1)} %bitcast.23, ...), custom_call_target="tpu_custom_call" | custom-call | flops 1000 | bytes 1000 | tf_op jit(solution)/shard_map/gram_parts/pallas_call | solution.py:213
  23.5 1.9 %collective-permute-done.10.refs_6_ = s16[1,1056,128]{2,1,0:T(8,128)(2,1)S(1)} collective-permute-done((s16[1,1056,128]{2,1,0:T(8,128)(2,1)S(1)}, s16[1,1056,128]{2,1,0:T(8,128)(2,1)S(1)}, u32[]{:S(2)}, u32[]{:S(2)}) %collective-permute-start.10) | collective-permute-done | bytes 270368 | tf_op jit(solution)/shard_map/ppermute | solution.py:558
  26.7 1.6 %collective-permute-start.11 = (s16[1,528,128]{2,1,0:T(8,128)(2,1)S(1)}, s16[1,528,128]{2,1,0:T(8,128)(2,1)S(1)}, u32[]{:S(2)}, u32[]{:S(2)}) collective-permute-start(s16[1,528,128]{2,1,0:T(8,128)(2,1)S(1)} %get-tuple-element.122), channel_id=1, source_target_pairs={{0,8},{1,9},{2,10},{3,11},{4,12},{5,13},{6,14},{7,15},{8,0},{9,1},... | collective-permute-start | bytes 405512 | tf_op jit(solution)/shard_map/ppermute | solution.py:558
  28.3 2.6 %collective-permute-start.12 = (s16[1,528,128]{2,1,0:T(8,128)(2,1)S(1)}, s16[1,528,128]{2,1,0:T(8,128)(2,1)S(1)}, u32[]{:S(2)}, u32[]{:S(2)}) collective-permute-start(s16[1,528,128]{2,1,0:T(8,128)(2,1)S(1)} %get-tuple-element.123), channel_id=1, source_target_pairs={{0,4},{1,5},{2,6},{3,7},{4,0},{5,1},{6,2},{7,3},{8,12},{9,13},{10,... | collective-permute-start | bytes 405512 | tf_op jit(solution)/shard_map/ppermute | solution.py:558
  31.8 3.8 %collective-permute-done.12.arrived_b = s16[1,528,128]{2,1,0:T(8,128)(2,1)S(1)} collective-permute-done((s16[1,528,128]{2,1,0:T(8,128)(2,1)S(1)}, s16[1,528,128]{2,1,0:T(8,128)(2,1)S(1)}, u32[]{:S(2)}, u32[]{:S(2)}) %collective-permute-start.12) | collective-permute-done | bytes 135200 | tf_op jit(solution)/shard_map/ppermute | solution.py:558
  36.0 1.3 %collective-permute-start.13 = (s16[1,528,128]{2,1,0:T(8,128)(2,1)S(1)}, s16[1,528,128]{2,1,0:T(8,128)(2,1)S(1)}, u32[]{:S(2)}, u32[]{:S(2)}) collective-permute-start(s16[1,528,128]{2,1,0:T(8,128)(2,1)S(1)} %get-tuple-element.125), channel_id=1, source_target_pairs={{0,4},{1,5},{2,6},{3,7},{4,0},{5,1},{6,2},{7,3},{8,12},{9,13},{10,... | collective-permute-start | bytes 405512 | tf_op jit(solution)/shard_map/ppermute | solution.py:558
  37.9 4.3 %collective-permute-done.13.arrived_a = s16[1,528,128]{2,1,0:T(8,128)(2,1)S(1)} collective-permute-done((s16[1,528,128]{2,1,0:T(8,128)(2,1)S(1)}, s16[1,528,128]{2,1,0:T(8,128)(2,1)S(1)}, u32[]{:S(2)}, u32[]{:S(2)}) %collective-permute-start.13) | collective-permute-done | bytes 135200 | tf_op jit(solution)/shard_map/ppermute | solution.py:558
  42.3 7.0 %iterations.1.refs_0_ = bf16[1056,128]{1,0:T(8,128)(2,1)S(1)} custom-call(f32[1,1040,128]{2,1,0:T(8,128)S(1)} %get-tuple-element.124.kept, s16[1,528,128]{2,1,0:T(8,128)(2,1)S(1)} %collective-permute-done.13.arrived_a, s16[1,528,128]{2,1,0:T(8,128)(2,1)S(1)} %collective-permute-done.14.arrived_b), custom_call_target="tpu_custom_call" | custom-call | flops 1000 | bytes 1000 | tf_op jit(solution)/shard_map/iterations/pallas_call | solution.py:432
  49.4 2.2 %collective-permute-start.15 = (bf16[1056,128]{1,0:T(8,128)(2,1)S(1)}, bf16[1056,128]{1,0:T(8,128)(2,1)S(1)}, u32[]{:S(2)}, u32[]{:S(2)}) collective-permute-start(bf16[1056,128]{1,0:T(8,128)(2,1)S(1)} %iterations.1.refs_0_), channel_id=1, source_target_pairs={{0,16},{1,3},{2,18},{3,1},{4,20},{5,7},{6,22},{7,5},{8,24},{9,11},... | collective-permute-start | bytes 811016 | tf_op jit(solution)/shard_map/ppermute | solution.py:569
  51.6 2.1 %collective-permute-start.16 = (bf16[1056,128]{1,0:T(8,128)(2,1)S(1)}, bf16[1056,128]{1,0:T(8,128)(2,1)S(1)}, u32[]{:S(2)}, u32[]{:S(2)}) collective-permute-start(bf16[1056,128]{1,0:T(8,128)(2,1)S(1)} %iterations.1.refs_0_), channel_id=1, source_target_pairs={{0,2},{1,17},{2,0},{3,19},{4,6},{5,21},{6,4},{7,23},{8,10},{9,25},... | collective-permute-start | bytes 811016 | tf_op jit(solution)/shard_map/ppermute | solution.py:569
  53.7 1.6 %apply_rows.5 = (bf16[8,640,512]{2,1,0:T(8,128)(2,1)}, bf16[8,640,512]{2,1,0:T(8,128)(2,1)}) custom-call(bf16[1056,128]{1,0:T(8,128)(2,1)S(1)} %iterations.1.refs_0_, bf16[2,640,512]{2,1,0:T(8,128)(2,1)S(1)} %get-tuple-element.127.refs_1_.refs_3_, bf16[8,640,512]{2,1,0:T(8,128)(2,1)S(1)} %bitcast.9), custom_call_target="tpu_custom_call" | custom-call | flops 1000 | bytes 1000 | tf_op jit(solution)/shard_map/apply_rows/pallas_call | solution.py:531
  55.3 2.5 %collective-permute-done.15.refs_0_ = bf16[1056,128]{1,0:T(8,128)(2,1)S(1)} collective-permute-done((bf16[1056,128]{1,0:T(8,128)(2,1)S(1)}, bf16[1056,128]{1,0:T(8,128)(2,1)S(1)}, u32[]{:S(2)}, u32[]{:S(2)}) %collective-permute-start.15) | collective-permute-done | bytes 270368 | tf_op jit(solution)/shard_map/ppermute | solution.py:569
  58.6 1.9 %collective-permute-start.17 = (bf16[1056,128]{1,0:T(8,128)(2,1)S(1)}, bf16[1056,128]{1,0:T(8,128)(2,1)S(1)}, u32[]{:S(2)}, u32[]{:S(2)}) collective-permute-start(bf16[1056,128]{1,0:T(8,128)(2,1)S(1)} %collective-permute-done.16.refs_1_), channel_id=1, source_target_pairs={{0,16},{1,3},{2,18},{3,1},{4,20},{5,7},{6,22},{7,5},{8,24},{9,11},... | collective-permute-start | bytes 811016 | tf_op jit(solution)/shard_map/ppermute | solution.py:569
  60.6 2.2 %apply_rows.6 = (bf16[8,640,512]{2,1,0:T(8,128)(2,1)}, bf16[8,640,512]{2,1,0:T(8,128)(2,1)}) custom-call(bf16[1056,128]{1,0:T(8,128)(2,1)S(1)} %collective-permute-done.15.refs_0_, bf16[1056,128]{1,0:T(8,128)(2,1)S(1)} %collective-permute-done.16.refs_1_, ...), custom_call_target="tpu_custom_call", output_to_operand_aliasing={{0}: (4, {}), {1}: (5, {})} | custom-call | flops 1000 | bytes 1000 | tf_op jit(solution)/shard_map/apply_rows/pallas_call | solution.py:531
  62.8 2.9 %apply_rows.7 = (bf16[8,640,512]{2,1,0:T(8,128)(2,1)}, bf16[8,640,512]{2,1,0:T(8,128)(2,1)}) custom-call(bf16[1056,128]{1,0:T(8,128)(2,1)S(1)} %collective-permute-done.18.refs_0_, bf16[1056,128]{1,0:T(8,128)(2,1)S(1)} %collective-permute-done.19.refs_1_, ...), custom_call_target="tpu_custom_call", output_to_operand_aliasing={{0}: (6, {}), {1}: (7, {})} | custom-call | flops 1000 | bytes 1000 | tf_op jit(solution)/shard_map/apply_rows/pallas_call | solution.py:531
  66.1 1.6 %apply_rows.8 = (bf16[8,640,512]{2,1,0:T(8,128)(2,1)}, bf16[8,640,512]{2,1,0:T(8,128)(2,1)}) custom-call(bf16[1056,128]{1,0:T(8,128)(2,1)S(1)} %collective-permute-done.17.refs_0_, bf16[1,640,512]{2,1,0:T(8,128)(2,1)S(1)} %get-tuple-element.143.refs_1_, bf16[8,640,512]{2,1,0:T(8,128)(2,1)S(1)} %bitcast.12, ...), custom_call_target="tpu_custom_call", output_to_operand_aliasing={{0}: (3, {}), {1}: (4, {})} | custom-call | flops 1000 | bytes 1000 | tf_op jit(solution)/shard_map/apply_rows/pallas_call | solution.py:531
  67.7 1.6 %apply_rows.9 = (bf16[8,640,512]{2,1,0:T(8,128)(2,1)}, bf16[8,640,512]{2,1,0:T(8,128)(2,1)}) custom-call(bf16[1056,128]{1,0:T(8,128)(2,1)S(1)} %collective-permute-done.21.refs_0_, bf16[1,640,512]{2,1,0:T(8,128)(2,1)S(1)} %get-tuple-element.142.refs_1_, bf16[8,640,512]{2,1,0:T(8,128)(2,1)S(1)} %bitcast.13, ...), custom_call_target="tpu_custom_call", output_to_operand_aliasing={{0}: (3, {}), {1}: (4, {})} | custom-call | flops 1000 | bytes 1000 | tf_op jit(solution)/shard_map/apply_rows/pallas_call | solution.py:531
  (40 shorter events, 9.3 us)
Async XLA Ops:
  3.3 1.9 %collective-permute-start = (f32[1,520,128]{2,1,0:T(8,128)S(1)}, f32[1,520,128]{2,1,0:T(8,128)S(1)}, u32[]{:S(2)}, u32[]{:S(2)}) collective-permute-start(f32[1,520,128]{2,1,0:T(8,128)S(1)} %get-tuple-element.83), channel_id=1, source_target_pairs={{0,1},{1,0},{2,3},{3,2},{4,5},{5,4},{6,7},{7,6},{8,9},{9,8},{10,11... | collective-permute-start | bytes 798728 | tf_op jit(solution)/shard_map/ppermute | solution.py:558
  3.9 1.5 %collective-permute-start.1 = (f32[1,520,128]{2,1,0:T(8,128)S(1)}, f32[1,520,128]{2,1,0:T(8,128)S(1)}, u32[]{:S(2)}, u32[]{:S(2)}) collective-permute-start(f32[1,520,128]{2,1,0:T(8,128)S(1)} %get-tuple-element.84), channel_id=1, source_target_pairs={{0,1},{1,0},{2,3},{3,2},{4,5},{5,4},{6,7},{7,6},{8,9},{9,8},{10,11... | collective-permute-start | bytes 798728 | tf_op jit(solution)/shard_map/ppermute | solution.py:558
  5.7 10.7 %collective-permute-start.6 = (s16[1,1056,128]{2,1,0:T(8,128)(2,1)S(1)}, s16[1,1056,128]{2,1,0:T(8,128)(2,1)S(1)}, u32[]{:S(2)}, u32[]{:S(2)}) collective-permute-start(s16[1,1056,128]{2,1,0:T(8,128)(2,1)S(1)} %send.2), channel_id=1, source_target_pairs={{0,18},{1,19},{2,16},{3,17},{4,22},{5,23},{6,20},{7,21},{8,26},{9,... | collective-permute-start | bytes 811016 | tf_op jit(solution)/shard_map/ppermute | solution.py:558
  12.4 3.9 %collective-permute-start.2 = (f32[1,520,128]{2,1,0:T(8,128)S(1)}, f32[1,520,128]{2,1,0:T(8,128)S(1)}, u32[]{:S(2)}, u32[]{:S(2)}) collective-permute-start(f32[1,520,128]{2,1,0:T(8,128)S(1)} %get-tuple-element.95), channel_id=1, source_target_pairs={{0,1},{1,0},{2,3},{3,2},{4,5},{5,4},{6,7},{7,6},{8,9},{9,8},{10,11... | collective-permute-start | bytes 798728 | tf_op jit(solution)/shard_map/ppermute | solution.py:558
  12.5 3.8 %collective-permute-start.3 = (f32[1,520,128]{2,1,0:T(8,128)S(1)}, f32[1,520,128]{2,1,0:T(8,128)S(1)}, u32[]{:S(2)}, u32[]{:S(2)}) collective-permute-start(f32[1,520,128]{2,1,0:T(8,128)S(1)} %get-tuple-element.96), channel_id=1, source_target_pairs={{0,1},{1,0},{2,3},{3,2},{4,5},{5,4},{6,7},{7,6},{8,9},{9,8},{10,11... | collective-permute-start | bytes 798728 | tf_op jit(solution)/shard_map/ppermute | solution.py:558
  13.0 3.3 %collective-permute-start.4 = (f32[1,520,128]{2,1,0:T(8,128)S(1)}, f32[1,520,128]{2,1,0:T(8,128)S(1)}, u32[]{:S(2)}, u32[]{:S(2)}) collective-permute-start(f32[1,520,128]{2,1,0:T(8,128)S(1)} %get-tuple-element.99), channel_id=1, source_target_pairs={{0,1},{1,0},{2,3},{3,2},{4,5},{5,4},{6,7},{7,6},{8,9},{9,8},{10,11... | collective-permute-start | bytes 798728 | tf_op jit(solution)/shard_map/ppermute | solution.py:558
  13.1 3.3 %collective-permute-start.5 = (f32[1,520,128]{2,1,0:T(8,128)S(1)}, f32[1,520,128]{2,1,0:T(8,128)S(1)}, u32[]{:S(2)}, u32[]{:S(2)}) collective-permute-start(f32[1,520,128]{2,1,0:T(8,128)S(1)} %get-tuple-element.100), channel_id=1, source_target_pairs={{0,1},{1,0},{2,3},{3,2},{4,5},{5,4},{6,7},{7,6},{8,9},{9,8},{10,11... | collective-permute-start | bytes 798728 | tf_op jit(solution)/shard_map/ppermute | solution.py:558
  16.9 36.8 %slice-start = ((s8[5242880]{0:T(1024)(128)(4,1)}), s8[4194304]{0:T(1024)(128)(4,1)S(1)}, s32[]{:S(2)}) async-start(s8[5242880]{0:T(1024)(128)(4,1)} %bitcast.7), calls=%async_computation | async-start | bytes 8388608
  16.9 36.8 %slice-start.1 = ((s8[5242880]{0:T(1024)(128)(4,1)}), s8[1048576]{0:T(1024)(128)(4,1)S(1)}, s32[]{:S(2)}) async-start(s8[5242880]{0:T(1024)(128)(4,1)} %bitcast.7), calls=%async_computation.1 | async-start | bytes 2097152
  16.9 8.4 %collective-permute-start.10 = (s16[1,1056,128]{2,1,0:T(8,128)(2,1)S(1)}, s16[1,1056,128]{2,1,0:T(8,128)(2,1)S(1)}, u32[]{:S(2)}, u32[]{:S(2)}) collective-permute-start(s16[1,1056,128]{2,1,0:T(8,128)(2,1)S(1)} %get-tuple-element.120), channel_id=1, source_target_pairs={{0,2},{1,3},{2,0},{3,1},{4,6},{5,7},{6,4},{7,5},{8,10},{9,11},{10,... | collective-permute-start | bytes 811016 | tf_op jit(solution)/shard_map/ppermute | solution.py:558
  18.7 7.4 %collective-permute-start.9 = (s16[1,1056,128]{2,1,0:T(8,128)(2,1)S(1)}, s16[1,1056,128]{2,1,0:T(8,128)(2,1)S(1)}, u32[]{:S(2)}, u32[]{:S(2)}) collective-permute-start(s16[1,1056,128]{2,1,0:T(8,128)(2,1)S(1)} %get-tuple-element.119), channel_id=1, source_target_pairs={{0,16},{1,17},{2,18},{3,19},{4,20},{5,21},{6,22},{7,23},{8,24},{9,... | collective-permute-start | bytes 811016 | tf_op jit(solution)/shard_map/ppermute | solution.py:558
  21.5 1.6 %collective-permute-start.7 = (f32[1,520,128]{2,1,0:T(8,128)S(1)}, f32[1,520,128]{2,1,0:T(8,128)S(1)}, u32[]{:S(2)}, u32[]{:S(2)}) collective-permute-start(f32[1,520,128]{2,1,0:T(8,128)S(1)} %get-tuple-element.116), channel_id=1, source_target_pairs={{0,1},{1,0},{2,3},{3,2},{4,5},{5,4},{6,7},{7,6},{8,9},{9,8},{10,11... | collective-permute-start | bytes 798728 | tf_op jit(solution)/shard_map/ppermute | solution.py:558
  21.6 1.9 %collective-permute-start.8 = (f32[1,520,128]{2,1,0:T(8,128)S(1)}, f32[1,520,128]{2,1,0:T(8,128)S(1)}, u32[]{:S(2)}, u32[]{:S(2)}) collective-permute-start(f32[1,520,128]{2,1,0:T(8,128)S(1)} %get-tuple-element.117), channel_id=1, source_target_pairs={{0,1},{1,0},{2,3},{3,2},{4,5},{5,4},{6,7},{7,6},{8,9},{9,8},{10,11... | collective-permute-start | bytes 798728 | tf_op jit(solution)/shard_map/ppermute | solution.py:558
  26.7 5.1 %collective-permute-start.11 = (s16[1,528,128]{2,1,0:T(8,128)(2,1)S(1)}, s16[1,528,128]{2,1,0:T(8,128)(2,1)S(1)}, u32[]{:S(2)}, u32[]{:S(2)}) collective-permute-start(s16[1,528,128]{2,1,0:T(8,128)(2,1)S(1)} %get-tuple-element.122), channel_id=1, source_target_pairs={{0,8},{1,9},{2,10},{3,11},{4,12},{5,13},{6,14},{7,15},{8,0},{9,1},... | collective-permute-start | bytes 405512 | tf_op jit(solution)/shard_map/ppermute | solution.py:558
  28.3 7.4 %collective-permute-start.12 = (s16[1,528,128]{2,1,0:T(8,128)(2,1)S(1)}, s16[1,528,128]{2,1,0:T(8,128)(2,1)S(1)}, u32[]{:S(2)}, u32[]{:S(2)}) collective-permute-start(s16[1,528,128]{2,1,0:T(8,128)(2,1)S(1)} %get-tuple-element.123), channel_id=1, source_target_pairs={{0,4},{1,5},{2,6},{3,7},{4,0},{5,1},{6,2},{7,3},{8,12},{9,13},{10,... | collective-permute-start | bytes 405512 | tf_op jit(solution)/shard_map/ppermute | solution.py:558
  36.0 6.1 %collective-permute-start.13 = (s16[1,528,128]{2,1,0:T(8,128)(2,1)S(1)}, s16[1,528,128]{2,1,0:T(8,128)(2,1)S(1)}, u32[]{:S(2)}, u32[]{:S(2)}) collective-permute-start(s16[1,528,128]{2,1,0:T(8,128)(2,1)S(1)} %get-tuple-element.125), channel_id=1, source_target_pairs={{0,4},{1,5},{2,6},{3,7},{4,0},{5,1},{6,2},{7,3},{8,12},{9,13},{10,... | collective-permute-start | bytes 405512 | tf_op jit(solution)/shard_map/ppermute | solution.py:558
  37.3 5.0 %collective-permute-start.14 = (s16[1,528,128]{2,1,0:T(8,128)(2,1)S(1)}, s16[1,528,128]{2,1,0:T(8,128)(2,1)S(1)}, u32[]{:S(2)}, u32[]{:S(2)}) collective-permute-start(s16[1,528,128]{2,1,0:T(8,128)(2,1)S(1)} %get-tuple-element.126), channel_id=1, source_target_pairs={{0,8},{1,9},{2,10},{3,11},{4,12},{5,13},{6,14},{7,15},{8,0},{9,1},... | collective-permute-start | bytes 405512 | tf_op jit(solution)/shard_map/ppermute | solution.py:558
  49.4 8.4 %collective-permute-start.15 = (bf16[1056,128]{1,0:T(8,128)(2,1)S(1)}, bf16[1056,128]{1,0:T(8,128)(2,1)S(1)}, u32[]{:S(2)}, u32[]{:S(2)}) collective-permute-start(bf16[1056,128]{1,0:T(8,128)(2,1)S(1)} %iterations.1.refs_0_), channel_id=1, source_target_pairs={{0,16},{1,3},{2,18},{3,1},{4,20},{5,7},{6,22},{7,5},{8,24},{9,11},... | collective-permute-start | bytes 811016 | tf_op jit(solution)/shard_map/ppermute | solution.py:569
  51.6 6.5 %collective-permute-start.16 = (bf16[1056,128]{1,0:T(8,128)(2,1)S(1)}, bf16[1056,128]{1,0:T(8,128)(2,1)S(1)}, u32[]{:S(2)}, u32[]{:S(2)}) collective-permute-start(bf16[1056,128]{1,0:T(8,128)(2,1)S(1)} %iterations.1.refs_0_), channel_id=1, source_target_pairs={{0,2},{1,17},{2,0},{3,19},{4,6},{5,21},{6,4},{7,23},{8,10},{9,25},... | collective-permute-start | bytes 811016 | tf_op jit(solution)/shard_map/ppermute | solution.py:569
  58.1 4.7 %collective-permute-start.18 = (bf16[1056,128]{1,0:T(8,128)(2,1)S(1)}, bf16[1056,128]{1,0:T(8,128)(2,1)S(1)}, u32[]{:S(2)}, u32[]{:S(2)}) collective-permute-start(bf16[1056,128]{1,0:T(8,128)(2,1)S(1)} %iterations.1.refs_0_), channel_id=1, source_target_pairs={{0,1},{1,0},{2,3},{3,2},{4,5},{5,4},{6,7},{7,6},{8,9},{9,8},{10,11... | collective-permute-start | bytes 811016 | tf_op jit(solution)/shard_map/ppermute | solution.py:558
  58.1 4.7 %collective-permute-start.19 = (bf16[1056,128]{1,0:T(8,128)(2,1)S(1)}, bf16[1056,128]{1,0:T(8,128)(2,1)S(1)}, u32[]{:S(2)}, u32[]{:S(2)}) collective-permute-start(bf16[1056,128]{1,0:T(8,128)(2,1)S(1)} %collective-permute-done.15.refs_0_), channel_id=1, source_target_pairs={{0,1},{1,0},{2,3},{3,2},{4,5},{5,4},{6,7},{7,6},{8,9},{9,8},{10,11... | collective-permute-start | bytes 811016 | tf_op jit(solution)/shard_map/ppermute | solution.py:558
  58.6 4.2 %collective-permute-start.20 = (bf16[1056,128]{1,0:T(8,128)(2,1)S(1)}, bf16[1056,128]{1,0:T(8,128)(2,1)S(1)}, u32[]{:S(2)}, u32[]{:S(2)}) collective-permute-start(bf16[1056,128]{1,0:T(8,128)(2,1)S(1)} %collective-permute-done.16.refs_1_), channel_id=1, source_target_pairs={{0,1},{1,0},{2,3},{3,2},{4,5},{5,4},{6,7},{7,6},{8,9},{9,8},{10,11... | collective-permute-start | bytes 811016 | tf_op jit(solution)/shard_map/ppermute | solution.py:558
  58.6 7.1 %collective-permute-start.17 = (bf16[1056,128]{1,0:T(8,128)(2,1)S(1)}, bf16[1056,128]{1,0:T(8,128)(2,1)S(1)}, u32[]{:S(2)}, u32[]{:S(2)}) collective-permute-start(bf16[1056,128]{1,0:T(8,128)(2,1)S(1)} %collective-permute-done.16.refs_1_), channel_id=1, source_target_pairs={{0,16},{1,3},{2,18},{3,1},{4,20},{5,7},{6,22},{7,5},{8,24},{9,11},... | collective-permute-start | bytes 811016 | tf_op jit(solution)/shard_map/ppermute | solution.py:569
  65.7 1.9 %collective-permute-start.21 = (bf16[1056,128]{1,0:T(8,128)(2,1)S(1)}, bf16[1056,128]{1,0:T(8,128)(2,1)S(1)}, u32[]{:S(2)}, u32[]{:S(2)}) collective-permute-start(bf16[1056,128]{1,0:T(8,128)(2,1)S(1)} %collective-permute-done.17.refs_0_), channel_id=1, source_target_pairs={{0,1},{1,0},{2,3},{3,2},{4,5},{5,4},{6,7},{7,6},{8,9},{9,8},{10,11... | collective-permute-start | bytes 811016 | tf_op jit(solution)/shard_map/ppermute | solution.py:558
